TPU v7x, 32 devices: a whole 2x2x4 slice. The times are simulated.
32 devices in a mesh: seq: 16 (over z, y, x), head: 2 (over core).
Axes of the slice: x: 2, y: 2, z: 4, core: 2. Of those that a mesh axis runs over, the one named last changes fastest.
Arguments:
- hidden_in: bfloat16 [4096, 4096], P('seq', 'head'), may hold values from -6 to 6
- proj_weight: bfloat16 [4096, 256], replicated, may hold values from -0.09375 to 0.09375
- head_input: bfloat16 [4096, 8192], P('seq', 'head'), may hold values from -6 to 6
- gate_input: bfloat16 [4096, 8192], P('seq', 'head'), may hold values from -11 to 11
- step_size: float32 [4096, 128], P('seq', 'head'), may hold values from 0 to 4, as said below
- decay_rate: float32 [128], P('head'), may hold values from 0 to 1, as said below
- norm_gain: float32 [8192], P('head'), may hold values from 0.1 to 1.9
Outputs:
- layer_out: bfloat16 [4096, 8192], P('seq', 'head')
Inputs may be any that keep to these rules, and one draw needn't show every extreme that they name: `decay_rate`: positive. `step_size`: positive.
All inputs are finite; a program needn't handle non-finite values.
Results may differ from a plain program's by a relative error of at most 0.013.
Values may be sent and summed in bfloat16 or wider, within the bound.
No kernel may reach another device: no remote copies, remote signals or barrier semaphores. Data moves between devices by JAX's collectives and lax.ppermute only.
A program may use at most 128 MiB of HBM per device.

v0:
```python
import jax
import jax.numpy as jnp
from jax import lax
from jax.sharding import PartitionSpec as P

HEADS = 128
HEAD_DIM = 64
STATE = 128
GROUP = 256


def carried_in(value, axis, join, neutral):
    count, mine = (lax.axis_size(axis), lax.axis_index(axis))
    pieces = jax.tree.map(lambda part: lax.all_gather(part, axis), value)
    running = jax.tree.map(
        lambda part, zero: jnp.full_like(part, 0) + jnp.asarray(zero, part.dtype), value, neutral
    )

    def step(position, running):
        longer = join(running, jax.tree.map(lambda part: part[position], pieces))
        return jax.tree.map(lambda new, old: jnp.where(position < mine, new, old), longer, running)

    return lax.fori_loop(0, count - 1, step, running)


def combine_states(earlier, later):
    return (earlier[0] + later[0], jnp.exp(later[0])[:, None, None] * earlier[1] + later[1])


def shards(hidden_in, proj_weight, head_input, gate_input, step_size, decay_rate, norm_gain):
    tok_rows = hidden_in.shape[0]
    local_heads = step_size.shape[1]
    summed = jnp.dot(
        lax.all_gather(hidden_in, "head", axis=1, tiled=True),
        proj_weight,
        preferred_element_type=jnp.float32,
    )
    projected = summed.astype(jnp.bfloat16)
    count = tok_rows // GROUP
    b_rows = projected[:, :STATE].reshape(count, GROUP, STATE)
    c_rows = projected[:, STATE:].reshape(count, GROUP, STATE)
    log_decay = -step_size * decay_rate[None, :]
    cumulative = jnp.cumsum(log_decay.reshape(count, GROUP, local_heads), axis=1)
    scaled = (
        head_input.reshape(tok_rows, local_heads, HEAD_DIM).astype(jnp.float32)
        * step_size[:, :, None]
    ).astype(jnp.bfloat16)
    scaled = scaled.reshape(count, GROUP, local_heads, HEAD_DIM)
    positions = jnp.arange(GROUP, dtype=jnp.int32)
    causal = positions[:, None] >= positions[None, :]
    scores = jnp.einsum("ctn,csn->cts", c_rows, b_rows, preferred_element_type=jnp.float32)
    cum_heads = jnp.swapaxes(cumulative, 1, 2)
    gap = cum_heads[:, :, :, None] - cum_heads[:, :, None, :]
    weights = jnp.exp(jnp.where(causal[None, None], gap, -jnp.inf))
    mixing = (scores[:, None] * weights).astype(jnp.bfloat16)
    inner = jnp.einsum("chts,cshp->cthp", mixing, scaled, preferred_element_type=jnp.float32)
    ends = cumulative[:, -1, :]
    tail = jnp.exp(ends[:, None, :] - cumulative)
    weighted = (tail[:, :, :, None] * scaled.astype(jnp.float32)).astype(jnp.bfloat16)
    fresh = jnp.einsum("cshp,csn->chpn", weighted, b_rows, preferred_element_type=jnp.float32)
    block_state = jnp.zeros((local_heads, HEAD_DIM, STATE), jnp.float32)
    block_state = jnp.exp(ends[0])[:, None, None] * block_state + fresh[0]
    block_decay = jnp.sum(ends, axis=0)
    identity = (
        jnp.zeros((local_heads,), jnp.float32),
        jnp.zeros((local_heads, HEAD_DIM, STATE), jnp.float32),
    )
    decay_total, incoming = carried_in((block_decay, block_state), "seq", combine_states, identity)
    entering = [incoming]
    carried_low = jnp.stack(entering).astype(jnp.bfloat16)
    outer = jnp.einsum("ctn,chpn->cthp", c_rows, carried_low, preferred_element_type=jnp.float32)
    outer = outer * jnp.exp(cumulative)[:, :, :, None]
    mixed = (inner + outer).reshape(tok_rows, local_heads * HEAD_DIM)
    gated = mixed * jax.nn.silu(gate_input.astype(jnp.float32))
    squares = jnp.sum(gated * gated, axis=1)
    total_squares = lax.psum(squares, "head")
    mean_square = total_squares / (HEADS * HEAD_DIM)
    return (gated * lax.rsqrt(mean_square + 1e-05)[:, None] * norm_gain[None, :]).astype(
        jnp.bfloat16
    )


def solution(mesh):
    in_specs = (
        P("seq", "head"),
        P(),
        P("seq", "head"),
        P("seq", "head"),
        P("seq", "head"),
        P("head"),
        P("head"),
    )
    out_specs = P("seq", "head")
    return jax.shard_map(shards, mesh=mesh, in_specs=in_specs, out_specs=out_specs, check_vma=False)
```

profile of v0, /device:TPU:0, one launch (start us, length us, event | category | flops | bytes accessed | tf_op | source)
XLA Modules:
  0.0 443.1 jit_solution(13580671044078403524)
XLA Ops:
  6.5 0.0 copy-start
  6.5 0.0 copy-start.5
  6.5 0.0 all-gather.5.cloned.1.call-start
  6.5 0.7 all-gather.5.cloned.1.call-update
  7.3 0.0 all-gather.7.cloned.1.call-start
  7.3 0.9 copy_bitcast_fusion
  8.2 0.6 reduce-window.6
  8.8 0.1 copy.33
  8.9 0.2 slice_reduce_fusion
  9.1 0.1 copy.32
  9.2 0.1 broadcast.64
  9.3 0.1 fusion.24
  9.5 0.9 slice_reduce_fusion.1
  10.4 0.2 subtract_exponential_fusion
  10.6 4.1 copy.29
  14.7 0.0 copy-done.5
  14.7 3.4 fusion.12
  18.1 4.2 all-gather.5.cloned.1.call-done
  22.2 0.0 copy-done
  22.2 0.0 copy-start.4
  22.2 2.4 convolution_convert_fusion
  24.7 0.0 copy-done.4
  24.7 2.0 convolution_add_fusion
  26.7 0.0 all-gather.7.cloned.1.call-update
  26.7 0.1 copy.31
  26.8 0.1 copy.34
  26.9 41.1 %all-gather = f32[16,1,64]{2,1,0:T(1,128)S(1)} all-gather(f32[1,1,64]{2,1,0:T(1,128)S(1)} %copy.34), channel_id=2, replica_groups=mesh['seq'=16,'head'=2] {'seq'}, dimensions={0}, use_global_device_ids=true | all-gather | bytes 4352 | tf_op jit(solution)/shard_map/all_gather | solution.py:14
  68.0 0.2 fusion.19
  68.2 310.7 %all-gather.7.cloned.1.call-done = f32[1024,64,128]{2,1,0:T(8,128)} async-done(((f32[64,64,128]{2,1,0:T(8,128)}), f32[1024,64,128]{2,1,0:T(8,128)}) %all-gather.7.cloned.1.call-update) | async-done | bytes 33554448 | tf_op jit(solution)/shard_map/all_gather | solution.py:14
  378.9 31.8 %while.14 = (s32[]{:T(128)}, f32[64,64,128]{2,1,0:T(8,128)S(1)}, s32[]{:T(128)}, f32[16,64]{1,0:T(8,128)S(1)}, f32[16,64,64,128]{3,2,1,0:T(8,128)}, /*index=5*/s32[]{:T(128)}, s32[]{:T(128)}) while((s32[]{:T(128)}, f32[64,64,128]{2,1,0:T(8,128)S(1)}, s32[]{:T(128)}, f32[16,64]{1,0:T(8,128)S(1)}, f32[16,64,64,128]{3,2,1,0:T(8,128)}, ...), condition=%wide.region_3.4_spmd.clone, body=%wide.region_2.3_spmd.clone.sunk | while | flops 2097156 | bytes 6292329 | solution.py:23
  378.9 2.1 fusion.30
  381.1 2.1 fusion.30
  383.2 2.1 fusion.30
  385.3 2.1 fusion.30
  387.4 2.1 fusion.30
  389.6 2.1 fusion.30
  391.7 2.1 fusion.30
  393.8 2.1 fusion.30
  395.9 2.1 fusion.30
  398.1 2.1 fusion.30
  400.2 2.1 fusion.30
  402.3 2.1 fusion.30
  404.4 2.1 fusion.30
  406.6 2.1 fusion.30
  408.7 2.1 fusion.30
  410.8 0.0 copy-start.3
  410.8 0.7 fusion.14
  411.5 0.9 copy-done.3
  412.4 5.9 %bitcast_add_fusion.1 = f32[1,256,64,64]{1,3,2,0:T(8,128)} fusion(f32[256,64,64]{0,2,1:T(8,128)S(1)} %fusion.14, f32[64,256]{1,0:T(8,128)S(1)} %bitcast_add_fusion.2, f32[256,256]{1,0:T(8,128)S(1)} %fusion.19, pred[256,256]{1,0:T(8,128)(4,1)S(1)} %iota_compare_fusion, f32[256,64]{0,1:T(8,128)S(1)} %bitcast.79, f32[256,64]{0,1:T(8,128)S(1)} %copy-done.5, ...), kind=kOutput, calls=%fused_computation.16 | convolution fusion | flops 558891008 | bytes 11010048 | tf_op jit(solution)/shard_map/chts,cshp->cthp/dot_general | solution.py:56
  418.2 0.0 copy-start.2
  418.2 5.8 %copy.35 = f32[256,4096]{1,0:T(8,128)} copy(f32[256,4096]{0,1:T(8,128)} %bitcast.72) | data formatting | bytes 8388608 | tf_op jit(solution)/shard_map/reshape | solution.py:73
  424.0 0.0 copy-done.2
  424.0 0.0 copy-start.6
  424.0 3.7 multiply_reduce_fusion
  427.8 2.5 psum.7
  430.2 0.0 copy-start.1
  430.2 0.0 copy-done.6
  430.2 6.0 %multiply_convert_fusion.2 = bf16[256,4096]{1,0:T(8,128)(2,1)} fusion(f32[4096]{0:T(1024)S(1)} %copy-done.6, f32[256]{0:T(256)S(1)} %add_rsqrt_fusion, f32[256,4096]{1,0:T(8,128)} %copy.35, bf16[256,4096]{1,0:T(8,128)(2,1)} %param.12), kind=kLoop, calls=%fused_computation.21 | loop fusion | flops 9437184 | bytes 8406016 | tf_op jit(solution)/shard_map/convert_element_type | solution.py:78
  436.2 0.0 copy-done.1
  (24 shorter events, 0.3 us)
Async XLA Ops:
  6.5 15.7 %copy-start = (bf16[4096,256]{1,0:T(8,128)(2,1)S(1)}, bf16[4096,256]{1,0:T(8,128)(2,1)}, u32[]{:S(2)}) copy-start(bf16[4096,256]{1,0:T(8,128)(2,1)} %param.10) | copy-start | bytes 6291460
  6.5 8.1 %copy-start.5 = (f32[256,64]{0,1:T(8,128)S(1)}, f32[256,64]{0,1:T(8,128)}, u32[]{:S(2)}) copy-start(f32[256,64]{0,1:T(8,128)} %param.13) | copy-start | bytes 196612
  6.5 15.7 %all-gather.5.cloned.1.call-start = ((), (), s32[]{:S(2)}) async-start(), calls=%async_computation | async-start | bytes 3145728 | tf_op jit(solution)/shard_map/all_gather | solution.py:34
  7.3 371.7 %all-gather.7.cloned.1.call-start = ((), (), s32[]{:S(2)}) async-start(), calls=%async_computation.1 | async-start | bytes 35651584 | tf_op jit(solution)/shard_map/all_gather | solution.py:14
  22.2 2.5 copy-start.4
  410.8 1.6 copy-start.3
  418.2 5.8 %copy-start.2 = (bf16[256,4096]{1,0:T(8,128)(2,1)S(1)}, bf16[256,4096]{1,0:T(8,128)(2,1)}, u32[]{:S(2)}) copy-start(bf16[256,4096]{1,0:T(8,128)(2,1)} %param.12) | copy-start | bytes 6291460
  424.0 6.2 %copy-start.6 = (f32[4096]{0:T(1024)S(1)}, f32[4096]{0:T(1024)}, u32[]{:S(2)}) copy-start(f32[4096]{0:T(1024)} %param.15) | copy-start | bytes 49156
  430.2 6.0 %copy-start.1 = (bf16[4096,256]{1,0:T(8,128)(2,1)S(1)}, bf16[4096,256]{1,0:T(8,128)(2,1)}, u32[]{:S(2)}) copy-start(bf16[4096,256]{1,0:T(8,128)(2,1)} %param.10) | copy-start | bytes 6291460
Sparse Core Ops, SparseCore 0:
  8.9 13.2 all-gather.4
  26.9 352.0 all-gather.6
where the time goes:
time: 444 us; the launch traced here: 443 us
  waiting for transfers between devices  316 us (71%)
  other arithmetic  46.1 us (10%)
  blocking collectives  43.6 us (10%)
  between operations  13.5 us (3%)
  local copies, waits for them, and re-layouts  12.5 us (3%)
  matrix products  11.2 us (3%)
    all_gather x1, waiting for transfers between devices, carried_in(): pieces = jax.tree.map(lambda part: lax.all_gather(part, axis), value)  311 us
    all_gather x1, blocking collectives, carried_in(): pieces = jax.tree.map(lambda part: lax.all_gather(part, axis), value)  41.1 us
    select_n x15, other arithmetic, step(): jnp.where(position < mine, new, old)  31.2 us
  transfers between devices with their start and end apart: 2, of which 2 were waited for; matrix products, arithmetic and copies ran while one was open for 2% of the time, Pallas kernels for 0%

commit v1 on v0

v1 whole, which is shorter than its diff:
```python
import functools

import jax
import jax.numpy as jnp
from jax import lax
from jax.experimental import pallas as pl
from jax.experimental.pallas import tpu as pltpu
from jax.sharding import PartitionSpec as P

HEAD_DIM = 64
STATE = 128
GROUP = 256
EPS = 1e-05
EXTRA = 16
LIMIT = 48 * 1024 * 1024

F32 = jnp.float32
BF16 = jnp.bfloat16


def params():
    return pltpu.CompilerParams(vmem_limit_bytes=LIMIT)


def cost(flops, moved, exps=0):
    return pl.CostEstimate(flops=flops, bytes_accessed=moved, transcendentals=exps)


def halves(value, count):
    terms = []
    for _ in range(count):
        term = value.astype(BF16)
        terms.append(term)
        value = value - term.astype(F32)
    return jnp.concatenate(terms, axis=1)


def spread(value, first_head, heads, lanes, width, count):
    row = lax.broadcasted_iota(jnp.int32, (heads, lanes), 0)
    col = lax.broadcasted_iota(jnp.int32, (heads, lanes), 1)
    pick = jnp.where(row == first_head + col // width, 1.0, 0.0).astype(BF16)
    pick = jnp.concatenate([pick] * count, axis=0)
    return jnp.dot(halves(value, count), pick, preferred_element_type=F32)


def project_kernel(which, hidden, weight, out):
    @pl.when(pl.program_id(0) == 0)
    def _():
        out[...] = jnp.zeros_like(out)

    out[...] += jnp.dot(hidden[...], weight[...], preferred_element_type=F32)


def project(which, hidden, weight):
    rows, depth = hidden.shape
    cols = weight.shape[1]
    tiles = 4
    tile = depth // tiles
    return pl.pallas_call(
        project_kernel,
        grid_spec=pltpu.PrefetchScalarGridSpec(
            num_scalar_prefetch=1,
            grid=(tiles,),
            in_specs=[
                pl.BlockSpec((rows, tile), lambda k, w: (0, k)),
                pl.BlockSpec((tile, cols), lambda k, w: (w[0] * tiles + k, 0)),
            ],
            out_specs=pl.BlockSpec((rows, cols), lambda k, w: (0, 0)),
        ),
        out_shape=jax.ShapeDtypeStruct((rows, cols), F32),
        compiler_params=params(),
        cost_estimate=cost(2 * rows * depth * cols, 2 * rows * depth + 2 * depth * cols),
        name="project",
    )(which, hidden, weight)


def decay_kernel(step, rate, x, weighted, cum, cum_rows, ends, held):
    rows, heads = step.shape
    lanes = x.shape[1]
    at = pl.program_id(0)

    @pl.when(at == 0)
    def _():
        log_decay = -step[...] * rate[...]
        t = lax.broadcasted_iota(jnp.int32, (rows, rows), 0)
        s = lax.broadcasted_iota(jnp.int32, (rows, rows), 1)
        lower = jnp.where(s <= t, 1.0, 0.0).astype(BF16)
        parts = jnp.dot(lower, halves(log_decay, 3), preferred_element_type=F32)
        total = parts[:, :heads] + (parts[:, heads : 2 * heads] + parts[:, 2 * heads :])
        cum[...] = total
        cum_rows[...] = total.T
        held[:rows, :] = jnp.exp(total[rows - 1 :, :] - total) * step[...]
        held[rows:, :] = jnp.broadcast_to(jnp.exp(total[rows - 1 :, :]), (16, heads))

    wide = spread(held[...], at * (lanes // HEAD_DIM), heads, lanes, HEAD_DIM, 3)
    weighted[...] = (x[...].astype(F32) * wide[:rows]).astype(BF16)
    last = wide[rows:]
    high = last.astype(BF16).astype(F32)
    middle = (last - high).astype(BF16).astype(F32)
    low = last - high - middle
    row = lax.broadcasted_iota(jnp.int32, last.shape, 0)
    ends[...] = jnp.where(row == 0, high, jnp.where(row == 1, middle, low)).astype(BF16)


def decays(step, rate, x):
    rows, heads = step.shape
    cols = x.shape[1]
    tiles = min(4, cols // STATE)
    tile = cols // tiles
    whole = lambda i: (0, 0)
    return pl.pallas_call(
        decay_kernel,
        grid=(tiles,),
        in_specs=[
            pl.BlockSpec((rows, heads), whole),
            pl.BlockSpec((1, heads), whole),
            pl.BlockSpec((rows, tile), lambda i: (0, i)),
        ],
        out_specs=[
            pl.BlockSpec((rows, tile), lambda i: (0, i)),
            pl.BlockSpec((rows, heads), whole),
            pl.BlockSpec((heads, rows), whole),
            pl.BlockSpec((16, tile), lambda i: (0, i)),
        ],
        out_shape=[
            jax.ShapeDtypeStruct((rows, cols), BF16),
            jax.ShapeDtypeStruct((rows, heads), F32),
            jax.ShapeDtypeStruct((heads, rows), F32),
            jax.ShapeDtypeStruct((16, cols), BF16),
        ],
        scratch_shapes=[pltpu.VMEM((rows + 16, heads), F32)],
        compiler_params=params(),
        cost_estimate=cost(2 * rows * cols * 256, 4 * rows * cols, 2 * rows * heads),
        name="decays",
    )(step, rate, x)


def fresh_kernel(place, size, parts, weighted, ends, proj, *slices):
    total = parts[0][...]
    for part in parts[1:]:
        total = total + part[...]
    rounded = total.astype(BF16)
    proj[...] = rounded
    width = weighted.shape[1] // size
    b_rows = rounded[:, :STATE]
    for m in range(size):
        owner = place[0] ^ m
        cols = pl.ds(pl.multiple_of(owner * width, width), width)
        state = lax.dot_general(
            b_rows, weighted[:, cols], (((0,), (0,)), ((), ())), preferred_element_type=F32
        )
        slices[m][:STATE, :] = state.astype(BF16)
        slices[m][STATE:, :] = ends[:, cols]


def fresh_states(place, size, parts, weighted, ends):
    rows, cols = weighted.shape
    width = cols // size
    n = len(parts)

    def body(place, *refs):
        fresh_kernel(place, size, refs[:n], *refs[n:])

    return pl.pallas_call(
        body,
        in_specs=[pl.BlockSpec(memory_space=pltpu.SMEM)]
        + [pl.BlockSpec(memory_space=pltpu.VMEM)] * (n + 2),
        out_specs=[pl.BlockSpec(memory_space=pltpu.VMEM)] * (1 + size),
        out_shape=[jax.ShapeDtypeStruct((rows, 2 * STATE), BF16)]
        + [jax.ShapeDtypeStruct((STATE + EXTRA, width), BF16)] * size,
        compiler_params=params(),
        cost_estimate=cost(2 * rows * cols * STATE, 4 * rows * cols),
        name="fresh",
    )(place, *parts, weighted, ends)


def gather_order(place, size, slices, states, factors):
    for m in range(size):
        at = place[0] ^ m
        states[at] = slices[m][:STATE, :].astype(F32)
        tail = slices[m][STATE:, :].astype(F32)
        factors[at] = tail[:8, :]


def factor_of(factors, j):
    tail = factors[j]
    return tail[0:1] + (tail[1:2] + tail[2:3])


def total_kernel(size, place, *refs):
    slices, (out, decay, states, factors) = refs[:size], refs[size:]
    gather_order(place, size, slices, states, factors)
    running = states[0]
    product = factor_of(factors, 0)
    for j in range(1, size):
        step = factor_of(factors, j)
        running = running * step + states[j]
        product = product * step
    out[...] = running.astype(BF16)
    decay[...] = jnp.broadcast_to(product, decay.shape)


def group_total(place, slices):
    size = len(slices)
    width = slices[0].shape[1]
    return pl.pallas_call(
        functools.partial(total_kernel, size),
        in_specs=[pl.BlockSpec(memory_space=pltpu.SMEM)]
        + [pl.BlockSpec(memory_space=pltpu.VMEM)] * size,
        out_specs=[pl.BlockSpec(memory_space=pltpu.VMEM)] * 2,
        out_shape=[
            jax.ShapeDtypeStruct((STATE, width), BF16),
            jax.ShapeDtypeStruct((8, width), F32),
        ],
        scratch_shapes=[
            pltpu.VMEM((size, STATE, width), F32),
            pltpu.VMEM((size, 8, width), F32),
        ],
        compiler_params=params(),
        cost_estimate=cost(2 * size * STATE * width, 2 * size * STATE * width),
        name="total",
    )(place, *slices)


def enter_kernel(size, place, *refs):
    slices, before, outs = refs[:size], refs[size], refs[size + 1 : 2 * size + 1]
    states, factors = refs[2 * size + 1 :]
    gather_order(place, size, slices, states, factors)
    running = before[...].astype(F32)
    for j in range(size):
        following = running * factor_of(factors, j) + states[j]
        states[j] = running
        running = following
    for m in range(size):
        outs[m][...] = states[place[0] ^ m].astype(BF16)


def entering_states(place, slices, before):
    size = len(slices)
    width = slices[0].shape[1]
    return pl.pallas_call(
        functools.partial(enter_kernel, size),
        in_specs=[pl.BlockSpec(memory_space=pltpu.SMEM)]
        + [pl.BlockSpec(memory_space=pltpu.VMEM)] * (size + 1),
        out_specs=[pl.BlockSpec(memory_space=pltpu.VMEM)] * size,
        out_shape=[jax.ShapeDtypeStruct((STATE, width), BF16)] * size,
        scratch_shapes=[
            pltpu.VMEM((size, STATE, width), F32),
            pltpu.VMEM((size, 8, width), F32),
        ],
        compiler_params=params(),
        cost_estimate=cost(2 * size * STATE * width, 4 * size * STATE * width),
        name="entering",
    )(place, *slices, before)


def inner_kernel(heads, proj, cum, cum_rows, step, x, gate, base, slope, scores, mixed):
    rows = cum.shape[0]
    lanes = x.shape[1]
    here = lanes // HEAD_DIM
    half = rows // 2
    at = pl.program_id(0)

    @pl.when(at == 0)
    def _():
        scores[...] = lax.dot_general(
            proj[:, STATE:], proj[:, :STATE], (((1,), (1,)), ((), ())), preferred_element_type=F32
        )

    first = at * here
    columns = spread(cum[...], first, heads, here * STATE, STATE, 3)
    scaled = (x[...].astype(F32) * spread(step[...], first, heads, lanes, HEAD_DIM, 3)).astype(BF16)
    t = lax.broadcasted_iota(jnp.int32, (half, half), 0)
    s = lax.broadcasted_iota(jnp.int32, (half, half), 1)
    causal = s <= t
    for k in range(here):
        col = columns[:, k * STATE : (k + 1) * STATE]
        row = cum_rows[k : k + 1, :]
        blocks = []
        for i, j in ((0, 0), (1, 0), (1, 1)):
            gap = col[i * half : (i + 1) * half] - row[:, j * half : (j + 1) * half]
            if i == j:
                gap = jnp.where(causal, gap, -jnp.inf)
            piece = scores[i * half : (i + 1) * half, j * half : (j + 1) * half]
            blocks.append((piece * jnp.exp(gap)).astype(BF16))
        mine = scaled[:, k * HEAD_DIM : (k + 1) * HEAD_DIM]
        mixed[:half, k * HEAD_DIM : (k + 1) * HEAD_DIM] = jnp.dot(
            blocks[0], mine[:half], preferred_element_type=F32
        )
        mixed[half:, k * HEAD_DIM : (k + 1) * HEAD_DIM] = jnp.dot(
            jnp.concatenate(blocks[1:], axis=1), mine, preferred_element_type=F32
        )
    g = gate[...].astype(F32)
    silu = g / (1.0 + jnp.exp(-g))
    grown = spread(jnp.exp(cum[...]), first, heads, lanes, HEAD_DIM, 3)
    base[...] = mixed[...] * silu
    slope[...] = grown * silu


def inside(proj, cum, cum_rows, step, x, gate):
    rows, heads = step.shape
    cols = x.shape[1]
    here = min(8, heads)
    tile = here * HEAD_DIM
    whole = lambda i: (0, 0)
    part = lambda i: (0, i)
    return pl.pallas_call(
        functools.partial(inner_kernel, heads),
        grid=(heads // here,),
        in_specs=[
            pl.BlockSpec((rows, 2 * STATE), whole),
            pl.BlockSpec((rows, heads), whole),
            pl.BlockSpec((here, rows), lambda i: (i, 0)),
            pl.BlockSpec((rows, heads), whole),
            pl.BlockSpec((rows, tile), part),
            pl.BlockSpec((rows, tile), part),
        ],
        out_specs=[pl.BlockSpec((rows, tile), part)] * 2,
        out_shape=[jax.ShapeDtypeStruct((rows, cols), F32)] * 2,
        scratch_shapes=[pltpu.VMEM((rows, rows), F32), pltpu.VMEM((rows, tile), F32)],
        compiler_params=params(),
        cost_estimate=cost(8 * rows * rows * cols, 12 * rows * cols, rows * rows * heads),
        name="inner",
    )(proj, cum, cum_rows, step, x, gate)


def outer_kernel(size, place, proj, base, slope, *refs):
    states, (gated, squares) = refs[:size], refs[size:]
    c_rows = proj[:, STATE:]
    width = base.shape[1] // size
    total = jnp.zeros(squares.shape, F32)
    for m in range(size):
        cols = pl.ds(pl.multiple_of((place[0] ^ m) * width, width), width)
        read = jnp.dot(c_rows, states[m][...], preferred_element_type=F32)
        value = base[:, cols] + slope[:, cols] * read
        gated[:, cols] = value
        square = value * value
        for k in range(width // STATE):
            total = total + square[:, k * STATE : (k + 1) * STATE]
    squares[...] = total


def outer_part(place, proj, base, slope, states):
    size = len(states)
    rows, cols = base.shape
    return pl.pallas_call(
        functools.partial(outer_kernel, size),
        in_specs=[pl.BlockSpec(memory_space=pltpu.SMEM)]
        + [pl.BlockSpec(memory_space=pltpu.VMEM)] * (size + 3),
        out_specs=[pl.BlockSpec(memory_space=pltpu.VMEM)] * 2,
        out_shape=[
            jax.ShapeDtypeStruct((rows, cols), F32),
            jax.ShapeDtypeStruct((rows, STATE), F32),
        ],
        compiler_params=params(),
        cost_estimate=cost(2 * rows * cols * STATE, 12 * rows * cols),
        name="outer",
    )(place, proj, base, slope, *states)


def norm_kernel(count, n, *refs):
    parts, (gated, gain, out) = refs[:n], refs[n:]
    total = parts[0][...]
    for part in parts[1:]:
        total = total + part[...]
    mean = jnp.sum(total, axis=1, keepdims=True) * (1.0 / count)
    out[...] = (gated[...] * lax.rsqrt(mean + EPS) * gain[...]).astype(BF16)


def normalise(count, parts, gated, gain):
    rows, cols = gated.shape
    n = len(parts)
    tiles = 4
    tile = rows // tiles
    row = lambda i: (i, 0)
    return pl.pallas_call(
        functools.partial(norm_kernel, count, n),
        grid=(tiles,),
        in_specs=[pl.BlockSpec((tile, STATE), row)] * n
        + [pl.BlockSpec((tile, cols), row), pl.BlockSpec((1, cols), lambda i: (0, 0))],
        out_specs=pl.BlockSpec((tile, cols), row),
        out_shape=jax.ShapeDtypeStruct((rows, cols), BF16),
        compiler_params=params(),
        cost_estimate=cost(4 * rows * cols, 6 * rows * cols),
        name="norm",
    )(*parts, gated, gain)


def swap(value, axis, mask):
    pairs = [(i, i ^ mask) for i in range(lax.axis_size(axis))]
    return lax.ppermute(value, axis, pairs)


def terms_of_sum(value, axis):
    mask = 1
    terms = [value]
    while mask < lax.axis_size(axis):
        if len(terms) > 1:
            terms = [sum(terms[1:], terms[0])]
        terms.append(swap(terms[0], axis, mask))
        mask *= 2
    return terms


def shards(hidden, weight, head_input, gate_input, step, rate, gain):
    heads = step.shape[1]
    devices = lax.axis_size("seq")
    size = 8
    while devices % size or heads % size or (heads // size * HEAD_DIM) % STATE:
        size //= 2
    groups = devices // size
    place = (lax.axis_index("seq") % size).astype(jnp.int32).reshape(1)
    which = lax.axis_index("head").astype(jnp.int32).reshape(1)

    with jax.named_scope("projection"):
        parts = terms_of_sum(project(which, hidden, weight), "head")
    with jax.named_scope("decays"):
        weighted, cum, cum_rows, ends = decays(step, rate.reshape(1, heads), head_input)
    with jax.named_scope("states"):
        proj, *mine = fresh_states(place, size, parts, weighted, ends)
    with jax.named_scope("to_owners"):
        slices = [mine[0]] + [swap(mine[m], "seq", m) for m in range(1, size)]
    with jax.named_scope("groups"):
        total, decay = group_total(place, slices)
        up = [(i, i + size) for i in range(devices - size)]
        before = jnp.zeros_like(total)
        for k in range(groups - 1):
            if k > 0:
                sent = (before.astype(F32) * decay[:1] + total.astype(F32)).astype(BF16)
            else:
                sent = total
            before = lax.ppermute(sent, "seq", up)
    with jax.named_scope("inner"):
        base, slope = inside(proj, cum, cum_rows, step, head_input, gate_input)
    with jax.named_scope("from_owners"):
        outs = entering_states(place, slices, before)
        states = [outs[0]] + [swap(outs[m], "seq", m) for m in range(1, size)]
    with jax.named_scope("outer"):
        gated, squares = outer_part(place, proj, base, slope, states)
    with jax.named_scope("norm"):
        count = head_input.shape[1] * lax.axis_size("head")
        sums = terms_of_sum(squares, "head")
        return normalise(count, sums, gated, gain.reshape(1, -1))


def solution(mesh):
    in_specs = (
        P("seq", "head"),
        P(),
        P("seq", "head"),
        P("seq", "head"),
        P("seq", "head"),
        P("head"),
        P("head"),
    )
    return jax.shard_map(
        shards, mesh=mesh, in_specs=in_specs, out_specs=P("seq", "head"), check_vma=False
    )
```

time: 444 us -> 67.9 us (0.15)
  waiting for transfers between devices: 316 us -> 13.2 us
  other arithmetic: 46.1 us -> 0 us
  blocking collectives: 43.6 us -> 0 us
  starting transfers between devices: 0.04 us -> 28.6 us
  Pallas kernels: 0 us -> 22.3 us
  between operations: 13.5 us -> 0.14 us
  matrix products: 11.2 us -> 0 us
  local copies, waits for them, and re-layouts: 12.5 us -> 3.08 us
    all_gather x2 -> x0, waiting for transfers between devices: 315 us -> none  [the longest x1 311 us: carried_in(): pieces = jax.tree.map(lambda part: lax.all_gather(part, axis), value)]
    all_gather x1 -> x0, blocking collectives: 41.1 us -> none  [carried_in(): pieces = jax.tree.map(lambda part: lax.all_gather(part, axis), value)]
    select_n x15 -> x0, other arithmetic: 31.2 us -> none  [step(): jnp.where(position < mine, new, old)]
    ppermute x0 -> x17, starting transfers between devices: none -> 28.6 us  [the longest x16 24.1 us: swap(): return lax.ppermute(value, axis, pairs)]
    pallas_call x0 -> x8, Pallas kernels: none -> 22.3 us  [the longest x1 10.3 us: inside(): pl.pallas_call(functools.partial(inner_kernel, heads), grid=(heads // her...]
    ppermute x0 -> x17, waiting for transfers between devices: none -> 13.2 us  [the longest x16 10.7 us: swap(): return lax.ppermute(value, axis, pairs)]
    dot_general x5 -> x0, matrix products: 11.2 us -> none  [the longest x1 5.86 us: shards(): jnp.einsum('chts,cshp->cthp', mixing, scaled, preferred_element_type=jnp....]
    convert_element_type x2 -> x0, other arithmetic: 9.37 us -> none  [the longest x1 5.98 us: shards(): (gated * lax.rsqrt(mean_square + 1e-05)[:, None] * norm_gain[None, :]).as...]
  transfers between devices with their start and end apart: 2 -> 17, of which waited for: 2 -> 6; matrix products, arithmetic and copies ran while one was open for 2% -> 0% of each run, Pallas kernels for 0% -> 19%
where the time goes in v1:
time: 67.9 us; the launch traced here: 67.3 us
  starting transfers between devices  28.6 us (42%)
  Pallas kernels  22.3 us (33%)
  waiting for transfers between devices  13.2 us (19%)
  local copies, waits for them, and re-layouts  3.08 us (5%)
    ppermute x16, starting transfers between devices, swap(): return lax.ppermute(value, axis, pairs)  24.1 us
    ppermute x16, waiting for transfers between devices, swap(): return lax.ppermute(value, axis, pairs)  10.7 us
    pallas_call x1, Pallas kernels, inside(): pl.pallas_call(functools.partial(inner_kernel, heads), grid=(heads // her...  10.3 us
    ppermute x1, starting transfers between devices, shards(): before = lax.ppermute(sent, 'seq', up)  4.49 us
    pallas_call x1, Pallas kernels, outer_part(): pl.pallas_call(functools.partial(outer_kernel, size), in_specs=[pl.BlockS...  4.22 us
    unnamed x15, local copies, waits for them, and re-layouts  3.08 us
    ppermute x1, waiting for transfers between devices, shards(): before = lax.ppermute(sent, 'seq', up)  2.51 us
    pallas_call x1, Pallas kernels, normalise(): pl.pallas_call(functools.partial(norm_kernel, count, n), grid=(tiles,), i...  2.37 us
  transfers between devices with their start and end apart: 17, of which 6 were waited for; matrix products, arithmetic and copies ran while one was open for 0% of the time, Pallas kernels for 19%

profile of v1, /device:TPU:0, one launch (start us, length us, event | category | flops | bytes accessed | tf_op | source)
XLA Modules:
  0.0 67.3 jit_solution(1944941811672989511)
XLA Ops:
  0.0 0.0 copy-start
  0.0 0.0 copy-start.1
  0.0 1.7 %copy-done.1 = bf16[4096,256]{1,0:T(8,128)(2,1)S(1)} copy-done((bf16[4096,256]{1,0:T(8,128)(2,1)S(1)}, bf16[4096,256]{1,0:T(8,128)(2,1)}, u32[]{:S(2)}) %copy-start.1) | copy-done | bytes 2097176
  1.7 0.0 copy-start.2
  1.7 1.2 %copy-done.2 = bf16[256,2048]{1,0:T(8,128)(2,1)S(1)} copy-done((bf16[256,2048]{1,0:T(8,128)(2,1)S(1)}, bf16[256,2048]{1,0:T(8,128)(2,1)}, u32[]{:S(2)}) %copy-start.2) | copy-done | bytes 1048600
  3.0 0.0 copy-start.6
  3.0 0.0 copy-start.4
  3.0 1.1 %project.1.refs_0_ = f32[256,256]{1,0:T(8,128)S(1)} custom-call(s32[1]{0:T(128)} %bitcast.1.which, bf16[256,2048]{1,0:T(8,128)(2,1)S(1)} %copy-done.2, bf16[4096,256]{1,0:T(8,128)(2,1)S(1)} %copy-done.1), custom_call_target="tpu_custom_call" | custom-call | flops 268435456 | bytes 2097152 | tf_op jit(solution)/shard_map/projection/project/pallas_call | solution.py:59
  4.1 0.5 collective-permute-start
  4.6 0.0 copy-done.6
  4.6 0.1 copy.8.step
  4.7 0.0 copy-done
  4.7 0.0 copy-done.4
  4.7 2.2 %decays.1 = (bf16[256,4096]{1,0:T(8,128)(2,1)S(1)}, f32[256,64]{1,0:T(8,128)S(1)}, f32[64,256]{1,0:T(8,128)S(1)}, bf16[16,4096]{1,0:T(8,128)(2,1)S(1)}) custom-call(f32[256,64]{1,0:T(8,128)S(1)} %copy.8.step, f32[1,64]{1,0:T(1,128)S(1)} %bitcast.5, bf16[256,4096]{1,0:T(8,128)(2,1)S(1)} %copy-done), custom_call_target="tpu_custom_call" | custom-call | flops 536870912 | bytes 4194304 | tf_op jit(solution)/shard_map/decays/decays/pallas_call | solution.py:111
  7.0 0.0 collective-permute-done.refs_1_
  7.0 0.0 copy-start.5
  7.0 0.5 fresh.1
  7.5 2.6 %collective-permute-start.1 = (bf16[144,512]{1,0:T(8,128)(2,1)S(1)}, bf16[144,512]{1,0:T(8,128)(2,1)S(1)}, u32[]{:S(2)}, u32[]{:S(2)}) collective-permute-start(bf16[144,512]{1,0:T(8,128)(2,1)S(1)} %get-tuple-element.39), channel_id=1, source_target_pairs={{0,2},{2,0},{4,6},{6,4},{8,10},{10,8},{12,14},{14,12},{16,18},{18,... | collective-permute-start | bytes 442376 | tf_op jit(solution)/shard_map/to_owners/ppermute | solution.py:391
  10.1 1.5 %collective-permute-start.2 = (bf16[144,512]{1,0:T(8,128)(2,1)S(1)}, bf16[144,512]{1,0:T(8,128)(2,1)S(1)}, u32[]{:S(2)}, u32[]{:S(2)}) collective-permute-start(bf16[144,512]{1,0:T(8,128)(2,1)S(1)} %get-tuple-element.40), channel_id=1, source_target_pairs={{0,4},{2,6},{4,0},{6,2},{8,12},{10,14},{12,8},{14,10},{16,20},{18,... | collective-permute-start | bytes 442376 | tf_op jit(solution)/shard_map/to_owners/ppermute | solution.py:391
  11.6 0.0 collective-permute-start.3
  11.6 2.0 %collective-permute-start.4 = (bf16[144,512]{1,0:T(8,128)(2,1)S(1)}, bf16[144,512]{1,0:T(8,128)(2,1)S(1)}, u32[]{:S(2)}, u32[]{:S(2)}) collective-permute-start(bf16[144,512]{1,0:T(8,128)(2,1)S(1)} %get-tuple-element.42), channel_id=1, source_target_pairs={{0,8},{2,10},{4,12},{6,14},{8,0},{10,2},{12,4},{14,6},{16,24},{18,... | collective-permute-start | bytes 442376 | tf_op jit(solution)/shard_map/to_owners/ppermute | solution.py:391
  13.6 1.4 %collective-permute-start.5 = (bf16[144,512]{1,0:T(8,128)(2,1)S(1)}, bf16[144,512]{1,0:T(8,128)(2,1)S(1)}, u32[]{:S(2)}, u32[]{:S(2)}) collective-permute-start(bf16[144,512]{1,0:T(8,128)(2,1)S(1)} %get-tuple-element.43), channel_id=1, source_target_pairs={{0,10},{2,8},{4,14},{6,12},{8,2},{10,0},{12,6},{14,4},{16,26},{18,... | collective-permute-start | bytes 442376 | tf_op jit(solution)/shard_map/to_owners/ppermute | solution.py:391
  15.0 0.0 collective-permute-done.1.refs_1_
  15.0 2.7 %collective-permute-start.6 = (bf16[144,512]{1,0:T(8,128)(2,1)S(1)}, bf16[144,512]{1,0:T(8,128)(2,1)S(1)}, u32[]{:S(2)}, u32[]{:S(2)}) collective-permute-start(bf16[144,512]{1,0:T(8,128)(2,1)S(1)} %get-tuple-element.44), channel_id=1, source_target_pairs={{0,12},{2,14},{4,8},{6,10},{8,4},{10,6},{12,0},{14,2},{16,28},{18,... | collective-permute-start | bytes 442376 | tf_op jit(solution)/shard_map/to_owners/ppermute | solution.py:391
  17.7 0.6 collective-permute-done.2.refs_2_
  18.4 1.7 %collective-permute-start.7 = (bf16[144,512]{1,0:T(8,128)(2,1)S(1)}, bf16[144,512]{1,0:T(8,128)(2,1)S(1)}, u32[]{:S(2)}, u32[]{:S(2)}) collective-permute-start(bf16[144,512]{1,0:T(8,128)(2,1)S(1)} %get-tuple-element.45), channel_id=1, source_target_pairs={{0,14},{2,12},{4,10},{6,8},{8,6},{10,4},{12,2},{14,0},{16,30},{18,... | collective-permute-start | bytes 442376 | tf_op jit(solution)/shard_map/to_owners/ppermute | solution.py:391
  20.1 0.0 collective-permute-done.3.refs_3_
  20.1 0.0 collective-permute-done.4.refs_4_
  20.1 2.8 %collective-permute-done.5.refs_5_ = bf16[144,512]{1,0:T(8,128)(2,1)S(1)} collective-permute-done((bf16[144,512]{1,0:T(8,128)(2,1)S(1)}, bf16[144,512]{1,0:T(8,128)(2,1)S(1)}, u32[]{:S(2)}, u32[]{:S(2)}) %collective-permute-start.5) | collective-permute-done | bytes 147488 | tf_op jit(solution)/shard_map/to_owners/ppermute | solution.py:391
  22.9 2.8 %collective-permute-done.6.refs_6_ = bf16[144,512]{1,0:T(8,128)(2,1)S(1)} collective-permute-done((bf16[144,512]{1,0:T(8,128)(2,1)S(1)}, bf16[144,512]{1,0:T(8,128)(2,1)S(1)}, u32[]{:S(2)}, u32[]{:S(2)}) %collective-permute-start.6) | collective-permute-done | bytes 147488 | tf_op jit(solution)/shard_map/to_owners/ppermute | solution.py:391
  25.7 3.1 %collective-permute-done.7.refs_7_ = bf16[144,512]{1,0:T(8,128)(2,1)S(1)} collective-permute-done((bf16[144,512]{1,0:T(8,128)(2,1)S(1)}, bf16[144,512]{1,0:T(8,128)(2,1)S(1)}, u32[]{:S(2)}, u32[]{:S(2)}) %collective-permute-start.7) | collective-permute-done | bytes 147488 | tf_op jit(solution)/shard_map/to_owners/ppermute | solution.py:391
  28.8 1.0 %total.1 = (bf16[128,512]{1,0:T(8,128)(2,1)S(1)}, f32[8,512]{1,0:T(8,128)}) custom-call(s32[1]{0:T(128)} %bitcast.place, bf16[144,512]{1,0:T(8,128)(2,1)S(1)} %get-tuple-element.38.refs_0_, bf16[144,512]{1,0:T(8,128)(2,1)S(1)} %collective-permute-done.1.refs_1_, bf16[144,512]{1,0:T(8,128)(2,1)S(1)} %collective-permute-done.2.refs_2_, ...), custom_call_target="tpu_custom_call" | custom-call | flops 1048576 | bytes 1048576 | tf_op jit(solution)/shard_map/groups/total/pallas_call | solution.py:206
  29.8 4.5 %collective-permute-start.8 = (bf16[128,512]{1,0:T(8,128)(2,1)S(1)}, bf16[128,512]{1,0:T(8,128)(2,1)S(1)}, u32[]{:S(2)}, u32[]{:S(2)}) collective-permute-start(bf16[128,512]{1,0:T(8,128)(2,1)S(1)} %get-tuple-element.46), channel_id=1, source_target_pairs={{0,16},{2,18},{4,20},{6,22},{8,24},{10,26},{12,28},{14,30},{1,17},... | collective-permute-start | bytes 393224 | tf_op jit(solution)/shard_map/groups/ppermute | solution.py:432
  34.3 2.5 %collective-permute-done.8.refs_8_ = bf16[128,512]{1,0:T(8,128)(2,1)S(1)} collective-permute-done((bf16[128,512]{1,0:T(8,128)(2,1)S(1)}, bf16[128,512]{1,0:T(8,128)(2,1)S(1)}, u32[]{:S(2)}, u32[]{:S(2)}) %collective-permute-start.8) | collective-permute-done | bytes 131104 | tf_op jit(solution)/shard_map/groups/ppermute | solution.py:432
  36.8 0.6 entering.1
  37.4 0.8 %collective-permute-start.9 = (bf16[128,512]{1,0:T(8,128)(2,1)S(1)}, bf16[128,512]{1,0:T(8,128)(2,1)S(1)}, u32[]{:S(2)}, u32[]{:S(2)}) collective-permute-start(bf16[128,512]{1,0:T(8,128)(2,1)S(1)} %get-tuple-element.48), channel_id=1, source_target_pairs={{0,2},{2,0},{4,6},{6,4},{8,10},{10,8},{12,14},{14,12},{16,18},{18,... | collective-permute-start | bytes 393224 | tf_op jit(solution)/shard_map/from_owners/ppermute | solution.py:391
  38.3 0.5 collective-permute-start.10
  38.8 2.2 %collective-permute-start.11 = (bf16[128,512]{1,0:T(8,128)(2,1)S(1)}, bf16[128,512]{1,0:T(8,128)(2,1)S(1)}, u32[]{:S(2)}, u32[]{:S(2)}) collective-permute-start(bf16[128,512]{1,0:T(8,128)(2,1)S(1)} %get-tuple-element.50), channel_id=1, source_target_pairs={{0,6},{2,4},{4,2},{6,0},{8,14},{10,12},{12,10},{14,8},{16,22},{18,... | collective-permute-start | bytes 393224 | tf_op jit(solution)/shard_map/from_owners/ppermute | solution.py:391
  41.0 3.4 %collective-permute-start.12 = (bf16[128,512]{1,0:T(8,128)(2,1)S(1)}, bf16[128,512]{1,0:T(8,128)(2,1)S(1)}, u32[]{:S(2)}, u32[]{:S(2)}) collective-permute-start(bf16[128,512]{1,0:T(8,128)(2,1)S(1)} %get-tuple-element.51), channel_id=1, source_target_pairs={{0,8},{2,10},{4,12},{6,14},{8,0},{10,2},{12,4},{14,6},{16,24},{18,... | collective-permute-start | bytes 393224 | tf_op jit(solution)/shard_map/from_owners/ppermute | solution.py:391
  44.4 0.1 collective-permute-start.13
  44.5 0.0 collective-permute-done.9.refs_1_
  44.5 3.9 %collective-permute-start.14 = (bf16[128,512]{1,0:T(8,128)(2,1)S(1)}, bf16[128,512]{1,0:T(8,128)(2,1)S(1)}, u32[]{:S(2)}, u32[]{:S(2)}) collective-permute-start(bf16[128,512]{1,0:T(8,128)(2,1)S(1)} %get-tuple-element.53), channel_id=1, source_target_pairs={{0,12},{2,14},{4,8},{6,10},{8,4},{10,6},{12,0},{14,2},{16,28},{18,... | collective-permute-start | bytes 393224 | tf_op jit(solution)/shard_map/from_owners/ppermute | solution.py:391
  48.4 0.0 collective-permute-done.10.refs_2_
  48.4 0.5 collective-permute-start.15
  48.9 0.0 copy-done.5
  48.9 10.3 %inner.1 = (f32[256,4096]{1,0:T(8,128)}, f32[256,4096]{1,0:T(8,128)}) custom-call(bf16[256,256]{1,0:T(8,128)(2,1)S(1)} %get-tuple-element.33.proj, f32[256,64]{1,0:T(8,128)S(1)} %get-tuple-element.34.cum, f32[64,256]{1,0:T(8,128)S(1)} %get-tuple-element.35.cum_rows, f32[256,64]{1,0:T(8,128)S(1)} %copy.8.step, bf16[256,4096]{1,0:T(8,128)(2,1)S(1)} %copy-done, ...), custom_call_target="tpu_custom_call" | custom-call | flops 2147483648 | bytes 12582912 | tf_op jit(solution)/shard_map/inner/inner/pallas_call | solution.py:307
  59.2 0.0 collective-permute-done.11.refs_3_
  59.2 0.0 collective-permute-done.12.refs_4_
  59.2 0.0 collective-permute-done.13.refs_5_
  59.2 0.0 collective-permute-done.14.refs_6_
  59.2 0.0 collective-permute-done.15.refs_7_
  59.2 0.0 copy-start.3
  59.3 4.2 %outer.1 = (f32[256,4096]{1,0:T(8,128)S(1)}, f32[256,128]{1,0:T(8,128)S(1)}) custom-call(s32[1]{0:T(128)} %bitcast.place, bf16[256,256]{1,0:T(8,128)(2,1)S(1)} %get-tuple-element.33.proj, f32[256,4096]{1,0:T(8,128)} %get-tuple-element.36.base, f32[256,4096]{1,0:T(8,128)} %get-tuple-element.37.slope, bf16[128,512]{1,0:T(8,128)(2,1)S(1)} %get-tuple-element.47.refs_0_, ...), custom_call_target="tpu_custom_call" | custom-call | flops 268435456 | bytes 12582912 | tf_op jit(solution)/shard_map/outer/outer/pallas_call | solution.py:346
  63.5 0.1 collective-permute-start.16
  63.6 1.3 %collective-permute-done.16.refs_1_ = f32[256,128]{1,0:T(8,128)S(1)} collective-permute-done((f32[256,128]{1,0:T(8,128)S(1)}, f32[256,128]{1,0:T(8,128)S(1)}, u32[]{:S(2)}, u32[]{:S(2)}) %collective-permute-start.16) | collective-permute-done | bytes 131104 | tf_op jit(solution)/shard_map/norm/ppermute | solution.py:391
  64.9 0.0 copy-done.3
  64.9 2.4 %norm.1 = bf16[256,4096]{1,0:T(8,128)(2,1)} custom-call(f32[256,128]{1,0:T(8,128)S(1)} %get-tuple-element.55.refs_0_, f32[256,128]{1,0:T(8,128)S(1)} %collective-permute-done.16.refs_1_, f32[256,4096]{1,0:T(8,128)S(1)} %get-tuple-element.56.refs_2_, f32[1,4096]{1,0:T(1,128)S(1)} %bitcast.4), custom_call_target="tpu_custom_call" | custom-call | flops 4194304 | bytes 6291456 | tf_op jit(solution)/shard_map/norm/norm/pallas_call | solution.py:376
Async XLA Ops:
  0.0 4.7 %copy-start = (bf16[256,4096]{1,0:T(8,128)(2,1)S(1)}, bf16[256,4096]{1,0:T(8,128)(2,1)}, u32[]{:S(2)}) copy-start(bf16[256,4096]{1,0:T(8,128)(2,1)} %x.3) | copy-start | bytes 6291460
  0.0 1.7 %copy-start.1 = (bf16[4096,256]{1,0:T(8,128)(2,1)S(1)}, bf16[4096,256]{1,0:T(8,128)(2,1)}, u32[]{:S(2)}) copy-start(bf16[4096,256]{1,0:T(8,128)(2,1)} %weight.1) | copy-start | bytes 6291460
  1.7 1.2 %copy-start.2 = (bf16[256,2048]{1,0:T(8,128)(2,1)S(1)}, bf16[256,2048]{1,0:T(8,128)(2,1)}, u32[]{:S(2)}) copy-start(bf16[256,2048]{1,0:T(8,128)(2,1)} %hidden.1) | copy-start | bytes 3145732
  3.0 1.6 %copy-start.6 = (f32[256,64]{0,1:T(8,128)S(1)}, f32[256,64]{0,1:T(8,128)}, u32[]{:S(2)}) copy-start(f32[256,64]{0,1:T(8,128)} %param.11) | copy-start | bytes 196612
  3.0 1.7 %copy-start.4 = (f32[64]{0:T(128)S(1)}, f32[64]{0:T(128)}, u32[]{:S(2)}) copy-start(f32[64]{0:T(128)} %param.12) | copy-start | bytes 772
  4.1 2.9 %collective-permute-start = (f32[256,256]{1,0:T(8,128)S(1)}, f32[256,256]{1,0:T(8,128)S(1)}, u32[]{:S(2)}, u32[]{:S(2)}) collective-permute-start(f32[256,256]{1,0:T(8,128)S(1)} %project.1.refs_0_), channel_id=1, source_target_pairs={{0,1},{1,0},{2,3},{3,2},{4,5},{5,4},{6,7},{7,6},{8,9},{9,8},{10,11... | collective-permute-start | bytes 786440 | tf_op jit(solution)/shard_map/projection/ppermute | solution.py:391
  7.0 42.0 %copy-start.5 = (bf16[256,4096]{1,0:T(8,128)(2,1)S(1)}, bf16[256,4096]{1,0:T(8,128)(2,1)}, u32[]{:S(2)}) copy-start(bf16[256,4096]{1,0:T(8,128)(2,1)} %gate.1) | copy-start | bytes 6291460
  7.5 7.5 %collective-permute-start.1 = (bf16[144,512]{1,0:T(8,128)(2,1)S(1)}, bf16[144,512]{1,0:T(8,128)(2,1)S(1)}, u32[]{:S(2)}, u32[]{:S(2)}) collective-permute-start(bf16[144,512]{1,0:T(8,128)(2,1)S(1)} %get-tuple-element.39), channel_id=1, source_target_pairs={{0,2},{2,0},{4,6},{6,4},{8,10},{10,8},{12,14},{14,12},{16,18},{18,... | collective-permute-start | bytes 442376 | tf_op jit(solution)/shard_map/to_owners/ppermute | solution.py:391
  10.1 8.3 %collective-permute-start.2 = (bf16[144,512]{1,0:T(8,128)(2,1)S(1)}, bf16[144,512]{1,0:T(8,128)(2,1)S(1)}, u32[]{:S(2)}, u32[]{:S(2)}) collective-permute-start(bf16[144,512]{1,0:T(8,128)(2,1)S(1)} %get-tuple-element.40), channel_id=1, source_target_pairs={{0,4},{2,6},{4,0},{6,2},{8,12},{10,14},{12,8},{14,10},{16,20},{18,... | collective-permute-start | bytes 442376 | tf_op jit(solution)/shard_map/to_owners/ppermute | solution.py:391
  11.6 8.5 %collective-permute-start.3 = (bf16[144,512]{1,0:T(8,128)(2,1)S(1)}, bf16[144,512]{1,0:T(8,128)(2,1)S(1)}, u32[]{:S(2)}, u32[]{:S(2)}) collective-permute-start(bf16[144,512]{1,0:T(8,128)(2,1)S(1)} %get-tuple-element.41), channel_id=1, source_target_pairs={{0,6},{2,4},{4,2},{6,0},{8,14},{10,12},{12,10},{14,8},{16,22},{18,... | collective-permute-start | bytes 442376 | tf_op jit(solution)/shard_map/to_owners/ppermute | solution.py:391
  11.6 8.5 %collective-permute-start.4 = (bf16[144,512]{1,0:T(8,128)(2,1)S(1)}, bf16[144,512]{1,0:T(8,128)(2,1)S(1)}, u32[]{:S(2)}, u32[]{:S(2)}) collective-permute-start(bf16[144,512]{1,0:T(8,128)(2,1)S(1)} %get-tuple-element.42), channel_id=1, source_target_pairs={{0,8},{2,10},{4,12},{6,14},{8,0},{10,2},{12,4},{14,6},{16,24},{18,... | collective-permute-start | bytes 442376 | tf_op jit(solution)/shard_map/to_owners/ppermute | solution.py:391
  13.6 9.3 %collective-permute-start.5 = (bf16[144,512]{1,0:T(8,128)(2,1)S(1)}, bf16[144,512]{1,0:T(8,128)(2,1)S(1)}, u32[]{:S(2)}, u32[]{:S(2)}) collective-permute-start(bf16[144,512]{1,0:T(8,128)(2,1)S(1)} %get-tuple-element.43), channel_id=1, source_target_pairs={{0,10},{2,8},{4,14},{6,12},{8,2},{10,0},{12,6},{14,4},{16,26},{18,... | collective-permute-start | bytes 442376 | tf_op jit(solution)/shard_map/to_owners/ppermute | solution.py:391
  15.0 10.7 %collective-permute-start.6 = (bf16[144,512]{1,0:T(8,128)(2,1)S(1)}, bf16[144,512]{1,0:T(8,128)(2,1)S(1)}, u32[]{:S(2)}, u32[]{:S(2)}) collective-permute-start(bf16[144,512]{1,0:T(8,128)(2,1)S(1)} %get-tuple-element.44), channel_id=1, source_target_pairs={{0,12},{2,14},{4,8},{6,10},{8,4},{10,6},{12,0},{14,2},{16,28},{18,... | collective-permute-start | bytes 442376 | tf_op jit(solution)/shard_map/to_owners/ppermute | solution.py:391
  18.4 10.4 %collective-permute-start.7 = (bf16[144,512]{1,0:T(8,128)(2,1)S(1)}, bf16[144,512]{1,0:T(8,128)(2,1)S(1)}, u32[]{:S(2)}, u32[]{:S(2)}) collective-permute-start(bf16[144,512]{1,0:T(8,128)(2,1)S(1)} %get-tuple-element.45), channel_id=1, source_target_pairs={{0,14},{2,12},{4,10},{6,8},{8,6},{10,4},{12,2},{14,0},{16,30},{18,... | collective-permute-start | bytes 442376 | tf_op jit(solution)/shard_map/to_owners/ppermute | solution.py:391
  29.8 7.0 %collective-permute-start.8 = (bf16[128,512]{1,0:T(8,128)(2,1)S(1)}, bf16[128,512]{1,0:T(8,128)(2,1)S(1)}, u32[]{:S(2)}, u32[]{:S(2)}) collective-permute-start(bf16[128,512]{1,0:T(8,128)(2,1)S(1)} %get-tuple-element.46), channel_id=1, source_target_pairs={{0,16},{2,18},{4,20},{6,22},{8,24},{10,26},{12,28},{14,30},{1,17},... | collective-permute-start | bytes 393224 | tf_op jit(solution)/shard_map/groups/ppermute | solution.py:432
  37.4 7.0 %collective-permute-start.9 = (bf16[128,512]{1,0:T(8,128)(2,1)S(1)}, bf16[128,512]{1,0:T(8,128)(2,1)S(1)}, u32[]{:S(2)}, u32[]{:S(2)}) collective-permute-start(bf16[128,512]{1,0:T(8,128)(2,1)S(1)} %get-tuple-element.48), channel_id=1, source_target_pairs={{0,2},{2,0},{4,6},{6,4},{8,10},{10,8},{12,14},{14,12},{16,18},{18,... | collective-permute-start | bytes 393224 | tf_op jit(solution)/shard_map/from_owners/ppermute | solution.py:391
  38.3 10.1 %collective-permute-start.10 = (bf16[128,512]{1,0:T(8,128)(2,1)S(1)}, bf16[128,512]{1,0:T(8,128)(2,1)S(1)}, u32[]{:S(2)}, u32[]{:S(2)}) collective-permute-start(bf16[128,512]{1,0:T(8,128)(2,1)S(1)} %get-tuple-element.49), channel_id=1, source_target_pairs={{0,4},{2,6},{4,0},{6,2},{8,12},{10,14},{12,8},{14,10},{16,20},{18,... | collective-permute-start | bytes 393224 | tf_op jit(solution)/shard_map/from_owners/ppermute | solution.py:391
  38.8 20.5 %collective-permute-start.11 = (bf16[128,512]{1,0:T(8,128)(2,1)S(1)}, bf16[128,512]{1,0:T(8,128)(2,1)S(1)}, u32[]{:S(2)}, u32[]{:S(2)}) collective-permute-start(bf16[128,512]{1,0:T(8,128)(2,1)S(1)} %get-tuple-element.50), channel_id=1, source_target_pairs={{0,6},{2,4},{4,2},{6,0},{8,14},{10,12},{12,10},{14,8},{16,22},{18,... | collective-permute-start | bytes 393224 | tf_op jit(solution)/shard_map/from_owners/ppermute | solution.py:391
  41.0 18.2 %collective-permute-start.12 = (bf16[128,512]{1,0:T(8,128)(2,1)S(1)}, bf16[128,512]{1,0:T(8,128)(2,1)S(1)}, u32[]{:S(2)}, u32[]{:S(2)}) collective-permute-start(bf16[128,512]{1,0:T(8,128)(2,1)S(1)} %get-tuple-element.51), channel_id=1, source_target_pairs={{0,8},{2,10},{4,12},{6,14},{8,0},{10,2},{12,4},{14,6},{16,24},{18,... | collective-permute-start | bytes 393224 | tf_op jit(solution)/shard_map/from_owners/ppermute | solution.py:391
  44.4 14.9 %collective-permute-start.13 = (bf16[128,512]{1,0:T(8,128)(2,1)S(1)}, bf16[128,512]{1,0:T(8,128)(2,1)S(1)}, u32[]{:S(2)}, u32[]{:S(2)}) collective-permute-start(bf16[128,512]{1,0:T(8,128)(2,1)S(1)} %get-tuple-element.52), channel_id=1, source_target_pairs={{0,10},{2,8},{4,14},{6,12},{8,2},{10,0},{12,6},{14,4},{16,26},{18,... | collective-permute-start | bytes 393224 | tf_op jit(solution)/shard_map/from_owners/ppermute | solution.py:391
  44.5 14.8 %collective-permute-start.14 = (bf16[128,512]{1,0:T(8,128)(2,1)S(1)}, bf16[128,512]{1,0:T(8,128)(2,1)S(1)}, u32[]{:S(2)}, u32[]{:S(2)}) collective-permute-start(bf16[128,512]{1,0:T(8,128)(2,1)S(1)} %get-tuple-element.53), channel_id=1, source_target_pairs={{0,12},{2,14},{4,8},{6,10},{8,4},{10,6},{12,0},{14,2},{16,28},{18,... | collective-permute-start | bytes 393224 | tf_op jit(solution)/shard_map/from_owners/ppermute | solution.py:391
  48.4 10.9 %collective-permute-start.15 = (bf16[128,512]{1,0:T(8,128)(2,1)S(1)}, bf16[128,512]{1,0:T(8,128)(2,1)S(1)}, u32[]{:S(2)}, u32[]{:S(2)}) collective-permute-start(bf16[128,512]{1,0:T(8,128)(2,1)S(1)} %get-tuple-element.54), channel_id=1, source_target_pairs={{0,14},{2,12},{4,10},{6,8},{8,6},{10,4},{12,2},{14,0},{16,30},{18,... | collective-permute-start | bytes 393224 | tf_op jit(solution)/shard_map/from_owners/ppermute | solution.py:391
  59.2 5.7 %copy-start.3 = (f32[4096]{0:T(1024)S(1)}, f32[4096]{0:T(1024)}, u32[]{:S(2)}) copy-start(f32[4096]{0:T(1024)} %param.13) | copy-start | bytes 49156
  63.5 1.4 %collective-permute-start.16 = (f32[256,128]{1,0:T(8,128)S(1)}, f32[256,128]{1,0:T(8,128)S(1)}, u32[]{:S(2)}, u32[]{:S(2)}) collective-permute-start(f32[256,128]{1,0:T(8,128)S(1)} %get-tuple-element.55.refs_0_), channel_id=1, source_target_pairs={{0,1},{1,0},{2,3},{3,2},{4,5},{5,4},{6,7},{7,6},{8,9},{9,8},{10,11... | collective-permute-start | bytes 393224 | tf_op jit(solution)/shard_map/norm/ppermute | solution.py:391

commit v2 on v0

v2 whole, which is shorter than its diff:
```python
import functools

import jax
import jax.numpy as jnp
from jax import lax
from jax.experimental import pallas as pl
from jax.experimental.pallas import tpu as pltpu
from jax.sharding import PartitionSpec as P

HEAD_DIM = 64
STATE = 128
GROUP = 256
EPS = 1e-05
EXTRA = 16
LIMIT = 16 * 1024 * 1024
WIDE = 62 * 1024 * 1024
LOG2E = 1.4426950408889634

F32 = jnp.float32
BF16 = jnp.bfloat16
VMEM = pl.BlockSpec(memory_space=pltpu.VMEM)
SMEM = pl.BlockSpec(memory_space=pltpu.SMEM)


def params(limit=LIMIT):
    return pltpu.CompilerParams(vmem_limit_bytes=limit)


def cost(flops, moved, exps=0):
    return pl.CostEstimate(flops=flops, bytes_accessed=moved, transcendentals=exps)


def position(size):
    return lax.axis_index("seq") % size


def halves(value, count):
    terms = []
    for _ in range(count):
        term = value.astype(BF16)
        terms.append(term)
        value = value - term.astype(F32)
    return jnp.concatenate(terms, axis=1)


def picks(first_head, heads, lanes, width, count):
    row = lax.broadcasted_iota(jnp.int32, (heads, lanes), 0)
    col = lax.broadcasted_iota(jnp.int32, (heads, lanes), 1)
    pick = jnp.where(row == first_head + col // width, 1.0, 0.0).astype(BF16)
    return jnp.concatenate([pick] * count, axis=0)


def project_kernel(tiles, hidden, weight, out, rows_held, weight_held, sems):
    tile = hidden.shape[1] // tiles
    copies = []
    for k in range(tiles):
        row = pl.multiple_of(lax.axis_index("head") * hidden.shape[1] + k * tile, tile)
        pair = (
            pltpu.make_async_copy(
                hidden.at[:, pl.ds(k * tile, tile)], rows_held.at[k], sems.at[0, k]
            ),
            pltpu.make_async_copy(weight.at[pl.ds(row, tile), :], weight_held.at[k], sems.at[1, k]),
        )
        for copy in pair:
            copy.start()
        copies.append(pair)
    total = jnp.zeros(out.shape, F32)
    for k in range(tiles):
        for copy in copies[k]:
            copy.wait()
        total = total + jnp.dot(rows_held[k], weight_held[k], preferred_element_type=F32)
    out[...] = total


def project(hidden, weight):
    rows, depth = hidden.shape
    cols = weight.shape[1]
    tiles = 4
    tile = depth // tiles
    return pl.pallas_call(
        functools.partial(project_kernel, tiles),
        in_specs=[
            pl.BlockSpec(memory_space=pltpu.HBM),
            pl.BlockSpec(memory_space=pltpu.HBM),
        ],
        out_specs=VMEM,
        out_shape=jax.ShapeDtypeStruct((rows, cols), F32),
        scratch_shapes=[
            pltpu.VMEM((tiles, rows, tile), BF16),
            pltpu.VMEM((tiles, tile, cols), BF16),
            pltpu.SemaphoreType.DMA((2, tiles)),
        ],
        compiler_params=params(WIDE),
        cost_estimate=cost(2 * rows * depth * cols, 2 * rows * depth + 2 * depth * cols),
        name="project",
    )(hidden, weight)


def decay_kernel(step_rows, rate, x, weighted, cum, cum_rows, ends, step_out):
    heads, rows = step_rows.shape
    cols = x.shape[1]
    step = step_rows[...].T
    step_out[...] = step
    log_decay = -step * rate[...]
    t = lax.broadcasted_iota(jnp.int32, (rows, rows), 0)
    s = lax.broadcasted_iota(jnp.int32, (rows, rows), 1)
    lower = jnp.where(s <= t, 1.0, 0.0).astype(BF16)
    parts = jnp.dot(lower, halves(log_decay, 3), preferred_element_type=F32)
    total = parts[:, :heads] + (parts[:, heads : 2 * heads] + parts[:, 2 * heads :])
    cum[...] = total
    cum_rows[...] = total.T
    last = total[rows - 1 :, :]
    factor = halves(jnp.exp(last - total) * step, 3)
    final = halves(jnp.broadcast_to(jnp.exp(last), (EXTRA, heads)), 3)
    both = jnp.concatenate([factor, final], axis=0)
    lanes = min(1024, cols)
    for at in range(cols // lanes):
        here = slice(at * lanes, (at + 1) * lanes)
        pick = picks(at * (lanes // HEAD_DIM), heads, lanes, HEAD_DIM, 3)
        wide = jnp.dot(both, pick, preferred_element_type=F32)
        weighted[:, here] = (x[:, here].astype(F32) * wide[:rows]).astype(BF16)
        end = wide[rows:]
        high = end.astype(BF16).astype(F32)
        middle = (end - high).astype(BF16).astype(F32)
        low = end - high - middle
        row = lax.broadcasted_iota(jnp.int32, end.shape, 0)
        ends[:, here] = jnp.where(row == 0, high, jnp.where(row == 1, middle, low)).astype(BF16)


def decays(step_rows, rate, x):
    heads, rows = step_rows.shape
    cols = x.shape[1]
    return pl.pallas_call(
        decay_kernel,
        in_specs=[VMEM] * 3,
        out_specs=[VMEM] * 5,
        out_shape=[
            jax.ShapeDtypeStruct((rows, cols), BF16),
            jax.ShapeDtypeStruct((rows, heads), F32),
            jax.ShapeDtypeStruct((heads, rows), F32),
            jax.ShapeDtypeStruct((EXTRA, cols), BF16),
            jax.ShapeDtypeStruct((rows, heads), F32),
        ],
        compiler_params=params(),
        cost_estimate=cost(2 * rows * cols * 256, 4 * rows * cols, 2 * rows * heads),
        name="decays",
    )(step_rows, rate, x)


def fresh_kernel(n, *refs):
    parts, (weighted, ends, proj), slices = refs[:n], refs[n : n + 3], refs[n + 3 :]
    size = len(slices)
    place = position(size)
    total = parts[0][...]
    for part in parts[1:]:
        total = total + part[...]
    rounded = total.astype(BF16)
    proj[...] = rounded
    width = weighted.shape[1] // size
    b_rows = rounded[:, :STATE]
    for m in range(size):
        cols = pl.ds(pl.multiple_of((place ^ m) * width, width), width)
        state = lax.dot_general(
            b_rows, weighted[:, cols], (((0,), (0,)), ((), ())), preferred_element_type=F32
        )
        slices[m][:STATE, :] = state.astype(BF16)
        slices[m][STATE:, :] = ends[:, cols]


def fresh_states(size, parts, weighted, ends):
    rows, cols = weighted.shape
    width = cols // size
    n = len(parts)
    return pl.pallas_call(
        functools.partial(fresh_kernel, n),
        in_specs=[VMEM] * (n + 2),
        out_specs=[VMEM] * (1 + size),
        out_shape=[jax.ShapeDtypeStruct((rows, 2 * STATE), BF16)]
        + [jax.ShapeDtypeStruct((STATE + EXTRA, width), BF16)] * size,
        compiler_params=params(),
        cost_estimate=cost(2 * rows * cols * STATE, 4 * rows * cols),
        name="fresh",
    )(*parts, weighted, ends)


def gather_factors(order, slices, factors):
    place = position(len(order))
    for m, piece in zip(order, slices):
        tail = piece[STATE:, :].astype(F32)
        factors[place ^ m] = jnp.broadcast_to(tail[0:1] + (tail[1:2] + tail[2:3]), factors.shape[1:])


def total_kernel(order, *refs):
    place = position(len(order))
    slices, (out, decay, factors) = refs[:-3], refs[-3:]
    size = len(slices)
    gather_factors(order, slices, factors)
    product = jnp.ones(factors.shape[1:], F32)
    for j in reversed(range(size)):
        factor = factors[j]
        factors[j] = product
        product = product * factor
    decay[...] = product
    total = jnp.zeros(out.shape, F32)
    for m, piece in zip(order, slices):
        total = total + factors[place ^ m][:1] * piece[:STATE, :].astype(F32)
    out[...] = total.astype(BF16)


def group_total(order, slices):
    size = len(slices)
    width = slices[0].shape[1]
    return pl.pallas_call(
        functools.partial(total_kernel, order),
        in_specs=[VMEM] * size,
        out_specs=[VMEM] * 2,
        out_shape=[
            jax.ShapeDtypeStruct((STATE, width), BF16),
            jax.ShapeDtypeStruct((8, width), F32),
        ],
        scratch_shapes=[pltpu.VMEM((size, 8, width), F32)],
        compiler_params=params(),
        cost_estimate=cost(2 * size * STATE * width, 2 * size * STATE * width),
        name="total",
    )(*slices)


def local_kernel(order, *refs):
    place = position(len(order))
    slices, (states, scales, ordered, factors) = refs[:-4], refs[-4:]
    size = len(slices)
    gather_factors(order, slices, factors)
    for m, piece in zip(order, slices):
        ordered[place ^ m] = piece[:STATE, :]
    running = jnp.zeros(states.shape[1:], F32)
    product = jnp.ones(factors.shape[1:], F32)
    for j in range(size):
        at = jnp.int32(0)
        for i, m in enumerate(order):
            at = jnp.where(place ^ j == m, i, at)
        states[at] = running
        scales[at] = product
        running = running * factors[j][:1] + ordered[j].astype(F32)
        product = product * factors[j]


def local_states(order, slices):
    size = len(slices)
    width = slices[0].shape[1]
    return pl.pallas_call(
        functools.partial(local_kernel, order),
        in_specs=[VMEM] * size,
        out_specs=[VMEM] * 2,
        out_shape=[
            jax.ShapeDtypeStruct((size, STATE, width), F32),
            jax.ShapeDtypeStruct((size, 8, width), F32),
        ],
        scratch_shapes=[
            pltpu.VMEM((size, STATE, width), BF16),
            pltpu.VMEM((size, 8, width), F32),
        ],
        compiler_params=params(),
        cost_estimate=cost(2 * size * STATE * width, 6 * size * STATE * width),
        name="local",
    )(*slices)


def enter_kernel(states, scales, before, token, *outs):
    group = lax.axis_index("seq") // len(outs)
    entering = jnp.where(group > 0, before[...].astype(F32), 0.0)
    for m, out in enumerate(outs):
        out[...] = (entering * scales[m][:1] + states[m]).astype(BF16)


def entering_states(states, scales, before, token):
    size, _, width = states.shape
    return pl.pallas_call(
        enter_kernel,
        in_specs=[VMEM] * 4,
        out_specs=[VMEM] * size,
        out_shape=[jax.ShapeDtypeStruct((STATE, width), BF16)] * size,
        compiler_params=params(),
        cost_estimate=cost(2 * size * STATE * width, 6 * size * STATE * width),
        name="entering",
    )(states, scales, before, token)


def inner_kernel(order, proj, cum, cum_rows, step, x, gate, base, slope, token, scores, mixed):
    rows, heads = cum.shape
    width = base.shape[2]
    here = width // HEAD_DIM
    half = rows // 2
    place = position(len(order))
    all_scores = lax.dot_general(
        proj[:, STATE:], proj[:, :STATE], (((1,), (1,)), ((), ())), preferred_element_type=F32
    )
    t = lax.broadcasted_iota(jnp.int32, (half, half), 0)
    s = lax.broadcasted_iota(jnp.int32, (half, half), 1)
    scores[0] = jnp.where(s <= t, all_scores[:half, :half], 0.0)
    scores[1] = jnp.where(s <= t, all_scores[half:, half:], 0.0)
    lower = all_scores[half:, :half].astype(BF16)
    total = cum[...]
    middle = total[half - 1 : half, :]
    grown = jnp.exp(total)
    later = jnp.concatenate(
        [jnp.exp(middle - total[:half]) * step[:half, :], jnp.exp(total[half:] - middle)], axis=0
    )
    per_head = jnp.concatenate([halves(value, 3) for value in (step[...], grown, later)], axis=0)
    parts = halves(total * LOG2E, 3)
    token[...] = jnp.zeros(token.shape, F32)

    def one(at, carry):
        owner = place ^ entry(order, at)
        cols = pl.ds(pl.multiple_of(owner * width, width), width)
        first = owner * here
        wide = jnp.dot(per_head, picks(first, heads, width, HEAD_DIM, 3), preferred_element_type=F32)
        columns = jnp.dot(
            parts, picks(first, heads, here * half, half, 3), preferred_element_type=F32
        )
        values = x[:, cols].astype(F32)
        scaled = (values * wide[:rows]).astype(BF16)
        early = (values[:half] * wide[2 * rows : 2 * rows + half]).astype(BF16)
        cross = jnp.dot(lower, early, preferred_element_type=F32) * wide[2 * rows + half :]
        for k in range(here):
            line = cum_rows[pl.ds(first + k, 1), :] * LOG2E
            mine = slice(k * HEAD_DIM, (k + 1) * HEAD_DIM)
            for i in range(2):
                span = slice(i * half, (i + 1) * half)
                gap = columns[span, k * half : (k + 1) * half] - line[:, span]
                block = (scores[i] * jnp.exp2(jnp.minimum(gap, 0.0))).astype(BF16)
                mixed[span, mine] = jnp.dot(block, scaled[span, mine], preferred_element_type=F32)
        g = gate[:, cols].astype(F32)
        silu = g / (1.0 + jnp.exp(-g))
        base[at, :half, :] = mixed[:half, :] * silu[:half]
        base[at, half:, :] = (mixed[half:, :] + cross) * silu[half:]
        slope[at] = wide[rows : 2 * rows] * silu
        return carry

    lax.fori_loop(0, base.shape[0], one, 0)


def entry(order, at):
    value = jnp.int32(order[0])
    for i, m in enumerate(order):
        value = jnp.where(at == i, m, value)
    return value


def inside(order, proj, cum, cum_rows, step, x, gate):
    rows, heads = step.shape
    n = len(order)
    width = x.shape[1] // n
    return pl.pallas_call(
        functools.partial(inner_kernel, order),
        in_specs=[VMEM] * 6,
        out_specs=[VMEM] * 3,
        out_shape=[jax.ShapeDtypeStruct((n, rows, width), F32)] * 2
        + [jax.ShapeDtypeStruct((8, STATE), F32)],
        scratch_shapes=[
            pltpu.VMEM((2, rows // 2, rows // 2), F32),
            pltpu.VMEM((rows, width), F32),
        ],
        compiler_params=params(),
        cost_estimate=cost(8 * rows * rows * n * width, 12 * rows * n * width, rows * rows * heads),
        name="inner",
    )(proj, cum, cum_rows, step, x, gate)


def outer_kernel(first, proj, base, slope, *refs):
    states, (gated, squares) = refs[:-2], refs[-2:]
    c_rows = proj[:, STATE:]
    if first:
        total, states = states[0][...], states[1:]
    else:
        total = jnp.zeros(squares.shape, F32)
    for m, state in enumerate(states):
        read = jnp.dot(c_rows, state[...], preferred_element_type=F32)
        value = base[first + m] + slope[first + m] * read
        gated[m] = value
        square = value * value
        for k in range(value.shape[1] // STATE):
            total = total + square[:, k * STATE : (k + 1) * STATE]
    squares[...] = total


def outer_part(first, proj, base, slope, prior, states):
    n = len(states)
    _, rows, width = base.shape
    states = [*prior, *states]
    return pl.pallas_call(
        functools.partial(outer_kernel, first),
        in_specs=[VMEM] * (len(states) + 3),
        out_specs=[VMEM] * 2,
        out_shape=[
            jax.ShapeDtypeStruct((n, rows, width), F32),
            jax.ShapeDtypeStruct((rows, STATE), F32),
        ],
        compiler_params=params(),
        cost_estimate=cost(2 * rows * n * width * STATE, 12 * rows * n * width),
        name="outer",
    )(proj, base, slope, *states)


def norm_kernel(count, order, n, k, gain, *refs):
    place = position(len(order))
    parts, gated, (out, held, sems) = refs[:n], refs[n : n + k], refs[n + k :]
    total = parts[0][...]
    for part in parts[1:]:
        total = total + part[...]
    mean = jnp.sum(total, axis=1, keepdims=True) * (1.0 / count)
    scale = lax.rsqrt(mean + EPS)
    copies = []
    width = held.shape[2]
    pieces = [(ref, i) for ref in gated for i in range(ref.shape[0])]
    for at, (ref, i) in enumerate(pieces):
        cols = pl.ds(pl.multiple_of((place ^ order[at]) * width, width), width)
        held[at] = (ref[i] * scale * gain[:, cols]).astype(BF16)
        copy = pltpu.make_async_copy(held.at[at], out.at[:, cols], sems.at[at])
        copy.start()
        copies.append(copy)
    for copy in copies:
        copy.wait()


def normalise(count, order, parts, gated, gain):
    size = len(order)
    _, rows, width = gated[0].shape
    cols = size * width
    n, k = len(parts), len(gated)
    return pl.pallas_call(
        functools.partial(norm_kernel, count, order, n, k),
        in_specs=[VMEM] * (1 + n + k),
        out_specs=pl.BlockSpec(memory_space=pltpu.HBM),
        out_shape=jax.ShapeDtypeStruct((rows, cols), BF16),
        scratch_shapes=[pltpu.VMEM((size, rows, width), BF16), pltpu.SemaphoreType.DMA((size,))],
        compiler_params=params(),
        cost_estimate=cost(4 * rows * cols, 6 * rows * cols),
        name="norm",
    )(gain, *parts, *gated)


def swap(value, axis, mask):
    pairs = [(i, i ^ mask) for i in range(lax.axis_size(axis))]
    return lax.ppermute(value, axis, pairs)


def terms_of_sum(value, axis):
    mask = 1
    terms = [value]
    while mask < lax.axis_size(axis):
        if len(terms) > 1:
            terms = [sum(terms[1:], terms[0])]
        terms.append(swap(terms[0], axis, mask))
        mask *= 2
    return terms


def shards(hidden, weight, head_input, gate_input, step, rate, gain):
    heads = step.shape[1]
    devices = lax.axis_size("seq")
    size = 8
    while devices % size or heads % size or (heads // size * HEAD_DIM) % STATE:
        size //= 2
    groups = devices // size

    masks = [m for m in (1, 2, 4, 7, 3, 5, 6) if m < size]
    order = [0] + masks

    with jax.named_scope("projection"):
        parts = terms_of_sum(project(hidden, weight), "head")
    with jax.named_scope("decays"):
        weighted, cum, cum_rows, ends, step = decays(step.T, rate.reshape(1, heads), head_input)
    with jax.named_scope("states"):
        proj, *mine = fresh_states(size, parts, weighted, ends)
    with jax.named_scope("to_owners"):
        slices = [mine[0]] + [swap(mine[m], "seq", m) for m in masks]
    with jax.named_scope("groups"):
        total, decay = group_total(order, slices)
        up = [(i, (i + size) % devices) for i in range(devices)]
        before = jnp.zeros_like(total)
        for k in range(groups - 1):
            if k > 0:
                prior = jnp.where(lax.axis_index("seq") // size > 0, before.astype(F32), 0.0)
                sent = (prior * decay[:1] + total.astype(F32)).astype(BF16)
            else:
                sent = total
            before = lax.ppermute(sent, "seq", up)
        states, scales = local_states(order, slices)
    with jax.named_scope("inner"):
        base, slope, token = inside(order, proj, cum, cum_rows, step, head_input, gate_input)
    with jax.named_scope("from_owners"):
        outs = entering_states(states, scales, before, token)
        back = [outs[0]] + [swap(out, "seq", m) for m, out in zip(masks, outs[1:])]
    with jax.named_scope("outer"):
        cut = size // 2 + 1
        some, squares = outer_part(0, proj, base, slope, [], back[:cut])
        rest, squares = outer_part(cut, proj, base, slope, [squares], back[cut:])
    with jax.named_scope("norm"):
        count = head_input.shape[1] * lax.axis_size("head")
        sums = terms_of_sum(squares, "head")
        return normalise(count, order, sums, [some, rest], gain.reshape(1, -1))


def solution(mesh):
    in_specs = (
        P("seq", "head"),
        P(),
        P("seq", "head"),
        P("seq", "head"),
        P("seq", "head"),
        P("head"),
        P("head"),
    )
    return jax.shard_map(
        shards, mesh=mesh, in_specs=in_specs, out_specs=P("seq", "head"), check_vma=False
    )
```

time: 444 us -> 59.8 us (0.13)
  waiting for transfers between devices: 316 us -> 14.3 us
  other arithmetic: 46.1 us -> 0 us
  blocking collectives: 43.6 us -> 0 us
  starting transfers between devices: 0.04 us -> 26.5 us
  Pallas kernels: 0 us -> 16.3 us
  between operations: 13.5 us -> 0.12 us
  matrix products: 11.2 us -> 0 us
  local copies, waits for them, and re-layouts: 12.5 us -> 1.62 us
    all_gather x2 -> x0, waiting for transfers between devices: 315 us -> none  [the longest x1 311 us: carried_in(): pieces = jax.tree.map(lambda part: lax.all_gather(part, axis), value)]
    all_gather x1 -> x0, blocking collectives: 41.1 us -> none  [carried_in(): pieces = jax.tree.map(lambda part: lax.all_gather(part, axis), value)]
    select_n x15 -> x0, other arithmetic: 31.2 us -> none  [step(): jnp.where(position < mine, new, old)]
    ppermute x0 -> x17, starting transfers between devices: none -> 26.5 us  [the longest x16 23.8 us: swap(): return lax.ppermute(value, axis, pairs)]
    pallas_call x0 -> x10, Pallas kernels: none -> 16.3 us  [the longest x1 7.67 us: inside(): pl.pallas_call(functools.partial(inner_kernel, order), in_specs=[VMEM] *...]
    ppermute x0 -> x17, waiting for transfers between devices: none -> 14.3 us  [the longest x16 14.2 us: swap(): return lax.ppermute(value, axis, pairs)]
    dot_general x5 -> x0, matrix products: 11.2 us -> none  [the longest x1 5.86 us: shards(): jnp.einsum('chts,cshp->cthp', mixing, scaled, preferred_element_type=jnp....]
    convert_element_type x2 -> x0, other arithmetic: 9.37 us -> none  [the longest x1 5.98 us: shards(): (gated * lax.rsqrt(mean_square + 1e-05)[:, None] * norm_gain[None, :]).as...]
  transfers between devices with their start and end apart: 2 -> 17, of which waited for: 2 -> 7; matrix products, arithmetic and copies ran while one was open for 2% -> 0% of each run, Pallas kernels for 0% -> 17%
where the time goes in v2:
time: 59.8 us; the launch traced here: 58.8 us
  starting transfers between devices  26.5 us (44%)
  Pallas kernels  16.3 us (27%)
  waiting for transfers between devices  14.3 us (24%)
  local copies, waits for them, and re-layouts  1.62 us (3%)
    ppermute x16, starting transfers between devices, swap(): return lax.ppermute(value, axis, pairs)  23.8 us
    ppermute x16, waiting for transfers between devices, swap(): return lax.ppermute(value, axis, pairs)  14.2 us
    pallas_call x1, Pallas kernels, inside(): pl.pallas_call(functools.partial(inner_kernel, order), in_specs=[VMEM] *...  7.67 us
    pallas_call x1, Pallas kernels, project(): pl.pallas_call(functools.partial(project_kernel, tiles), in_specs=[pl.Blo...  2.87 us
    ppermute x1, starting transfers between devices, shards(): before = lax.ppermute(sent, 'seq', up)  2.66 us
    unnamed x14, local copies, waits for them, and re-layouts  1.62 us
    pallas_call x1, Pallas kernels, normalise(): pl.pallas_call(functools.partial(norm_kernel, count, order, n, k), in_spe...  1.54 us
    pallas_call x1, Pallas kernels, decays(): pl.pallas_call(decay_kernel, in_specs=[VMEM] * 3, out_specs=[VMEM] * 5, o...  1.39 us
  transfers between devices with their start and end apart: 17, of which 7 were waited for; matrix products, arithmetic and copies ran while one was open for 0% of the time, Pallas kernels for 17%

profile of v2, /device:TPU:0, one launch (start us, length us, event | category | flops | bytes accessed | tf_op | source)
XLA Modules:
  0.0 58.8 jit_solution(9302249259679957941)
XLA Ops:
  0.0 0.0 copy-start.5
  0.0 0.0 copy-start.3
  0.0 2.9 %project.1.refs_0_ = f32[256,256]{1,0:T(8,128)} custom-call(bf16[256,2048]{1,0:T(8,128)(2,1)} %hidden.1, bf16[4096,256]{1,0:T(8,128)(2,1)} %weight.1), custom_call_target="tpu_custom_call" | custom-call | flops 268435456 | bytes 2097152 | tf_op jit(solution)/shard_map/projection/project/pallas_call | solution.py:80
  2.9 0.5 collective-permute-start
  3.4 0.0 copy-done.5
  3.4 0.0 copy-done.3
  3.4 0.0 copy-start
  3.4 1.6 %copy-done = bf16[256,4096]{1,0:T(8,128)(2,1)S(1)} copy-done((bf16[256,4096]{1,0:T(8,128)(2,1)S(1)}, bf16[256,4096]{1,0:T(8,128)(2,1)}, u32[]{:S(2)}) %copy-start) | copy-done | bytes 2097176
  5.0 0.0 copy-start.2
  5.0 0.0 copy-start.6
  5.0 1.4 %decays.1 = (bf16[256,4096]{1,0:T(8,128)(2,1)S(1)}, f32[256,64]{1,0:T(8,128)S(1)}, f32[64,256]{1,0:T(8,128)S(1)}, bf16[16,4096]{1,0:T(8,128)(2,1)S(1)}, f32[256,64]{1,0:T(8,128)S(1)}) custom-call(f32[64,256]{1,0:T(8,128)S(1)} %bitcast.3, f32[1,64]{1,0:T(1,128)S(1)} %bitcast.5, bf16[256,4096]{1,0:T(8,128)(2,1)S(1)} %copy-done), custom_call_target="tpu_custom_call" | custom-call | flops 536870912 | bytes 4194304 | tf_op jit(solution)/shard_map/decays/decays/pallas_call | solution.py:133
  6.4 0.0 copy-start.1
  6.4 0.0 collective-permute-done.refs_1_
  6.4 0.0 copy-done.2
  6.4 0.5 fresh.1
  6.9 2.6 %collective-permute-start.1 = (bf16[144,512]{1,0:T(8,128)(2,1)S(1)}, bf16[144,512]{1,0:T(8,128)(2,1)S(1)}, u32[]{:S(2)}, u32[]{:S(2)}) collective-permute-start(bf16[144,512]{1,0:T(8,128)(2,1)S(1)} %get-tuple-element.46), channel_id=1, source_target_pairs={{0,2},{2,0},{4,6},{6,4},{8,10},{10,8},{12,14},{14,12},{16,18},{18,... | collective-permute-start | bytes 442376 | tf_op jit(solution)/shard_map/to_owners/ppermute | solution.py:444
  9.5 1.5 %collective-permute-start.2 = (bf16[144,512]{1,0:T(8,128)(2,1)S(1)}, bf16[144,512]{1,0:T(8,128)(2,1)S(1)}, u32[]{:S(2)}, u32[]{:S(2)}) collective-permute-start(bf16[144,512]{1,0:T(8,128)(2,1)S(1)} %get-tuple-element.47), channel_id=1, source_target_pairs={{0,4},{2,6},{4,0},{6,2},{8,12},{10,14},{12,8},{14,10},{16,20},{18,... | collective-permute-start | bytes 442376 | tf_op jit(solution)/shard_map/to_owners/ppermute | solution.py:444
  11.0 1.6 %collective-permute-start.3 = (bf16[144,512]{1,0:T(8,128)(2,1)S(1)}, bf16[144,512]{1,0:T(8,128)(2,1)S(1)}, u32[]{:S(2)}, u32[]{:S(2)}) collective-permute-start(bf16[144,512]{1,0:T(8,128)(2,1)S(1)} %get-tuple-element.48), channel_id=1, source_target_pairs={{0,8},{2,10},{4,12},{6,14},{8,0},{10,2},{12,4},{14,6},{16,24},{18,... | collective-permute-start | bytes 442376 | tf_op jit(solution)/shard_map/to_owners/ppermute | solution.py:444
  12.6 0.0 collective-permute-start.4
  12.6 2.8 %collective-permute-start.5 = (bf16[144,512]{1,0:T(8,128)(2,1)S(1)}, bf16[144,512]{1,0:T(8,128)(2,1)S(1)}, u32[]{:S(2)}, u32[]{:S(2)}) collective-permute-start(bf16[144,512]{1,0:T(8,128)(2,1)S(1)} %get-tuple-element.50), channel_id=1, source_target_pairs={{0,6},{2,4},{4,2},{6,0},{8,14},{10,12},{12,10},{14,8},{16,22},{18,... | collective-permute-start | bytes 442376 | tf_op jit(solution)/shard_map/to_owners/ppermute | solution.py:444
  15.4 0.0 collective-permute-done.1.refs_1_
  15.4 1.5 %collective-permute-start.6 = (bf16[144,512]{1,0:T(8,128)(2,1)S(1)}, bf16[144,512]{1,0:T(8,128)(2,1)S(1)}, u32[]{:S(2)}, u32[]{:S(2)}) collective-permute-start(bf16[144,512]{1,0:T(8,128)(2,1)S(1)} %get-tuple-element.51), channel_id=1, source_target_pairs={{0,10},{2,8},{4,14},{6,12},{8,2},{10,0},{12,6},{14,4},{16,26},{18,... | collective-permute-start | bytes 442376 | tf_op jit(solution)/shard_map/to_owners/ppermute | solution.py:444
  17.0 0.0 collective-permute-done.2.refs_2_
  17.0 1.2 %collective-permute-start.7 = (bf16[144,512]{1,0:T(8,128)(2,1)S(1)}, bf16[144,512]{1,0:T(8,128)(2,1)S(1)}, u32[]{:S(2)}, u32[]{:S(2)}) collective-permute-start(bf16[144,512]{1,0:T(8,128)(2,1)S(1)} %get-tuple-element.52), channel_id=1, source_target_pairs={{0,12},{2,14},{4,8},{6,10},{8,4},{10,6},{12,0},{14,2},{16,28},{18,... | collective-permute-start | bytes 442376 | tf_op jit(solution)/shard_map/to_owners/ppermute | solution.py:444
  18.2 0.0 collective-permute-done.3.refs_3_
  18.2 3.0 %collective-permute-done.4.refs_4_ = bf16[144,512]{1,0:T(8,128)(2,1)S(1)} collective-permute-done((bf16[144,512]{1,0:T(8,128)(2,1)S(1)}, bf16[144,512]{1,0:T(8,128)(2,1)S(1)}, u32[]{:S(2)}, u32[]{:S(2)}) %collective-permute-start.4) | collective-permute-done | bytes 147488 | tf_op jit(solution)/shard_map/to_owners/ppermute | solution.py:444
  21.2 5.0 %collective-permute-done.5.refs_5_ = bf16[144,512]{1,0:T(8,128)(2,1)S(1)} collective-permute-done((bf16[144,512]{1,0:T(8,128)(2,1)S(1)}, bf16[144,512]{1,0:T(8,128)(2,1)S(1)}, u32[]{:S(2)}, u32[]{:S(2)}) %collective-permute-start.5) | collective-permute-done | bytes 147488 | tf_op jit(solution)/shard_map/to_owners/ppermute | solution.py:444
  26.3 0.0 collective-permute-done.6.refs_6_
  26.3 1.0 %collective-permute-done.7.refs_7_ = bf16[144,512]{1,0:T(8,128)(2,1)S(1)} collective-permute-done((bf16[144,512]{1,0:T(8,128)(2,1)S(1)}, bf16[144,512]{1,0:T(8,128)(2,1)S(1)}, u32[]{:S(2)}, u32[]{:S(2)}) %collective-permute-start.7) | collective-permute-done | bytes 147488 | tf_op jit(solution)/shard_map/to_owners/ppermute | solution.py:444
  27.3 0.8 %total.1 = (bf16[128,512]{1,0:T(8,128)(2,1)S(1)}, f32[8,512]{1,0:T(8,128)}) custom-call(bf16[144,512]{1,0:T(8,128)(2,1)S(1)} %get-tuple-element.45.refs_0_, bf16[144,512]{1,0:T(8,128)(2,1)S(1)} %collective-permute-done.1.refs_1_, bf16[144,512]{1,0:T(8,128)(2,1)S(1)} %collective-permute-done.2.refs_2_, bf16[144,512]{1,0:T(8,128)(2,1)S(1)} %collective-permute-done.3.refs_3_, ...), custom_call_target="tpu_custom_call" | custom-call | flops 1048576 | bytes 1048576 | tf_op jit(solution)/shard_map/groups/total/pallas_call | solution.py:213
  28.1 2.7 %collective-permute-start.8 = (bf16[128,512]{1,0:T(8,128)(2,1)S(1)}, bf16[128,512]{1,0:T(8,128)(2,1)S(1)}, u32[]{:S(2)}, u32[]{:S(2)}) collective-permute-start(bf16[128,512]{1,0:T(8,128)(2,1)S(1)} %get-tuple-element.55), channel_id=1, source_target_pairs={{0,16},{2,18},{4,20},{6,22},{8,24},{10,26},{12,28},{14,30},{16,0},... | collective-permute-start | bytes 393224 | tf_op jit(solution)/shard_map/groups/ppermute | solution.py:487
  30.8 0.0 copy-done.6
  30.8 0.0 copy-done.1
  30.8 7.7 %inner.1 = (f32[8,256,512]{2,1,0:T(8,128)S(1)}, f32[8,256,512]{2,1,0:T(8,128)S(1)}, f32[8,128]{1,0:T(8,128)S(1)}) custom-call(bf16[256,256]{1,0:T(8,128)(2,1)S(1)} %get-tuple-element.39.proj, f32[256,64]{1,0:T(8,128)S(1)} %get-tuple-element.40.cum, f32[64,256]{1,0:T(8,128)S(1)} %get-tuple-element.41.cum_rows, f32[256,64]{1,0:T(8,128)S(1)} %get-tuple-element.42.step, ...), custom_call_target="tpu_custom_call" | custom-call | flops 2147483648 | bytes 12582912 | tf_op jit(solution)/shard_map/inner/inner/pallas_call | solution.py:353
  38.4 0.4 local.1
  38.9 0.0 collective-permute-done.8.before
  38.9 0.2 entering.1
  39.1 1.0 %collective-permute-start.9 = (bf16[128,512]{1,0:T(8,128)(2,1)S(1)}, bf16[128,512]{1,0:T(8,128)(2,1)S(1)}, u32[]{:S(2)}, u32[]{:S(2)}) collective-permute-start(bf16[128,512]{1,0:T(8,128)(2,1)S(1)} %get-tuple-element.58), channel_id=1, source_target_pairs={{0,2},{2,0},{4,6},{6,4},{8,10},{10,8},{12,14},{14,12},{16,18},{18,... | collective-permute-start | bytes 393224 | tf_op jit(solution)/shard_map/from_owners/ppermute | solution.py:444
  40.1 1.5 %collective-permute-start.10 = (bf16[128,512]{1,0:T(8,128)(2,1)S(1)}, bf16[128,512]{1,0:T(8,128)(2,1)S(1)}, u32[]{:S(2)}, u32[]{:S(2)}) collective-permute-start(bf16[128,512]{1,0:T(8,128)(2,1)S(1)} %get-tuple-element.59), channel_id=1, source_target_pairs={{0,4},{2,6},{4,0},{6,2},{8,12},{10,14},{12,8},{14,10},{16,20},{18,... | collective-permute-start | bytes 393224 | tf_op jit(solution)/shard_map/from_owners/ppermute | solution.py:444
  41.7 1.5 %collective-permute-start.11 = (bf16[128,512]{1,0:T(8,128)(2,1)S(1)}, bf16[128,512]{1,0:T(8,128)(2,1)S(1)}, u32[]{:S(2)}, u32[]{:S(2)}) collective-permute-start(bf16[128,512]{1,0:T(8,128)(2,1)S(1)} %get-tuple-element.60), channel_id=1, source_target_pairs={{0,8},{2,10},{4,12},{6,14},{8,0},{10,2},{12,4},{14,6},{16,24},{18,... | collective-permute-start | bytes 393224 | tf_op jit(solution)/shard_map/from_owners/ppermute | solution.py:444
  43.2 0.9 %collective-permute-start.12 = (bf16[128,512]{1,0:T(8,128)(2,1)S(1)}, bf16[128,512]{1,0:T(8,128)(2,1)S(1)}, u32[]{:S(2)}, u32[]{:S(2)}) collective-permute-start(bf16[128,512]{1,0:T(8,128)(2,1)S(1)} %get-tuple-element.61), channel_id=1, source_target_pairs={{0,14},{2,12},{4,10},{6,8},{8,6},{10,4},{12,2},{14,0},{16,30},{18,... | collective-permute-start | bytes 393224 | tf_op jit(solution)/shard_map/from_owners/ppermute | solution.py:444
  44.1 1.9 %collective-permute-start.13 = (bf16[128,512]{1,0:T(8,128)(2,1)S(1)}, bf16[128,512]{1,0:T(8,128)(2,1)S(1)}, u32[]{:S(2)}, u32[]{:S(2)}) collective-permute-start(bf16[128,512]{1,0:T(8,128)(2,1)S(1)} %get-tuple-element.63), channel_id=1, source_target_pairs={{0,6},{2,4},{4,2},{6,0},{8,14},{10,12},{12,10},{14,8},{16,22},{18,... | collective-permute-start | bytes 393224 | tf_op jit(solution)/shard_map/from_owners/ppermute | solution.py:444
  46.1 0.0 collective-permute-done.9.refs_1_
  46.1 2.0 %collective-permute-start.14 = (bf16[128,512]{1,0:T(8,128)(2,1)S(1)}, bf16[128,512]{1,0:T(8,128)(2,1)S(1)}, u32[]{:S(2)}, u32[]{:S(2)}) collective-permute-start(bf16[128,512]{1,0:T(8,128)(2,1)S(1)} %get-tuple-element.64), channel_id=1, source_target_pairs={{0,10},{2,8},{4,14},{6,12},{8,2},{10,0},{12,6},{14,4},{16,26},{18,... | collective-permute-start | bytes 393224 | tf_op jit(solution)/shard_map/from_owners/ppermute | solution.py:444
  48.0 0.0 collective-permute-done.10.refs_2_
  48.1 3.1 %collective-permute-start.15 = (bf16[128,512]{1,0:T(8,128)(2,1)S(1)}, bf16[128,512]{1,0:T(8,128)(2,1)S(1)}, u32[]{:S(2)}, u32[]{:S(2)}) collective-permute-start(bf16[128,512]{1,0:T(8,128)(2,1)S(1)} %get-tuple-element.65), channel_id=1, source_target_pairs={{0,12},{2,14},{4,8},{6,10},{8,4},{10,6},{12,0},{14,2},{16,28},{18,... | collective-permute-start | bytes 393224 | tf_op jit(solution)/shard_map/from_owners/ppermute | solution.py:444
  51.1 0.0 collective-permute-done.11.refs_3_
  51.1 1.2 %collective-permute-done.12.refs_4_ = bf16[128,512]{1,0:T(8,128)(2,1)S(1)} collective-permute-done((bf16[128,512]{1,0:T(8,128)(2,1)S(1)}, bf16[128,512]{1,0:T(8,128)(2,1)S(1)}, u32[]{:S(2)}, u32[]{:S(2)}) %collective-permute-start.12) | collective-permute-done | bytes 131104 | tf_op jit(solution)/shard_map/from_owners/ppermute | solution.py:444
  52.3 0.5 outer.2
  52.8 0.7 %collective-permute-done.13.refs_1_ = bf16[128,512]{1,0:T(8,128)(2,1)S(1)} collective-permute-done((bf16[128,512]{1,0:T(8,128)(2,1)S(1)}, bf16[128,512]{1,0:T(8,128)(2,1)S(1)}, u32[]{:S(2)}, u32[]{:S(2)}) %collective-permute-start.13) | collective-permute-done | bytes 131104 | tf_op jit(solution)/shard_map/from_owners/ppermute | solution.py:444
  53.5 0.0 collective-permute-done.14.refs_2_
  53.5 1.9 %collective-permute-done.15.refs_3_ = bf16[128,512]{1,0:T(8,128)(2,1)S(1)} collective-permute-done((bf16[128,512]{1,0:T(8,128)(2,1)S(1)}, bf16[128,512]{1,0:T(8,128)(2,1)S(1)}, u32[]{:S(2)}, u32[]{:S(2)}) %collective-permute-start.15) | collective-permute-done | bytes 131104 | tf_op jit(solution)/shard_map/from_owners/ppermute | solution.py:444
  55.5 0.0 copy-start.4
  55.5 0.4 outer.3
  55.8 0.1 collective-permute-start.16
  55.9 1.3 %collective-permute-done.16.refs_1_ = f32[256,128]{1,0:T(8,128)S(1)} collective-permute-done((f32[256,128]{1,0:T(8,128)S(1)}, f32[256,128]{1,0:T(8,128)S(1)}, u32[]{:S(2)}, u32[]{:S(2)}) %collective-permute-start.16) | collective-permute-done | bytes 131104 | tf_op jit(solution)/shard_map/norm/ppermute | solution.py:444
  57.3 0.0 copy-done.4
  57.3 1.5 %norm.1 = bf16[256,4096]{1,0:T(8,128)(2,1)} custom-call(f32[1,4096]{1,0:T(1,128)S(1)} %bitcast.4, f32[256,128]{1,0:T(8,128)S(1)} %get-tuple-element.66.refs_0_, f32[256,128]{1,0:T(8,128)S(1)} %collective-permute-done.16.refs_1_, f32[5,256,512]{2,1,0:T(8,128)S(1)} %get-tuple-element.67.refs_2_, f32[3,256,512]{2,1,0:T(8,128)S(1)} %get-tuple-element.68.refs_3_), custom_call_target="tpu_custom_call" | custom-call | flops 4194304 | bytes 6291456 | tf_op jit(solution)/shard_map/norm/norm/pallas_call | solution.py:430
Async XLA Ops:
  0.0 3.4 %copy-start.5 = (f32[64]{0:T(128)S(1)}, f32[64]{0:T(128)}, u32[]{:S(2)}) copy-start(f32[64]{0:T(128)} %param.12) | copy-start | bytes 772
  0.0 3.4 %copy-start.3 = (f32[256,64]{0,1:T(8,128)S(1)}, f32[256,64]{0,1:T(8,128)}, u32[]{:S(2)}) copy-start(f32[256,64]{0,1:T(8,128)} %param.11) | copy-start | bytes 196612
  2.9 3.5 %collective-permute-start = (f32[256,256]{1,0:T(8,128)}, f32[256,256]{1,0:T(8,128)S(1)}, u32[]{:S(2)}, u32[]{:S(2)}) collective-permute-start(f32[256,256]{1,0:T(8,128)} %project.1.refs_0_), channel_id=1, source_target_pairs={{0,1},{1,0},{2,3},{3,2},{4,5},{5,4},{6,7},{7,6},{8,9},{9,8},{10,11... | collective-permute-start | bytes 786440 | tf_op jit(solution)/shard_map/projection/ppermute | solution.py:444
  3.4 1.6 %copy-start = (bf16[256,4096]{1,0:T(8,128)(2,1)S(1)}, bf16[256,4096]{1,0:T(8,128)(2,1)}, u32[]{:S(2)}) copy-start(bf16[256,4096]{1,0:T(8,128)(2,1)} %x.3) | copy-start | bytes 6291460
  5.0 1.4 %copy-start.2 = (f32[256,256]{1,0:T(8,128)S(1)}, f32[256,256]{1,0:T(8,128)}, u32[]{:S(2)}) copy-start(f32[256,256]{1,0:T(8,128)} %project.1.refs_0_) | copy-start | bytes 786436
  5.0 25.7 %copy-start.6 = (bf16[256,4096]{1,0:T(8,128)(2,1)S(1)}, bf16[256,4096]{1,0:T(8,128)(2,1)}, u32[]{:S(2)}) copy-start(bf16[256,4096]{1,0:T(8,128)(2,1)} %gate.1) | copy-start | bytes 6291460
  6.4 24.4 %copy-start.1 = (bf16[256,4096]{1,0:T(8,128)(2,1)S(1)}, bf16[256,4096]{1,0:T(8,128)(2,1)}, u32[]{:S(2)}) copy-start(bf16[256,4096]{1,0:T(8,128)(2,1)} %x.3) | copy-start | bytes 6291460
  6.9 8.5 %collective-permute-start.1 = (bf16[144,512]{1,0:T(8,128)(2,1)S(1)}, bf16[144,512]{1,0:T(8,128)(2,1)S(1)}, u32[]{:S(2)}, u32[]{:S(2)}) collective-permute-start(bf16[144,512]{1,0:T(8,128)(2,1)S(1)} %get-tuple-element.46), channel_id=1, source_target_pairs={{0,2},{2,0},{4,6},{6,4},{8,10},{10,8},{12,14},{14,12},{16,18},{18,... | collective-permute-start | bytes 442376 | tf_op jit(solution)/shard_map/to_owners/ppermute | solution.py:444
  9.5 7.5 %collective-permute-start.2 = (bf16[144,512]{1,0:T(8,128)(2,1)S(1)}, bf16[144,512]{1,0:T(8,128)(2,1)S(1)}, u32[]{:S(2)}, u32[]{:S(2)}) collective-permute-start(bf16[144,512]{1,0:T(8,128)(2,1)S(1)} %get-tuple-element.47), channel_id=1, source_target_pairs={{0,4},{2,6},{4,0},{6,2},{8,12},{10,14},{12,8},{14,10},{16,20},{18,... | collective-permute-start | bytes 442376 | tf_op jit(solution)/shard_map/to_owners/ppermute | solution.py:444
  11.0 7.1 %collective-permute-start.3 = (bf16[144,512]{1,0:T(8,128)(2,1)S(1)}, bf16[144,512]{1,0:T(8,128)(2,1)S(1)}, u32[]{:S(2)}, u32[]{:S(2)}) collective-permute-start(bf16[144,512]{1,0:T(8,128)(2,1)S(1)} %get-tuple-element.48), channel_id=1, source_target_pairs={{0,8},{2,10},{4,12},{6,14},{8,0},{10,2},{12,4},{14,6},{16,24},{18,... | collective-permute-start | bytes 442376 | tf_op jit(solution)/shard_map/to_owners/ppermute | solution.py:444
  12.6 8.6 %collective-permute-start.4 = (bf16[144,512]{1,0:T(8,128)(2,1)S(1)}, bf16[144,512]{1,0:T(8,128)(2,1)S(1)}, u32[]{:S(2)}, u32[]{:S(2)}) collective-permute-start(bf16[144,512]{1,0:T(8,128)(2,1)S(1)} %get-tuple-element.49), channel_id=1, source_target_pairs={{0,14},{2,12},{4,10},{6,8},{8,6},{10,4},{12,2},{14,0},{16,30},{18,... | collective-permute-start | bytes 442376 | tf_op jit(solution)/shard_map/to_owners/ppermute | solution.py:444
  12.6 13.7 %collective-permute-start.5 = (bf16[144,512]{1,0:T(8,128)(2,1)S(1)}, bf16[144,512]{1,0:T(8,128)(2,1)S(1)}, u32[]{:S(2)}, u32[]{:S(2)}) collective-permute-start(bf16[144,512]{1,0:T(8,128)(2,1)S(1)} %get-tuple-element.50), channel_id=1, source_target_pairs={{0,6},{2,4},{4,2},{6,0},{8,14},{10,12},{12,10},{14,8},{16,22},{18,... | collective-permute-start | bytes 442376 | tf_op jit(solution)/shard_map/to_owners/ppermute | solution.py:444
  15.4 10.8 %collective-permute-start.6 = (bf16[144,512]{1,0:T(8,128)(2,1)S(1)}, bf16[144,512]{1,0:T(8,128)(2,1)S(1)}, u32[]{:S(2)}, u32[]{:S(2)}) collective-permute-start(bf16[144,512]{1,0:T(8,128)(2,1)S(1)} %get-tuple-element.51), channel_id=1, source_target_pairs={{0,10},{2,8},{4,14},{6,12},{8,2},{10,0},{12,6},{14,4},{16,26},{18,... | collective-permute-start | bytes 442376 | tf_op jit(solution)/shard_map/to_owners/ppermute | solution.py:444
  17.0 10.3 %collective-permute-start.7 = (bf16[144,512]{1,0:T(8,128)(2,1)S(1)}, bf16[144,512]{1,0:T(8,128)(2,1)S(1)}, u32[]{:S(2)}, u32[]{:S(2)}) collective-permute-start(bf16[144,512]{1,0:T(8,128)(2,1)S(1)} %get-tuple-element.52), channel_id=1, source_target_pairs={{0,12},{2,14},{4,8},{6,10},{8,4},{10,6},{12,0},{14,2},{16,28},{18,... | collective-permute-start | bytes 442376 | tf_op jit(solution)/shard_map/to_owners/ppermute | solution.py:444
  28.1 10.8 %collective-permute-start.8 = (bf16[128,512]{1,0:T(8,128)(2,1)S(1)}, bf16[128,512]{1,0:T(8,128)(2,1)S(1)}, u32[]{:S(2)}, u32[]{:S(2)}) collective-permute-start(bf16[128,512]{1,0:T(8,128)(2,1)S(1)} %get-tuple-element.55), channel_id=1, source_target_pairs={{0,16},{2,18},{4,20},{6,22},{8,24},{10,26},{12,28},{14,30},{16,0},... | collective-permute-start | bytes 393224 | tf_op jit(solution)/shard_map/groups/ppermute | solution.py:487
  39.1 7.0 %collective-permute-start.9 = (bf16[128,512]{1,0:T(8,128)(2,1)S(1)}, bf16[128,512]{1,0:T(8,128)(2,1)S(1)}, u32[]{:S(2)}, u32[]{:S(2)}) collective-permute-start(bf16[128,512]{1,0:T(8,128)(2,1)S(1)} %get-tuple-element.58), channel_id=1, source_target_pairs={{0,2},{2,0},{4,6},{6,4},{8,10},{10,8},{12,14},{14,12},{16,18},{18,... | collective-permute-start | bytes 393224 | tf_op jit(solution)/shard_map/from_owners/ppermute | solution.py:444
  40.1 7.9 %collective-permute-start.10 = (bf16[128,512]{1,0:T(8,128)(2,1)S(1)}, bf16[128,512]{1,0:T(8,128)(2,1)S(1)}, u32[]{:S(2)}, u32[]{:S(2)}) collective-permute-start(bf16[128,512]{1,0:T(8,128)(2,1)S(1)} %get-tuple-element.59), channel_id=1, source_target_pairs={{0,4},{2,6},{4,0},{6,2},{8,12},{10,14},{12,8},{14,10},{16,20},{18,... | collective-permute-start | bytes 393224 | tf_op jit(solution)/shard_map/from_owners/ppermute | solution.py:444
  41.7 9.5 %collective-permute-start.11 = (bf16[128,512]{1,0:T(8,128)(2,1)S(1)}, bf16[128,512]{1,0:T(8,128)(2,1)S(1)}, u32[]{:S(2)}, u32[]{:S(2)}) collective-permute-start(bf16[128,512]{1,0:T(8,128)(2,1)S(1)} %get-tuple-element.60), channel_id=1, source_target_pairs={{0,8},{2,10},{4,12},{6,14},{8,0},{10,2},{12,4},{14,6},{16,24},{18,... | collective-permute-start | bytes 393224 | tf_op jit(solution)/shard_map/from_owners/ppermute | solution.py:444
  43.2 9.1 %collective-permute-start.12 = (bf16[128,512]{1,0:T(8,128)(2,1)S(1)}, bf16[128,512]{1,0:T(8,128)(2,1)S(1)}, u32[]{:S(2)}, u32[]{:S(2)}) collective-permute-start(bf16[128,512]{1,0:T(8,128)(2,1)S(1)} %get-tuple-element.61), channel_id=1, source_target_pairs={{0,14},{2,12},{4,10},{6,8},{8,6},{10,4},{12,2},{14,0},{16,30},{18,... | collective-permute-start | bytes 393224 | tf_op jit(solution)/shard_map/from_owners/ppermute | solution.py:444
  44.1 9.4 %collective-permute-start.13 = (bf16[128,512]{1,0:T(8,128)(2,1)S(1)}, bf16[128,512]{1,0:T(8,128)(2,1)S(1)}, u32[]{:S(2)}, u32[]{:S(2)}) collective-permute-start(bf16[128,512]{1,0:T(8,128)(2,1)S(1)} %get-tuple-element.63), channel_id=1, source_target_pairs={{0,6},{2,4},{4,2},{6,0},{8,14},{10,12},{12,10},{14,8},{16,22},{18,... | collective-permute-start | bytes 393224 | tf_op jit(solution)/shard_map/from_owners/ppermute | solution.py:444
  46.1 7.5 %collective-permute-start.14 = (bf16[128,512]{1,0:T(8,128)(2,1)S(1)}, bf16[128,512]{1,0:T(8,128)(2,1)S(1)}, u32[]{:S(2)}, u32[]{:S(2)}) collective-permute-start(bf16[128,512]{1,0:T(8,128)(2,1)S(1)} %get-tuple-element.64), channel_id=1, source_target_pairs={{0,10},{2,8},{4,14},{6,12},{8,2},{10,0},{12,6},{14,4},{16,26},{18,... | collective-permute-start | bytes 393224 | tf_op jit(solution)/shard_map/from_owners/ppermute | solution.py:444
  48.1 7.4 %collective-permute-start.15 = (bf16[128,512]{1,0:T(8,128)(2,1)S(1)}, bf16[128,512]{1,0:T(8,128)(2,1)S(1)}, u32[]{:S(2)}, u32[]{:S(2)}) collective-permute-start(bf16[128,512]{1,0:T(8,128)(2,1)S(1)} %get-tuple-element.65), channel_id=1, source_target_pairs={{0,12},{2,14},{4,8},{6,10},{8,4},{10,6},{12,0},{14,2},{16,28},{18,... | collective-permute-start | bytes 393224 | tf_op jit(solution)/shard_map/from_owners/ppermute | solution.py:444
  55.5 1.8 %copy-start.4 = (f32[4096]{0:T(1024)S(1)}, f32[4096]{0:T(1024)}, u32[]{:S(2)}) copy-start(f32[4096]{0:T(1024)} %param.13) | copy-start | bytes 49156
  55.8 1.4 %collective-permute-start.16 = (f32[256,128]{1,0:T(8,128)S(1)}, f32[256,128]{1,0:T(8,128)S(1)}, u32[]{:S(2)}, u32[]{:S(2)}) collective-permute-start(f32[256,128]{1,0:T(8,128)S(1)} %get-tuple-element.66.refs_0_), channel_id=1, source_target_pairs={{0,1},{1,0},{2,3},{3,2},{4,5},{5,4},{6,7},{7,6},{8,9},{9,8},{10,11... | collective-permute-start | bytes 393224 | tf_op jit(solution)/shard_map/norm/ppermute | solution.py:444

commit v3 on v2

--- a/solution.py
+++ b/solution.py
@@ -11,15 +11,20 @@
 STATE = 128
 GROUP = 256
 EPS = 1e-05
-EXTRA = 16
+EXTRA = 8
 LIMIT = 16 * 1024 * 1024
-WIDE = 62 * 1024 * 1024
+SEND_ORDER = (0, 1, 6, 2, 5, 4, 3, 7)
+BACK_ORDER = (0, 1, 6, 2, 5, 4, 3, 7)
 LOG2E = 1.4426950408889634
 
 F32 = jnp.float32
 BF16 = jnp.bfloat16
 VMEM = pl.BlockSpec(memory_space=pltpu.VMEM)
 SMEM = pl.BlockSpec(memory_space=pltpu.SMEM)
+
+
+def in_hbm(value):
+    return pltpu.with_memory_space_constraint(value, pltpu.HBM)
 
 
 def params(limit=LIMIT):
@@ -90,15 +95,21 @@
             pltpu.VMEM((tiles, tile, cols), BF16),
             pltpu.SemaphoreType.DMA((2, tiles)),
         ],
-        compiler_params=params(WIDE),
+        compiler_params=params(),
         cost_estimate=cost(2 * rows * depth * cols, 2 * rows * depth + 2 * depth * cols),
         name="project",
-    )(hidden, weight)
-
-
-def decay_kernel(step_rows, rate, x, weighted, cum, cum_rows, ends, step_out):
+    )(in_hbm(hidden), in_hbm(weight))
+
+
+def decay_kernel(tiles, step_rows, rate, x, weighted, cum, cum_rows, ends, step_out, held, sems):
     heads, rows = step_rows.shape
     cols = x.shape[1]
+    lanes = cols // tiles
+    copies = []
+    for at in range(tiles):
+        here = pl.ds(at * lanes, lanes)
+        copies.append(pltpu.make_async_copy(x.at[:, here], held.at[at], sems.at[at]))
+        copies[-1].start()
     step = step_rows[...].T
     step_out[...] = step
     log_decay = -step * rate[...]
@@ -113,12 +124,12 @@
     factor = halves(jnp.exp(last - total) * step, 3)
     final = halves(jnp.broadcast_to(jnp.exp(last), (EXTRA, heads)), 3)
     both = jnp.concatenate([factor, final], axis=0)
-    lanes = min(1024, cols)
-    for at in range(cols // lanes):
+    for at in range(tiles):
         here = slice(at * lanes, (at + 1) * lanes)
         pick = picks(at * (lanes // HEAD_DIM), heads, lanes, HEAD_DIM, 3)
         wide = jnp.dot(both, pick, preferred_element_type=F32)
-        weighted[:, here] = (x[:, here].astype(F32) * wide[:rows]).astype(BF16)
+        copies[at].wait()
+        weighted[:, here] = (held[at].astype(F32) * wide[:rows]).astype(BF16)
         end = wide[rows:]
         high = end.astype(BF16).astype(F32)
         middle = (end - high).astype(BF16).astype(F32)
@@ -130,21 +141,24 @@
 def decays(step_rows, rate, x):
     heads, rows = step_rows.shape
     cols = x.shape[1]
-    return pl.pallas_call(
-        decay_kernel,
-        in_specs=[VMEM] * 3,
-        out_specs=[VMEM] * 5,
+    tiles = max(1, cols // 1024)
+    return pl.pallas_call(
+        functools.partial(decay_kernel, tiles),
+        in_specs=[VMEM, VMEM, pl.BlockSpec(memory_space=pltpu.HBM)],
+        out_specs=[VMEM] * 6,
         out_shape=[
             jax.ShapeDtypeStruct((rows, cols), BF16),
             jax.ShapeDtypeStruct((rows, heads), F32),
             jax.ShapeDtypeStruct((heads, rows), F32),
             jax.ShapeDtypeStruct((EXTRA, cols), BF16),
             jax.ShapeDtypeStruct((rows, heads), F32),
-        ],
+            jax.ShapeDtypeStruct((tiles, rows, cols // tiles), BF16),
+        ],
+        scratch_shapes=[pltpu.SemaphoreType.DMA((tiles,))],
         compiler_params=params(),
         cost_estimate=cost(2 * rows * cols * 256, 4 * rows * cols, 2 * rows * heads),
         name="decays",
-    )(step_rows, rate, x)
+    )(step_rows, rate, in_hbm(x))
 
 
 def fresh_kernel(n, *refs):
@@ -192,7 +206,7 @@
 
 def total_kernel(order, *refs):
     place = position(len(order))
-    slices, (out, decay, factors) = refs[:-3], refs[-3:]
+    slices, (token, out, decay, factors) = refs[:-4], refs[-4:]
     size = len(slices)
     gather_factors(order, slices, factors)
     product = jnp.ones(factors.shape[1:], F32)
@@ -201,18 +215,22 @@
         factors[j] = product
         product = product * factor
     decay[...] = product
-    total = jnp.zeros(out.shape, F32)
-    for m, piece in zip(order, slices):
-        total = total + factors[place ^ m][:1] * piece[:STATE, :].astype(F32)
-    out[...] = total.astype(BF16)
-
-
-def group_total(order, slices):
+    scales = [factors[place ^ m][:1] for m in order]
+    step = 16
+    for row in range(0, STATE, step):
+        rows = slice(row, row + step)
+        total = jnp.zeros((step, out.shape[1]), F32)
+        for scale, piece in zip(scales, slices):
+            total = total + scale * piece[rows, :].astype(F32)
+        out[rows, :] = total.astype(BF16)
+
+
+def group_total(order, slices, token):
     size = len(slices)
     width = slices[0].shape[1]
     return pl.pallas_call(
         functools.partial(total_kernel, order),
-        in_specs=[VMEM] * size,
+        in_specs=[VMEM] * (size + 1),
         out_specs=[VMEM] * 2,
         out_shape=[
             jax.ShapeDtypeStruct((STATE, width), BF16),
@@ -222,10 +240,10 @@
         compiler_params=params(),
         cost_estimate=cost(2 * size * STATE * width, 2 * size * STATE * width),
         name="total",
-    )(*slices)
-
-
-def local_kernel(order, *refs):
+    )(*slices, token)
+
+
+def local_kernel(order, back_order, *refs):
     place = position(len(order))
     slices, (states, scales, ordered, factors) = refs[:-4], refs[-4:]
     size = len(slices)
@@ -236,7 +254,7 @@
     product = jnp.ones(factors.shape[1:], F32)
     for j in range(size):
         at = jnp.int32(0)
-        for i, m in enumerate(order):
+        for i, m in enumerate(back_order):
             at = jnp.where(place ^ j == m, i, at)
         states[at] = running
         scales[at] = product
@@ -244,11 +262,11 @@
         product = product * factors[j]
 
 
-def local_states(order, slices):
+def local_states(order, back_order, slices):
     size = len(slices)
     width = slices[0].shape[1]
     return pl.pallas_call(
-        functools.partial(local_kernel, order),
+        functools.partial(local_kernel, order, back_order),
         in_specs=[VMEM] * size,
         out_specs=[VMEM] * 2,
         out_shape=[
@@ -285,12 +303,21 @@
     )(states, scales, before, token)
 
 
-def inner_kernel(order, proj, cum, cum_rows, step, x, gate, base, slope, token, scores, mixed):
+def inner_kernel(
+    size, order, proj, cum, cum_rows, step, x, gate, base, slope, token, scores, mixed, held, sems
+):
     rows, heads = cum.shape
     width = base.shape[2]
     here = width // HEAD_DIM
     half = rows // 2
-    place = position(len(order))
+    place = position(size)
+
+    def gate_copy(at):
+        cols = pl.ds(pl.multiple_of((place ^ entry(order, at)) * width, width), width)
+        return pltpu.make_async_copy(gate.at[:, cols], held.at[at], sems.at[at])
+
+    for at in range(len(order)):
+        gate_copy(at).start()
     all_scores = lax.dot_general(
         proj[:, STATE:], proj[:, :STATE], (((1,), (1,)), ((), ())), preferred_element_type=F32
     )
@@ -311,13 +338,14 @@
 
     def one(at, carry):
         owner = place ^ entry(order, at)
-        cols = pl.ds(pl.multiple_of(owner * width, width), width)
         first = owner * here
         wide = jnp.dot(per_head, picks(first, heads, width, HEAD_DIM, 3), preferred_element_type=F32)
         columns = jnp.dot(
             parts, picks(first, heads, here * half, half, 3), preferred_element_type=F32
         )
-        values = x[:, cols].astype(F32)
+        each = x.shape[2] // width
+        piece = pl.ds(pl.multiple_of(owner % each * width, width), width)
+        values = x[owner // each, :, piece].astype(F32)
         scaled = (values * wide[:rows]).astype(BF16)
         early = (values[:half] * wide[2 * rows : 2 * rows + half]).astype(BF16)
         cross = jnp.dot(lower, early, preferred_element_type=F32) * wide[2 * rows + half :]
@@ -329,7 +357,8 @@
                 gap = columns[span, k * half : (k + 1) * half] - line[:, span]
                 block = (scores[i] * jnp.exp2(jnp.minimum(gap, 0.0))).astype(BF16)
                 mixed[span, mine] = jnp.dot(block, scaled[span, mine], preferred_element_type=F32)
-        g = gate[:, cols].astype(F32)
+        gate_copy(at).wait()
+        g = held[at].astype(F32)
         silu = g / (1.0 + jnp.exp(-g))
         base[at, :half, :] = mixed[:half, :] * silu[:half]
         base[at, half:, :] = (mixed[half:, :] + cross) * silu[half:]
@@ -346,36 +375,38 @@
     return value
 
 
-def inside(order, proj, cum, cum_rows, step, x, gate):
+def inside(size, order, proj, cum, cum_rows, step, x, gate):
     rows, heads = step.shape
     n = len(order)
-    width = x.shape[1] // n
-    return pl.pallas_call(
-        functools.partial(inner_kernel, order),
-        in_specs=[VMEM] * 6,
+    width = gate.shape[1] // size
+    return pl.pallas_call(
+        functools.partial(inner_kernel, size, order),
+        in_specs=[VMEM] * 5 + [pl.BlockSpec(memory_space=pltpu.HBM)],
         out_specs=[VMEM] * 3,
         out_shape=[jax.ShapeDtypeStruct((n, rows, width), F32)] * 2
         + [jax.ShapeDtypeStruct((8, STATE), F32)],
         scratch_shapes=[
             pltpu.VMEM((2, rows // 2, rows // 2), F32),
             pltpu.VMEM((rows, width), F32),
+            pltpu.VMEM((n, rows, width), BF16),
+            pltpu.SemaphoreType.DMA((n,)),
         ],
         compiler_params=params(),
         cost_estimate=cost(8 * rows * rows * n * width, 12 * rows * n * width, rows * rows * heads),
         name="inner",
-    )(proj, cum, cum_rows, step, x, gate)
-
-
-def outer_kernel(first, proj, base, slope, *refs):
+    )(proj, cum, cum_rows, step, x, in_hbm(gate))
+
+
+def outer_kernel(prior, proj, base, slope, *refs):
     states, (gated, squares) = refs[:-2], refs[-2:]
     c_rows = proj[:, STATE:]
-    if first:
+    if prior:
         total, states = states[0][...], states[1:]
     else:
         total = jnp.zeros(squares.shape, F32)
     for m, state in enumerate(states):
         read = jnp.dot(c_rows, state[...], preferred_element_type=F32)
-        value = base[first + m] + slope[first + m] * read
+        value = base[m] + slope[m] * read
         gated[m] = value
         square = value * value
         for k in range(value.shape[1] // STATE):
@@ -383,12 +414,12 @@
     squares[...] = total
 
 
-def outer_part(first, proj, base, slope, prior, states):
+def outer_part(proj, base, slope, prior, states):
     n = len(states)
     _, rows, width = base.shape
     states = [*prior, *states]
     return pl.pallas_call(
-        functools.partial(outer_kernel, first),
+        functools.partial(outer_kernel, len(prior)),
         in_specs=[VMEM] * (len(states) + 3),
         out_specs=[VMEM] * 2,
         out_shape=[
@@ -463,19 +494,26 @@
         size //= 2
     groups = devices // size
 
-    masks = [m for m in (1, 2, 4, 7, 3, 5, 6) if m < size]
-    order = [0] + masks
+    order = [m for m in SEND_ORDER if m < size]
+    back_order = [m for m in BACK_ORDER if m < size]
 
     with jax.named_scope("projection"):
         parts = terms_of_sum(project(hidden, weight), "head")
     with jax.named_scope("decays"):
-        weighted, cum, cum_rows, ends, step = decays(step.T, rate.reshape(1, heads), head_input)
+        weighted, cum, cum_rows, ends, step, x = decays(
+            step.T, rate.reshape(1, heads), head_input
+        )
     with jax.named_scope("states"):
         proj, *mine = fresh_states(size, parts, weighted, ends)
     with jax.named_scope("to_owners"):
-        slices = [mine[0]] + [swap(mine[m], "seq", m) for m in masks]
+        slices = [mine[0]] + [swap(mine[m], "seq", m) for m in order[1:]]
+    with jax.named_scope("inner"):
+        cut = size // 2 + 1
+        given = (proj, cum, cum_rows, step, x, gate_input)
+        *early, token = inside(size, back_order[:cut], *given)
+        *late, late_token = inside(size, back_order[cut:], *given)
     with jax.named_scope("groups"):
-        total, decay = group_total(order, slices)
+        total, decay = group_total(order, slices, token)
         up = [(i, (i + size) % devices) for i in range(devices)]
         before = jnp.zeros_like(total)
         for k in range(groups - 1):
@@ -485,20 +523,17 @@
             else:
                 sent = total
             before = lax.ppermute(sent, "seq", up)
-        states, scales = local_states(order, slices)
-    with jax.named_scope("inner"):
-        base, slope, token = inside(order, proj, cum, cum_rows, step, head_input, gate_input)
+        states, scales = local_states(order, back_order, slices)
     with jax.named_scope("from_owners"):
-        outs = entering_states(states, scales, before, token)
-        back = [outs[0]] + [swap(out, "seq", m) for m, out in zip(masks, outs[1:])]
+        outs = entering_states(states, scales, before, late_token)
+        back = [outs[0]] + [swap(out, "seq", m) for m, out in zip(back_order[1:], outs[1:])]
     with jax.named_scope("outer"):
-        cut = size // 2 + 1
-        some, squares = outer_part(0, proj, base, slope, [], back[:cut])
-        rest, squares = outer_part(cut, proj, base, slope, [squares], back[cut:])
+        some, squares = outer_part(proj, *early, [], back[:cut])
+        rest, squares = outer_part(proj, *late, [squares], back[cut:])
     with jax.named_scope("norm"):
         count = head_input.shape[1] * lax.axis_size("head")
         sums = terms_of_sum(squares, "head")
-        return normalise(count, order, sums, [some, rest], gain.reshape(1, -1))
+        return normalise(count, back_order, sums, [some, rest], gain.reshape(1, -1))
 
 
 def solution(mesh):

time: 59.8 us -> 52.7 us (0.88); the launches traced: 58.8 us -> 52.5 us
  waiting for transfers between devices: 14.3 us -> 8.47 us
  local copies, waits for them, and re-layouts: 1.62 us -> 0.01 us
  Pallas kernels: 16.3 us -> 17.7 us
    ppermute x16, waiting for transfers between devices: 14.2 us -> 6.98 us  [swap(): return lax.ppermute(value, axis, pairs)]
    pallas_call x5 -> x6, Pallas kernels: 10.4 us -> 12.6 us  [the longest x2 8.64 us: inside(): pl.pallas_call(functools.partial(inner_kernel, size, order), in_specs=[VM...]
    unnamed x14 -> x6, local copies, waits for them, and re-layouts: 1.62 us -> 0.01 us
    ppermute x1, waiting for transfers between devices: 0.01 us -> 1.5 us  [shards(): before = lax.ppermute(sent, 'seq', up)]
    pallas_call x1, Pallas kernels: 2.87 us -> 2.17 us  [project(): pl.pallas_call(functools.partial(project_kernel, tiles), in_specs=[pl.Blo...]
  transfers between devices with their start and end apart: 17 -> 17, of which waited for: 7 -> 9; matrix products, arithmetic and copies ran while one was open for 0% -> 0% of each run, Pallas kernels for 17% -> 23%
where the time goes in v3:
time: 52.7 us; the launch traced here: 52.5 us
  starting transfers between devices  26.2 us (50%)
  Pallas kernels  17.7 us (34%)
  waiting for transfers between devices  8.47 us (16%)
    ppermute x16, starting transfers between devices, swap(): return lax.ppermute(value, axis, pairs)  23.6 us
    pallas_call x2, Pallas kernels, inside(): pl.pallas_call(functools.partial(inner_kernel, size, order), in_specs=[VM...  8.64 us
    ppermute x16, waiting for transfers between devices, swap(): return lax.ppermute(value, axis, pairs)  6.98 us
    pallas_call x1, Pallas kernels, decays(): pl.pallas_call(functools.partial(decay_kernel, tiles), in_specs=[VMEM, VM...  2.66 us
    ppermute x1, starting transfers between devices, shards(): before = lax.ppermute(sent, 'seq', up)  2.59 us
    pallas_call x1, Pallas kernels, project(): pl.pallas_call(functools.partial(project_kernel, tiles), in_specs=[pl.Blo...  2.17 us
    pallas_call x1, Pallas kernels, normalise(): pl.pallas_call(functools.partial(norm_kernel, count, order, n, k), in_spe...  1.54 us
    ppermute x1, waiting for transfers between devices, shards(): before = lax.ppermute(sent, 'seq', up)  1.5 us
  transfers between devices with their start and end apart: 17, of which 9 were waited for; matrix products, arithmetic and copies ran while one was open for 0% of the time, Pallas kernels for 23%

profile of v3, /device:TPU:0, one launch (start us, length us, event | category | flops | bytes accessed | tf_op | source)
XLA Modules:
  0.0 52.5 jit_solution(11362920057295968214)
XLA Ops:
  0.0 0.0 copy-start
  0.0 0.0 copy-start.2
  0.0 2.2 %project.1.refs_0_ = f32[256,256]{1,0:T(8,128)S(1)} custom-call(bf16[256,2048]{1,0:T(8,128)(2,1)} %hidden.1, bf16[4096,256]{1,0:T(8,128)(2,1)} %weight.1), custom_call_target="tpu_custom_call" | custom-call | flops 268435456 | bytes 2097152 | tf_op jit(solution)/shard_map/projection/project/pallas_call | solution.py:85
  2.2 0.5 collective-permute-start
  2.7 0.0 copy-done
  2.7 0.0 copy-done.2
  2.7 2.7 %decays.1 = (bf16[256,4096]{1,0:T(8,128)(2,1)S(1)}, f32[256,64]{1,0:T(8,128)S(1)}, f32[64,256]{1,0:T(8,128)S(1)}, bf16[8,4096]{1,0:T(8,128)(2,1)S(1)}, f32[256,6...) custom-call(f32[64,256]{1,0:T(8,128)S(1)} %bitcast.3, f32[1,64]{1,0:T(1,128)S(1)} %bitcast.5, bf16[256,4096]{1,0:T(8,128)(2,1)} %x.1), custom_call_target="tpu_custom_call" | custom-call | flops 536870912 | bytes 4194304 | tf_op jit(solution)/shard_map/decays/decays/pallas_call | solution.py:145
  5.4 0.0 collective-permute-done.refs_1_
  5.4 0.5 fresh.1
  5.9 2.6 %collective-permute-start.1 = (bf16[136,512]{1,0:T(8,128)(2,1)S(1)}, bf16[136,512]{1,0:T(8,128)(2,1)S(1)}, u32[]{:S(2)}, u32[]{:S(2)}) collective-permute-start(bf16[136,512]{1,0:T(8,128)(2,1)S(1)} %get-tuple-element.53), channel_id=1, source_target_pairs={{0,2},{2,0},{4,6},{6,4},{8,10},{10,8},{12,14},{14,12},{16,18},{18,... | collective-permute-start | bytes 417800 | tf_op jit(solution)/shard_map/to_owners/ppermute | solution.py:475
  8.5 2.5 %collective-permute-start.2 = (bf16[136,512]{1,0:T(8,128)(2,1)S(1)}, bf16[136,512]{1,0:T(8,128)(2,1)S(1)}, u32[]{:S(2)}, u32[]{:S(2)}) collective-permute-start(bf16[136,512]{1,0:T(8,128)(2,1)S(1)} %get-tuple-element.54), channel_id=1, source_target_pairs={{0,12},{2,14},{4,8},{6,10},{8,4},{10,6},{12,0},{14,2},{16,28},{18,... | collective-permute-start | bytes 417800 | tf_op jit(solution)/shard_map/to_owners/ppermute | solution.py:475
  11.0 0.5 collective-permute-start.3
  11.5 0.0 collective-permute-start.4
  11.5 2.0 %collective-permute-start.5 = (bf16[136,512]{1,0:T(8,128)(2,1)S(1)}, bf16[136,512]{1,0:T(8,128)(2,1)S(1)}, u32[]{:S(2)}, u32[]{:S(2)}) collective-permute-start(bf16[136,512]{1,0:T(8,128)(2,1)S(1)} %get-tuple-element.57), channel_id=1, source_target_pairs={{0,8},{2,10},{4,12},{6,14},{8,0},{10,2},{12,4},{14,6},{16,24},{18,... | collective-permute-start | bytes 417800 | tf_op jit(solution)/shard_map/to_owners/ppermute | solution.py:475
  13.5 0.0 collective-permute-done.1.refs_1_
  13.5 2.5 %collective-permute-start.6 = (bf16[136,512]{1,0:T(8,128)(2,1)S(1)}, bf16[136,512]{1,0:T(8,128)(2,1)S(1)}, u32[]{:S(2)}, u32[]{:S(2)}) collective-permute-start(bf16[136,512]{1,0:T(8,128)(2,1)S(1)} %get-tuple-element.58), channel_id=1, source_target_pairs={{0,6},{2,4},{4,2},{6,0},{8,14},{10,12},{12,10},{14,8},{16,22},{18,... | collective-permute-start | bytes 417800 | tf_op jit(solution)/shard_map/to_owners/ppermute | solution.py:475
  15.9 0.0 collective-permute-done.2.refs_2_
  15.9 2.5 %collective-permute-start.7 = (bf16[136,512]{1,0:T(8,128)(2,1)S(1)}, bf16[136,512]{1,0:T(8,128)(2,1)S(1)}, u32[]{:S(2)}, u32[]{:S(2)}) collective-permute-start(bf16[136,512]{1,0:T(8,128)(2,1)S(1)} %get-tuple-element.59), channel_id=1, source_target_pairs={{0,14},{2,12},{4,10},{6,8},{8,6},{10,4},{12,2},{14,0},{16,30},{18,... | collective-permute-start | bytes 417800 | tf_op jit(solution)/shard_map/to_owners/ppermute | solution.py:475
  18.4 5.3 %inner.3 = (f32[5,256,512]{2,1,0:T(8,128)S(1)}, f32[5,256,512]{2,1,0:T(8,128)S(1)}, f32[8,128]{1,0:T(8,128)S(1)}) custom-call(bf16[256,256]{1,0:T(8,128)(2,1)S(1)} %get-tuple-element.43.proj, f32[256,64]{1,0:T(8,128)S(1)} %get-tuple-element.44.cum, f32[64,256]{1,0:T(8,128)S(1)} %get-tuple-element.45.cum_rows, f32[256,64]{1,0:T(8,128)S(1)} %get-tuple-element.46.step, ...), custom_call_target="tpu_custom_call" | custom-call | flops 1342177280 | bytes 7864320 | tf_op jit(solution)/shard_map/inner/inner/pallas_call | solution.py:382
  23.7 0.0 collective-permute-done.3.refs_3_
  23.8 0.0 collective-permute-done.4.refs_4_
  23.8 0.0 collective-permute-done.5.refs_5_
  23.8 0.0 collective-permute-done.6.refs_6_
  23.8 0.7 %collective-permute-done.7.refs_7_ = bf16[136,512]{1,0:T(8,128)(2,1)S(1)} collective-permute-done((bf16[136,512]{1,0:T(8,128)(2,1)S(1)}, bf16[136,512]{1,0:T(8,128)(2,1)S(1)}, u32[]{:S(2)}, u32[]{:S(2)}) %collective-permute-start.7) | collective-permute-done | bytes 139296 | tf_op jit(solution)/shard_map/to_owners/ppermute | solution.py:475
  24.5 0.7 %total.1 = (bf16[128,512]{1,0:T(8,128)(2,1)S(1)}, f32[8,512]{1,0:T(8,128)}) custom-call(bf16[136,512]{1,0:T(8,128)(2,1)S(1)} %get-tuple-element.52.refs_0_, bf16[136,512]{1,0:T(8,128)(2,1)S(1)} %collective-permute-done.1.refs_1_, bf16[136,512]{1,0:T(8,128)(2,1)S(1)} %collective-permute-done.2.refs_2_, bf16[136,512]{1,0:T(8,128)(2,1)S(1)} %collective-permute-done.3.refs_3_, ...), custom_call_target="tpu_custom_call" | custom-call | flops 1048576 | bytes 1048576 | tf_op jit(solution)/shard_map/groups/total/pallas_call | solution.py:231
  25.2 2.6 %collective-permute-start.8 = (bf16[128,512]{1,0:T(8,128)(2,1)S(1)}, bf16[128,512]{1,0:T(8,128)(2,1)S(1)}, u32[]{:S(2)}, u32[]{:S(2)}) collective-permute-start(bf16[128,512]{1,0:T(8,128)(2,1)S(1)} %get-tuple-element.63), channel_id=1, source_target_pairs={{0,16},{2,18},{4,20},{6,22},{8,24},{10,26},{12,28},{14,30},{16,0},... | collective-permute-start | bytes 393224 | tf_op jit(solution)/shard_map/groups/ppermute | solution.py:525
  27.8 3.3 %inner.2 = (f32[3,256,512]{2,1,0:T(8,128)S(1)}, f32[3,256,512]{2,1,0:T(8,128)S(1)}, f32[8,128]{1,0:T(8,128)S(1)}) custom-call(bf16[256,256]{1,0:T(8,128)(2,1)S(1)} %get-tuple-element.43.proj, f32[256,64]{1,0:T(8,128)S(1)} %get-tuple-element.44.cum, f32[64,256]{1,0:T(8,128)S(1)} %get-tuple-element.45.cum_rows, f32[256,64]{1,0:T(8,128)S(1)} %get-tuple-element.46.step, ...), custom_call_target="tpu_custom_call" | custom-call | flops 805306368 | bytes 4718592 | tf_op jit(solution)/shard_map/inner/inner/pallas_call | solution.py:382
  31.1 0.4 local.1
  31.5 1.5 %collective-permute-done.8.before = bf16[128,512]{1,0:T(8,128)(2,1)S(1)} collective-permute-done((bf16[128,512]{1,0:T(8,128)(2,1)S(1)}, bf16[128,512]{1,0:T(8,128)(2,1)S(1)}, u32[]{:S(2)}, u32[]{:S(2)}) %collective-permute-start.8) | collective-permute-done | bytes 131104 | tf_op jit(solution)/shard_map/groups/ppermute | solution.py:525
  33.0 0.2 entering.1
  33.3 1.5 %collective-permute-start.9 = (bf16[128,512]{1,0:T(8,128)(2,1)S(1)}, bf16[128,512]{1,0:T(8,128)(2,1)S(1)}, u32[]{:S(2)}, u32[]{:S(2)}) collective-permute-start(bf16[128,512]{1,0:T(8,128)(2,1)S(1)} %get-tuple-element.66), channel_id=1, source_target_pairs={{0,2},{2,0},{4,6},{6,4},{8,10},{10,8},{12,14},{14,12},{16,18},{18,... | collective-permute-start | bytes 393224 | tf_op jit(solution)/shard_map/from_owners/ppermute | solution.py:475
  34.8 1.8 %collective-permute-start.10 = (bf16[128,512]{1,0:T(8,128)(2,1)S(1)}, bf16[128,512]{1,0:T(8,128)(2,1)S(1)}, u32[]{:S(2)}, u32[]{:S(2)}) collective-permute-start(bf16[128,512]{1,0:T(8,128)(2,1)S(1)} %get-tuple-element.67), channel_id=1, source_target_pairs={{0,12},{2,14},{4,8},{6,10},{8,4},{10,6},{12,0},{14,2},{16,28},{18,... | collective-permute-start | bytes 393224 | tf_op jit(solution)/shard_map/from_owners/ppermute | solution.py:475
  36.7 0.3 collective-permute-start.11
  37.0 1.3 %collective-permute-start.12 = (bf16[128,512]{1,0:T(8,128)(2,1)S(1)}, bf16[128,512]{1,0:T(8,128)(2,1)S(1)}, u32[]{:S(2)}, u32[]{:S(2)}) collective-permute-start(bf16[128,512]{1,0:T(8,128)(2,1)S(1)} %get-tuple-element.69), channel_id=1, source_target_pairs={{0,10},{2,8},{4,14},{6,12},{8,2},{10,0},{12,6},{14,4},{16,26},{18,... | collective-permute-start | bytes 393224 | tf_op jit(solution)/shard_map/from_owners/ppermute | solution.py:475
  38.3 0.7 %collective-permute-start.13 = (bf16[128,512]{1,0:T(8,128)(2,1)S(1)}, bf16[128,512]{1,0:T(8,128)(2,1)S(1)}, u32[]{:S(2)}, u32[]{:S(2)}) collective-permute-start(bf16[128,512]{1,0:T(8,128)(2,1)S(1)} %get-tuple-element.71), channel_id=1, source_target_pairs={{0,8},{2,10},{4,12},{6,14},{8,0},{10,2},{12,4},{14,6},{16,24},{18,... | collective-permute-start | bytes 393224 | tf_op jit(solution)/shard_map/from_owners/ppermute | solution.py:475
  39.0 0.0 collective-permute-done.9.refs_1_
  39.0 2.6 %collective-permute-start.14 = (bf16[128,512]{1,0:T(8,128)(2,1)S(1)}, bf16[128,512]{1,0:T(8,128)(2,1)S(1)}, u32[]{:S(2)}, u32[]{:S(2)}) collective-permute-start(bf16[128,512]{1,0:T(8,128)(2,1)S(1)} %get-tuple-element.72), channel_id=1, source_target_pairs={{0,6},{2,4},{4,2},{6,0},{8,14},{10,12},{12,10},{14,8},{16,22},{18,... | collective-permute-start | bytes 393224 | tf_op jit(solution)/shard_map/from_owners/ppermute | solution.py:475
  41.6 0.2 collective-permute-done.10.refs_2_
  41.8 2.1 %collective-permute-start.15 = (bf16[128,512]{1,0:T(8,128)(2,1)S(1)}, bf16[128,512]{1,0:T(8,128)(2,1)S(1)}, u32[]{:S(2)}, u32[]{:S(2)}) collective-permute-start(bf16[128,512]{1,0:T(8,128)(2,1)S(1)} %get-tuple-element.73), channel_id=1, source_target_pairs={{0,14},{2,12},{4,10},{6,8},{8,6},{10,4},{12,2},{14,0},{16,30},{18,... | collective-permute-start | bytes 393224 | tf_op jit(solution)/shard_map/from_owners/ppermute | solution.py:475
  43.9 0.1 collective-permute-done.11.refs_3_
  44.1 1.0 %collective-permute-done.12.refs_4_ = bf16[128,512]{1,0:T(8,128)(2,1)S(1)} collective-permute-done((bf16[128,512]{1,0:T(8,128)(2,1)S(1)}, bf16[128,512]{1,0:T(8,128)(2,1)S(1)}, u32[]{:S(2)}, u32[]{:S(2)}) %collective-permute-start.12) | collective-permute-done | bytes 131104 | tf_op jit(solution)/shard_map/from_owners/ppermute | solution.py:475
  45.0 0.5 outer.2
  45.6 0.0 copy-start.1
  45.6 1.5 %collective-permute-done.13.refs_1_ = bf16[128,512]{1,0:T(8,128)(2,1)S(1)} collective-permute-done((bf16[128,512]{1,0:T(8,128)(2,1)S(1)}, bf16[128,512]{1,0:T(8,128)(2,1)S(1)}, u32[]{:S(2)}, u32[]{:S(2)}) %collective-permute-start.13) | collective-permute-done | bytes 131104 | tf_op jit(solution)/shard_map/from_owners/ppermute | solution.py:475
  47.1 0.7 %collective-permute-done.14.refs_2_ = bf16[128,512]{1,0:T(8,128)(2,1)S(1)} collective-permute-done((bf16[128,512]{1,0:T(8,128)(2,1)S(1)}, bf16[128,512]{1,0:T(8,128)(2,1)S(1)}, u32[]{:S(2)}, u32[]{:S(2)}) %collective-permute-start.14) | collective-permute-done | bytes 131104 | tf_op jit(solution)/shard_map/from_owners/ppermute | solution.py:475
  47.7 1.4 %collective-permute-done.15.refs_3_ = bf16[128,512]{1,0:T(8,128)(2,1)S(1)} collective-permute-done((bf16[128,512]{1,0:T(8,128)(2,1)S(1)}, bf16[128,512]{1,0:T(8,128)(2,1)S(1)}, u32[]{:S(2)}, u32[]{:S(2)}) %collective-permute-start.15) | collective-permute-done | bytes 131104 | tf_op jit(solution)/shard_map/from_owners/ppermute | solution.py:475
  49.1 0.4 outer.3
  49.5 0.1 collective-permute-start.16
  49.6 1.3 %collective-permute-done.16.refs_1_ = f32[256,128]{1,0:T(8,128)S(1)} collective-permute-done((f32[256,128]{1,0:T(8,128)S(1)}, f32[256,128]{1,0:T(8,128)S(1)}, u32[]{:S(2)}, u32[]{:S(2)}) %collective-permute-start.16) | collective-permute-done | bytes 131104 | tf_op jit(solution)/shard_map/norm/ppermute | solution.py:475
  50.9 0.0 copy-done.1
  50.9 1.5 %norm.1 = bf16[256,4096]{1,0:T(8,128)(2,1)} custom-call(f32[1,4096]{1,0:T(1,128)S(1)} %bitcast.4, f32[256,128]{1,0:T(8,128)S(1)} %get-tuple-element.74.refs_0_, f32[256,128]{1,0:T(8,128)S(1)} %collective-permute-done.16.refs_1_, f32[5,256,512]{2,1,0:T(8,128)S(1)} %get-tuple-element.75.refs_2_, f32[3,256,512]{2,1,0:T(8,128)S(1)} %get-tuple-element.76.refs_3_), custom_call_target="tpu_custom_call" | custom-call | flops 4194304 | bytes 6291456 | tf_op jit(solution)/shard_map/norm/norm/pallas_call | solution.py:461
Async XLA Ops:
  0.0 2.7 %copy-start = (f32[256,64]{0,1:T(8,128)S(1)}, f32[256,64]{0,1:T(8,128)}, u32[]{:S(2)}) copy-start(f32[256,64]{0,1:T(8,128)} %param.11) | copy-start | bytes 196612
  0.0 2.7 %copy-start.2 = (f32[64]{0:T(128)S(1)}, f32[64]{0:T(128)}, u32[]{:S(2)}) copy-start(f32[64]{0:T(128)} %param.12) | copy-start | bytes 772
  2.2 3.2 %collective-permute-start = (f32[256,256]{1,0:T(8,128)S(1)}, f32[256,256]{1,0:T(8,128)S(1)}, u32[]{:S(2)}, u32[]{:S(2)}) collective-permute-start(f32[256,256]{1,0:T(8,128)S(1)} %project.1.refs_0_), channel_id=1, source_target_pairs={{0,1},{1,0},{2,3},{3,2},{4,5},{5,4},{6,7},{7,6},{8,9},{9,8},{10,11... | collective-permute-start | bytes 786440 | tf_op jit(solution)/shard_map/projection/ppermute | solution.py:475
  5.9 7.6 %collective-permute-start.1 = (bf16[136,512]{1,0:T(8,128)(2,1)S(1)}, bf16[136,512]{1,0:T(8,128)(2,1)S(1)}, u32[]{:S(2)}, u32[]{:S(2)}) collective-permute-start(bf16[136,512]{1,0:T(8,128)(2,1)S(1)} %get-tuple-element.53), channel_id=1, source_target_pairs={{0,2},{2,0},{4,6},{6,4},{8,10},{10,8},{12,14},{14,12},{16,18},{18,... | collective-permute-start | bytes 417800 | tf_op jit(solution)/shard_map/to_owners/ppermute | solution.py:475
  8.5 7.5 %collective-permute-start.2 = (bf16[136,512]{1,0:T(8,128)(2,1)S(1)}, bf16[136,512]{1,0:T(8,128)(2,1)S(1)}, u32[]{:S(2)}, u32[]{:S(2)}) collective-permute-start(bf16[136,512]{1,0:T(8,128)(2,1)S(1)} %get-tuple-element.54), channel_id=1, source_target_pairs={{0,12},{2,14},{4,8},{6,10},{8,4},{10,6},{12,0},{14,2},{16,28},{18,... | collective-permute-start | bytes 417800 | tf_op jit(solution)/shard_map/to_owners/ppermute | solution.py:475
  11.0 12.8 %collective-permute-start.3 = (bf16[136,512]{1,0:T(8,128)(2,1)S(1)}, bf16[136,512]{1,0:T(8,128)(2,1)S(1)}, u32[]{:S(2)}, u32[]{:S(2)}) collective-permute-start(bf16[136,512]{1,0:T(8,128)(2,1)S(1)} %get-tuple-element.55), channel_id=1, source_target_pairs={{0,4},{2,6},{4,0},{6,2},{8,12},{10,14},{12,8},{14,10},{16,20},{18,... | collective-permute-start | bytes 417800 | tf_op jit(solution)/shard_map/to_owners/ppermute | solution.py:475
  11.5 12.3 %collective-permute-start.4 = (bf16[136,512]{1,0:T(8,128)(2,1)S(1)}, bf16[136,512]{1,0:T(8,128)(2,1)S(1)}, u32[]{:S(2)}, u32[]{:S(2)}) collective-permute-start(bf16[136,512]{1,0:T(8,128)(2,1)S(1)} %get-tuple-element.56), channel_id=1, source_target_pairs={{0,10},{2,8},{4,14},{6,12},{8,2},{10,0},{12,6},{14,4},{16,26},{18,... | collective-permute-start | bytes 417800 | tf_op jit(solution)/shard_map/to_owners/ppermute | solution.py:475
  11.5 12.2 %collective-permute-start.5 = (bf16[136,512]{1,0:T(8,128)(2,1)S(1)}, bf16[136,512]{1,0:T(8,128)(2,1)S(1)}, u32[]{:S(2)}, u32[]{:S(2)}) collective-permute-start(bf16[136,512]{1,0:T(8,128)(2,1)S(1)} %get-tuple-element.57), channel_id=1, source_target_pairs={{0,8},{2,10},{4,12},{6,14},{8,0},{10,2},{12,4},{14,6},{16,24},{18,... | collective-permute-start | bytes 417800 | tf_op jit(solution)/shard_map/to_owners/ppermute | solution.py:475
  13.5 10.3 %collective-permute-start.6 = (bf16[136,512]{1,0:T(8,128)(2,1)S(1)}, bf16[136,512]{1,0:T(8,128)(2,1)S(1)}, u32[]{:S(2)}, u32[]{:S(2)}) collective-permute-start(bf16[136,512]{1,0:T(8,128)(2,1)S(1)} %get-tuple-element.58), channel_id=1, source_target_pairs={{0,6},{2,4},{4,2},{6,0},{8,14},{10,12},{12,10},{14,8},{16,22},{18,... | collective-permute-start | bytes 417800 | tf_op jit(solution)/shard_map/to_owners/ppermute | solution.py:475
  15.9 8.6 %collective-permute-start.7 = (bf16[136,512]{1,0:T(8,128)(2,1)S(1)}, bf16[136,512]{1,0:T(8,128)(2,1)S(1)}, u32[]{:S(2)}, u32[]{:S(2)}) collective-permute-start(bf16[136,512]{1,0:T(8,128)(2,1)S(1)} %get-tuple-element.59), channel_id=1, source_target_pairs={{0,14},{2,12},{4,10},{6,8},{8,6},{10,4},{12,2},{14,0},{16,30},{18,... | collective-permute-start | bytes 417800 | tf_op jit(solution)/shard_map/to_owners/ppermute | solution.py:475
  25.2 7.8 %collective-permute-start.8 = (bf16[128,512]{1,0:T(8,128)(2,1)S(1)}, bf16[128,512]{1,0:T(8,128)(2,1)S(1)}, u32[]{:S(2)}, u32[]{:S(2)}) collective-permute-start(bf16[128,512]{1,0:T(8,128)(2,1)S(1)} %get-tuple-element.63), channel_id=1, source_target_pairs={{0,16},{2,18},{4,20},{6,22},{8,24},{10,26},{12,28},{14,30},{16,0},... | collective-permute-start | bytes 393224 | tf_op jit(solution)/shard_map/groups/ppermute | solution.py:525
  33.3 5.7 %collective-permute-start.9 = (bf16[128,512]{1,0:T(8,128)(2,1)S(1)}, bf16[128,512]{1,0:T(8,128)(2,1)S(1)}, u32[]{:S(2)}, u32[]{:S(2)}) collective-permute-start(bf16[128,512]{1,0:T(8,128)(2,1)S(1)} %get-tuple-element.66), channel_id=1, source_target_pairs={{0,2},{2,0},{4,6},{6,4},{8,10},{10,8},{12,14},{14,12},{16,18},{18,... | collective-permute-start | bytes 393224 | tf_op jit(solution)/shard_map/from_owners/ppermute | solution.py:475
  34.8 7.0 %collective-permute-start.10 = (bf16[128,512]{1,0:T(8,128)(2,1)S(1)}, bf16[128,512]{1,0:T(8,128)(2,1)S(1)}, u32[]{:S(2)}, u32[]{:S(2)}) collective-permute-start(bf16[128,512]{1,0:T(8,128)(2,1)S(1)} %get-tuple-element.67), channel_id=1, source_target_pairs={{0,12},{2,14},{4,8},{6,10},{8,4},{10,6},{12,0},{14,2},{16,28},{18,... | collective-permute-start | bytes 393224 | tf_op jit(solution)/shard_map/from_owners/ppermute | solution.py:475
  36.7 7.4 %collective-permute-start.11 = (bf16[128,512]{1,0:T(8,128)(2,1)S(1)}, bf16[128,512]{1,0:T(8,128)(2,1)S(1)}, u32[]{:S(2)}, u32[]{:S(2)}) collective-permute-start(bf16[128,512]{1,0:T(8,128)(2,1)S(1)} %get-tuple-element.68), channel_id=1, source_target_pairs={{0,4},{2,6},{4,0},{6,2},{8,12},{10,14},{12,8},{14,10},{16,20},{18,... | collective-permute-start | bytes 393224 | tf_op jit(solution)/shard_map/from_owners/ppermute | solution.py:475
  37.0 8.1 %collective-permute-start.12 = (bf16[128,512]{1,0:T(8,128)(2,1)S(1)}, bf16[128,512]{1,0:T(8,128)(2,1)S(1)}, u32[]{:S(2)}, u32[]{:S(2)}) collective-permute-start(bf16[128,512]{1,0:T(8,128)(2,1)S(1)} %get-tuple-element.69), channel_id=1, source_target_pairs={{0,10},{2,8},{4,14},{6,12},{8,2},{10,0},{12,6},{14,4},{16,26},{18,... | collective-permute-start | bytes 393224 | tf_op jit(solution)/shard_map/from_owners/ppermute | solution.py:475
  38.3 8.8 %collective-permute-start.13 = (bf16[128,512]{1,0:T(8,128)(2,1)S(1)}, bf16[128,512]{1,0:T(8,128)(2,1)S(1)}, u32[]{:S(2)}, u32[]{:S(2)}) collective-permute-start(bf16[128,512]{1,0:T(8,128)(2,1)S(1)} %get-tuple-element.71), channel_id=1, source_target_pairs={{0,8},{2,10},{4,12},{6,14},{8,0},{10,2},{12,4},{14,6},{16,24},{18,... | collective-permute-start | bytes 393224 | tf_op jit(solution)/shard_map/from_owners/ppermute | solution.py:475
  39.0 8.8 %collective-permute-start.14 = (bf16[128,512]{1,0:T(8,128)(2,1)S(1)}, bf16[128,512]{1,0:T(8,128)(2,1)S(1)}, u32[]{:S(2)}, u32[]{:S(2)}) collective-permute-start(bf16[128,512]{1,0:T(8,128)(2,1)S(1)} %get-tuple-element.72), channel_id=1, source_target_pairs={{0,6},{2,4},{4,2},{6,0},{8,14},{10,12},{12,10},{14,8},{16,22},{18,... | collective-permute-start | bytes 393224 | tf_op jit(solution)/shard_map/from_owners/ppermute | solution.py:475
  41.8 7.3 %collective-permute-start.15 = (bf16[128,512]{1,0:T(8,128)(2,1)S(1)}, bf16[128,512]{1,0:T(8,128)(2,1)S(1)}, u32[]{:S(2)}, u32[]{:S(2)}) collective-permute-start(bf16[128,512]{1,0:T(8,128)(2,1)S(1)} %get-tuple-element.73), channel_id=1, source_target_pairs={{0,14},{2,12},{4,10},{6,8},{8,6},{10,4},{12,2},{14,0},{16,30},{18,... | collective-permute-start | bytes 393224 | tf_op jit(solution)/shard_map/from_owners/ppermute | solution.py:475
  45.6 5.4 %copy-start.1 = (f32[4096]{0:T(1024)S(1)}, f32[4096]{0:T(1024)}, u32[]{:S(2)}) copy-start(f32[4096]{0:T(1024)} %param.13) | copy-start | bytes 49156
  49.5 1.4 %collective-permute-start.16 = (f32[256,128]{1,0:T(8,128)S(1)}, f32[256,128]{1,0:T(8,128)S(1)}, u32[]{:S(2)}, u32[]{:S(2)}) collective-permute-start(f32[256,128]{1,0:T(8,128)S(1)} %get-tuple-element.74.refs_0_), channel_id=1, source_target_pairs={{0,1},{1,0},{2,3},{3,2},{4,5},{5,4},{6,7},{7,6},{8,9},{9,8},{10,11... | collective-permute-start | bytes 393224 | tf_op jit(solution)/shard_map/norm/ppermute | solution.py:475

commit v4 on v3

--- a/solution.py
+++ b/solution.py
@@ -33,6 +33,16 @@
 
 def cost(flops, moved, exps=0):
     return pl.CostEstimate(flops=flops, bytes_accessed=moved, transcendentals=exps)
+
+
+def turns(order, size):
+    last = size - 1
+    return [(m, m ^ last if 0 < m < last else m) for m in order if m < size]
+
+
+def partner(pair):
+    even, odd = pair
+    return even + (lax.axis_index("head") % 2) * (odd - even)
 
 
 def position(size):
@@ -80,7 +90,7 @@
 def project(hidden, weight):
     rows, depth = hidden.shape
     cols = weight.shape[1]
-    tiles = 4
+    tiles = 2
     tile = depth // tiles
     return pl.pallas_call(
         functools.partial(project_kernel, tiles),
@@ -124,18 +134,22 @@
     factor = halves(jnp.exp(last - total) * step, 3)
     final = halves(jnp.broadcast_to(jnp.exp(last), (EXTRA, heads)), 3)
     both = jnp.concatenate([factor, final], axis=0)
+    wides = []
     for at in range(tiles):
         here = slice(at * lanes, (at + 1) * lanes)
         pick = picks(at * (lanes // HEAD_DIM), heads, lanes, HEAD_DIM, 3)
         wide = jnp.dot(both, pick, preferred_element_type=F32)
-        copies[at].wait()
-        weighted[:, here] = (held[at].astype(F32) * wide[:rows]).astype(BF16)
+        wides.append(wide[:rows])
         end = wide[rows:]
         high = end.astype(BF16).astype(F32)
         middle = (end - high).astype(BF16).astype(F32)
         low = end - high - middle
         row = lax.broadcasted_iota(jnp.int32, end.shape, 0)
         ends[:, here] = jnp.where(row == 0, high, jnp.where(row == 1, middle, low)).astype(BF16)
+    for at in range(tiles):
+        copies[at].wait()
+        here = slice(at * lanes, (at + 1) * lanes)
+        weighted[:, here] = (held[at].astype(F32) * wides[at]).astype(BF16)
 
 
 def decays(step_rows, rate, x):
@@ -161,7 +175,7 @@
     )(step_rows, rate, in_hbm(x))
 
 
-def fresh_kernel(n, *refs):
+def fresh_kernel(order, n, *refs):
     parts, (weighted, ends, proj), slices = refs[:n], refs[n : n + 3], refs[n + 3 :]
     size = len(slices)
     place = position(size)
@@ -172,8 +186,8 @@
     proj[...] = rounded
     width = weighted.shape[1] // size
     b_rows = rounded[:, :STATE]
-    for m in range(size):
-        cols = pl.ds(pl.multiple_of((place ^ m) * width, width), width)
+    for m, pair in enumerate(order):
+        cols = pl.ds(pl.multiple_of((place ^ partner(pair)) * width, width), width)
         state = lax.dot_general(
             b_rows, weighted[:, cols], (((0,), (0,)), ((), ())), preferred_element_type=F32
         )
@@ -181,12 +195,13 @@
         slices[m][STATE:, :] = ends[:, cols]
 
 
-def fresh_states(size, parts, weighted, ends):
+def fresh_states(order, parts, weighted, ends):
     rows, cols = weighted.shape
+    size = len(order)
     width = cols // size
     n = len(parts)
     return pl.pallas_call(
-        functools.partial(fresh_kernel, n),
+        functools.partial(fresh_kernel, order, n),
         in_specs=[VMEM] * (n + 2),
         out_specs=[VMEM] * (1 + size),
         out_shape=[jax.ShapeDtypeStruct((rows, 2 * STATE), BF16)]
@@ -199,9 +214,9 @@
 
 def gather_factors(order, slices, factors):
     place = position(len(order))
-    for m, piece in zip(order, slices):
+    for pair, piece in zip(order, slices):
         tail = piece[STATE:, :].astype(F32)
-        factors[place ^ m] = jnp.broadcast_to(tail[0:1] + (tail[1:2] + tail[2:3]), factors.shape[1:])
+        factors[place ^ partner(pair)] = jnp.broadcast_to(tail[0:1] + (tail[1:2] + tail[2:3]), factors.shape[1:])
 
 
 def total_kernel(order, *refs):
@@ -215,7 +230,7 @@
         factors[j] = product
         product = product * factor
     decay[...] = product
-    scales = [factors[place ^ m][:1] for m in order]
+    scales = [factors[place ^ partner(pair)][:1] for pair in order]
     step = 16
     for row in range(0, STATE, step):
         rows = slice(row, row + step)
@@ -248,14 +263,14 @@
     slices, (states, scales, ordered, factors) = refs[:-4], refs[-4:]
     size = len(slices)
     gather_factors(order, slices, factors)
-    for m, piece in zip(order, slices):
-        ordered[place ^ m] = piece[:STATE, :]
+    for pair, piece in zip(order, slices):
+        ordered[place ^ partner(pair)] = piece[:STATE, :]
     running = jnp.zeros(states.shape[1:], F32)
     product = jnp.ones(factors.shape[1:], F32)
     for j in range(size):
         at = jnp.int32(0)
-        for i, m in enumerate(back_order):
-            at = jnp.where(place ^ j == m, i, at)
+        for i, pair in enumerate(back_order):
+            at = jnp.where(place ^ j == partner(pair), i, at)
         states[at] = running
         scales[at] = product
         running = running * factors[j][:1] + ordered[j].astype(F32)
@@ -303,9 +318,11 @@
     )(states, scales, before, token)
 
 
-def inner_kernel(
-    size, order, proj, cum, cum_rows, step, x, gate, base, slope, token, scores, mixed, held, sems
-):
+def inner_kernel(size, order, leads, proj, cum, cum_rows, step, x, gate, base, slope, *refs):
+    if leads:
+        token, held, scores, mixed, sems = refs
+    else:
+        token, scores, mixed = refs
     rows, heads = cum.shape
     width = base.shape[2]
     here = width // HEAD_DIM
@@ -316,8 +333,9 @@
         cols = pl.ds(pl.multiple_of((place ^ entry(order, at)) * width, width), width)
         return pltpu.make_async_copy(gate.at[:, cols], held.at[at], sems.at[at])
 
-    for at in range(len(order)):
-        gate_copy(at).start()
+    if leads:
+        for at in range(len(order)):
+            gate_copy(at).start()
     all_scores = lax.dot_general(
         proj[:, STATE:], proj[:, :STATE], (((1,), (1,)), ((), ())), preferred_element_type=F32
     )
@@ -335,9 +353,12 @@
     per_head = jnp.concatenate([halves(value, 3) for value in (step[...], grown, later)], axis=0)
     parts = halves(total * LOG2E, 3)
     token[...] = jnp.zeros(token.shape, F32)
+    lane = lax.broadcasted_iota(jnp.int32, (half, 2 * HEAD_DIM), 1)
+    first_head = jnp.where(lane < HEAD_DIM, 1.0, 0.0).astype(BF16)
+    second_head = jnp.where(lane < HEAD_DIM, 0.0, 1.0).astype(BF16)
 
     def one(at, carry):
-        owner = place ^ entry(order, at)
+        owner = place ^ entry(order if leads else order[-base.shape[0] :], at)
         first = owner * here
         wide = jnp.dot(per_head, picks(first, heads, width, HEAD_DIM, 3), preferred_element_type=F32)
         columns = jnp.dot(
@@ -349,16 +370,26 @@
         scaled = (values * wide[:rows]).astype(BF16)
         early = (values[:half] * wide[2 * rows : 2 * rows + half]).astype(BF16)
         cross = jnp.dot(lower, early, preferred_element_type=F32) * wide[2 * rows + half :]
-        for k in range(here):
-            line = cum_rows[pl.ds(first + k, 1), :] * LOG2E
-            mine = slice(k * HEAD_DIM, (k + 1) * HEAD_DIM)
+        for k in range(0, here, 2):
+            pair = slice(k * HEAD_DIM, (k + 2) * HEAD_DIM)
+            lines = [cum_rows[pl.ds(first + k + n, 1), :] * LOG2E for n in range(2)]
             for i in range(2):
                 span = slice(i * half, (i + 1) * half)
-                gap = columns[span, k * half : (k + 1) * half] - line[:, span]
-                block = (scores[i] * jnp.exp2(jnp.minimum(gap, 0.0))).astype(BF16)
-                mixed[span, mine] = jnp.dot(block, scaled[span, mine], preferred_element_type=F32)
-        gate_copy(at).wait()
-        g = held[at].astype(F32)
+                blocks = []
+                for n, line in enumerate(lines):
+                    gap = columns[span, (k + n) * half : (k + n + 1) * half] - line[:, span]
+                    blocks.append((scores[i] * jnp.exp2(jnp.minimum(gap, 0.0))).astype(BF16))
+                both = scaled[span, pair]
+                mixed[span, pair] = jnp.dot(
+                    jnp.concatenate(blocks, axis=1),
+                    jnp.concatenate([both * first_head, both * second_head], axis=0),
+                    preferred_element_type=F32,
+                )
+        if leads:
+            gate_copy(at).wait()
+            g = held[at].astype(F32)
+        else:
+            g = gate[at + len(order) - base.shape[0]].astype(F32)
         silu = g / (1.0 + jnp.exp(-g))
         base[at, :half, :] = mixed[:half, :] * silu[:half]
         base[at, half:, :] = (mixed[half:, :] + cross) * silu[half:]
@@ -366,35 +397,41 @@
         return carry
 
     lax.fori_loop(0, base.shape[0], one, 0)
+    if leads:
+        for at in range(base.shape[0], len(order)):
+            gate_copy(at).wait()
 
 
 def entry(order, at):
-    value = jnp.int32(order[0])
-    for i, m in enumerate(order):
-        value = jnp.where(at == i, m, value)
+    value = jnp.int32(0)
+    for i, pair in enumerate(order):
+        value = jnp.where(at == i, partner(pair), value)
     return value
 
 
-def inside(size, order, proj, cum, cum_rows, step, x, gate):
+def inside(order, start, stop, proj, cum, cum_rows, step, x, gate):
     rows, heads = step.shape
-    n = len(order)
-    width = gate.shape[1] // size
-    return pl.pallas_call(
-        functools.partial(inner_kernel, size, order),
-        in_specs=[VMEM] * 5 + [pl.BlockSpec(memory_space=pltpu.HBM)],
-        out_specs=[VMEM] * 3,
+    size, n = len(order), stop - start
+    first = start == 0
+    width = heads // size * HEAD_DIM
+    held = [jax.ShapeDtypeStruct((size, rows, width), BF16)] if first else []
+    sems = [pltpu.SemaphoreType.DMA((size,))] if first else []
+    return pl.pallas_call(
+        functools.partial(inner_kernel, size, order if first else order[:stop], first),
+        in_specs=[VMEM] * 5 + [pl.BlockSpec(memory_space=pltpu.HBM) if first else VMEM],
+        out_specs=[VMEM] * (3 + len(held)),
         out_shape=[jax.ShapeDtypeStruct((n, rows, width), F32)] * 2
-        + [jax.ShapeDtypeStruct((8, STATE), F32)],
+        + [jax.ShapeDtypeStruct((8, STATE), F32)]
+        + held,
         scratch_shapes=[
             pltpu.VMEM((2, rows // 2, rows // 2), F32),
             pltpu.VMEM((rows, width), F32),
-            pltpu.VMEM((n, rows, width), BF16),
-            pltpu.SemaphoreType.DMA((n,)),
-        ],
+        ]
+        + sems,
         compiler_params=params(),
         cost_estimate=cost(8 * rows * rows * n * width, 12 * rows * n * width, rows * rows * heads),
         name="inner",
-    )(proj, cum, cum_rows, step, x, in_hbm(gate))
+    )(proj, cum, cum_rows, step, x, in_hbm(gate) if first else gate)
 
 
 def outer_kernel(prior, proj, base, slope, *refs):
@@ -444,7 +481,7 @@
     width = held.shape[2]
     pieces = [(ref, i) for ref in gated for i in range(ref.shape[0])]
     for at, (ref, i) in enumerate(pieces):
-        cols = pl.ds(pl.multiple_of((place ^ order[at]) * width, width), width)
+        cols = pl.ds(pl.multiple_of((place ^ partner(order[at])) * width, width), width)
         held[at] = (ref[i] * scale * gain[:, cols]).astype(BF16)
         copy = pltpu.make_async_copy(held.at[at], out.at[:, cols], sems.at[at])
         copy.start()
@@ -473,6 +510,16 @@
 def swap(value, axis, mask):
     pairs = [(i, i ^ mask) for i in range(lax.axis_size(axis))]
     return lax.ppermute(value, axis, pairs)
+
+
+def exchange(value, pair):
+    count = lax.axis_size("head")
+    pairs = [
+        (i * count + c, (i ^ pair[c % 2]) * count + c)
+        for i in range(lax.axis_size("seq"))
+        for c in range(count)
+    ]
+    return lax.ppermute(value, ("seq", "head"), pairs)
 
 
 def terms_of_sum(value, axis):
@@ -494,8 +541,8 @@
         size //= 2
     groups = devices // size
 
-    order = [m for m in SEND_ORDER if m < size]
-    back_order = [m for m in BACK_ORDER if m < size]
+    order = turns(SEND_ORDER, size)
+    back_order = turns(BACK_ORDER, size)
 
     with jax.named_scope("projection"):
         parts = terms_of_sum(project(hidden, weight), "head")
@@ -504,16 +551,18 @@
             step.T, rate.reshape(1, heads), head_input
         )
     with jax.named_scope("states"):
-        proj, *mine = fresh_states(size, parts, weighted, ends)
+        proj, *mine = fresh_states(order, parts, weighted, ends)
     with jax.named_scope("to_owners"):
-        slices = [mine[0]] + [swap(mine[m], "seq", m) for m in order[1:]]
+        slices = [mine[0]] + [exchange(part, pair) for pair, part in zip(order[1:], mine[1:])]
     with jax.named_scope("inner"):
-        cut = size // 2 + 1
-        given = (proj, cum, cum_rows, step, x, gate_input)
-        *early, token = inside(size, back_order[:cut], *given)
-        *late, late_token = inside(size, back_order[cut:], *given)
+        ends_at = sorted({size // 2 + 1, size})
+        bounds = list(zip([0] + ends_at[:-1], ends_at))
+        inner, gate = [], gate_input
+        for a, b in bounds:
+            *made, gate = [*inside(back_order, a, b, proj, cum, cum_rows, step, x, gate), gate][:4]
+            inner.append(made)
     with jax.named_scope("groups"):
-        total, decay = group_total(order, slices, token)
+        total, decay = group_total(order, slices, inner[0][2])
         up = [(i, (i + size) % devices) for i in range(devices)]
         before = jnp.zeros_like(total)
         for k in range(groups - 1):
@@ -525,15 +574,18 @@
             before = lax.ppermute(sent, "seq", up)
         states, scales = local_states(order, back_order, slices)
     with jax.named_scope("from_owners"):
-        outs = entering_states(states, scales, before, late_token)
-        back = [outs[0]] + [swap(out, "seq", m) for m, out in zip(back_order[1:], outs[1:])]
+        outs = entering_states(states, scales, before, inner[min(1, len(inner) - 1)][2])
+        back = [outs[0]] + [exchange(out, pair) for pair, out in zip(back_order[1:], outs[1:])]
     with jax.named_scope("outer"):
-        some, squares = outer_part(proj, *early, [], back[:cut])
-        rest, squares = outer_part(proj, *late, [squares], back[cut:])
+        gated, squares = [], []
+        for (a, b), (base, slope, _) in zip(bounds, inner):
+            value, total = outer_part(proj, base, slope, squares, back[a:b])
+            gated.append(value)
+            squares = [total]
     with jax.named_scope("norm"):
         count = head_input.shape[1] * lax.axis_size("head")
-        sums = terms_of_sum(squares, "head")
-        return normalise(count, back_order, sums, [some, rest], gain.reshape(1, -1))
+        sums = terms_of_sum(squares[0], "head")
+        return normalise(count, back_order, sums, gated, gain.reshape(1, -1))
 
 
 def solution(mesh):

time: 52.7 us -> 51.9 us (0.985)
  waiting for transfers between devices: 8.47 us -> 11 us
  Pallas kernels: 17.7 us -> 15.7 us
  starting transfers between devices: 26.2 us -> 24.8 us
    ppermute x16 -> x2, starting transfers between devices: 23.6 us -> 0.59 us  [swap(): return lax.ppermute(value, axis, pairs)]
    ppermute x0 -> x14, starting transfers between devices: none -> 21.6 us  [exchange(): return lax.ppermute(value, ('seq', 'head'), pairs)]
    ppermute x0 -> x14, waiting for transfers between devices: none -> 7.45 us  [exchange(): return lax.ppermute(value, ('seq', 'head'), pairs)]
    ppermute x16 -> x2, waiting for transfers between devices: 6.98 us -> 1.34 us  [swap(): return lax.ppermute(value, axis, pairs)]
    pallas_call x3, Pallas kernels: 9.13 us -> 8.06 us  [the longest x2 7.58 us: inside(): pl.pallas_call(functools.partial(inner_kernel, size, order if first else...]
    pallas_call x1, Pallas kernels: 2.66 us -> 1.88 us  [decays(): pl.pallas_call(functools.partial(decay_kernel, tiles), in_specs=[VMEM, VM...]
    ppermute x1, waiting for transfers between devices: 1.5 us -> 2.24 us  [shards(): before = lax.ppermute(sent, 'seq', up)]
  transfers between devices with their start and end apart: 17 -> 17, of which waited for: 9 -> 6; matrix products, arithmetic and copies ran while one was open for 0% -> 0% of each run, Pallas kernels for 23% -> 20%
where the time goes in v4:
time: 51.9 us; the launch traced here: 51.7 us
  starting transfers between devices  24.8 us (48%)
  Pallas kernels  15.7 us (30%)
  waiting for transfers between devices  11 us (21%)
    ppermute x14, starting transfers between devices, exchange(): return lax.ppermute(value, ('seq', 'head'), pairs)  21.6 us
    pallas_call x2, Pallas kernels, inside(): pl.pallas_call(functools.partial(inner_kernel, size, order if first else...  7.58 us
    ppermute x14, waiting for transfers between devices, exchange(): return lax.ppermute(value, ('seq', 'head'), pairs)  7.45 us
    ppermute x1, starting transfers between devices, shards(): before = lax.ppermute(sent, 'seq', up)  2.58 us
    ppermute x1, waiting for transfers between devices, shards(): before = lax.ppermute(sent, 'seq', up)  2.24 us
    pallas_call x1, Pallas kernels, project(): pl.pallas_call(functools.partial(project_kernel, tiles), in_specs=[pl.Blo...  2.02 us
    pallas_call x1, Pallas kernels, decays(): pl.pallas_call(functools.partial(decay_kernel, tiles), in_specs=[VMEM, VM...  1.88 us
    pallas_call x1, Pallas kernels, normalise(): pl.pallas_call(functools.partial(norm_kernel, count, order, n, k), in_spe...  1.54 us
  transfers between devices with their start and end apart: 17, of which 6 were waited for; matrix products, arithmetic and copies ran while one was open for 0% of the time, Pallas kernels for 20%

profile of v4, /device:TPU:0, one launch (start us, length us, event | category | flops | bytes accessed | tf_op | source)
XLA Modules:
  0.0 51.7 jit_solution(6644114375220601597)
XLA Ops:
  0.0 0.0 copy-start
  0.0 0.0 copy-start.2
  0.0 2.0 %project.1.refs_0_ = f32[256,256]{1,0:T(8,128)S(1)} custom-call(bf16[256,2048]{1,0:T(8,128)(2,1)} %hidden.1, bf16[4096,256]{1,0:T(8,128)(2,1)} %weight.1), custom_call_target="tpu_custom_call" | custom-call | flops 268435456 | bytes 2097152 | tf_op jit(solution)/shard_map/projection/project/pallas_call | solution.py:95
  2.0 0.5 %collective-permute-start = (f32[256,256]{1,0:T(8,128)S(1)}, f32[256,256]{1,0:T(8,128)S(1)}, u32[]{:S(2)}, u32[]{:S(2)}) collective-permute-start(f32[256,256]{1,0:T(8,128)S(1)} %project.1.refs_0_), channel_id=1, source_target_pairs={{0,1},{1,0},{2,3},{3,2},{4,5},{5,4},{6,7},{7,6},{8,9},{9,8},{10,11... | collective-permute-start | bytes 786440 | tf_op jit(solution)/shard_map/projection/ppermute | solution.py:512
  2.6 0.0 copy-done
  2.6 0.0 copy-done.2
  2.6 1.9 %decays.1 = (bf16[256,4096]{1,0:T(8,128)(2,1)S(1)}, f32[256,64]{1,0:T(8,128)S(1)}, f32[64,256]{1,0:T(8,128)S(1)}, bf16[8,4096]{1,0:T(8,128)(2,1)S(1)}, f32[256,6...) custom-call(f32[64,256]{1,0:T(8,128)S(1)} %bitcast.3, f32[1,64]{1,0:T(1,128)S(1)} %bitcast.5, bf16[256,4096]{1,0:T(8,128)(2,1)} %x.1), custom_call_target="tpu_custom_call" | custom-call | flops 536870912 | bytes 4194304 | tf_op jit(solution)/shard_map/decays/decays/pallas_call | solution.py:159
  4.4 0.0 collective-permute-done.refs_1_
  4.5 0.5 fresh.1
  4.9 2.6 %collective-permute-start.1 = (bf16[136,512]{1,0:T(8,128)(2,1)S(1)}, bf16[136,512]{1,0:T(8,128)(2,1)S(1)}, u32[]{:S(2)}, u32[]{:S(2)}) collective-permute-start(bf16[136,512]{1,0:T(8,128)(2,1)S(1)} %get-tuple-element.55), channel_id=1, source_target_pairs={{0,2},{1,13},{2,0},{3,15},{4,6},{5,9},{6,4},{7,11},{8,10},{9,5},{1... | collective-permute-start | bytes 417800 | tf_op jit(solution)/shard_map/to_owners/ppermute | solution.py:522
  7.5 2.5 %collective-permute-start.2 = (bf16[136,512]{1,0:T(8,128)(2,1)S(1)}, bf16[136,512]{1,0:T(8,128)(2,1)S(1)}, u32[]{:S(2)}, u32[]{:S(2)}) collective-permute-start(bf16[136,512]{1,0:T(8,128)(2,1)S(1)} %get-tuple-element.56), channel_id=1, source_target_pairs={{0,12},{1,3},{2,14},{3,1},{4,8},{5,7},{6,10},{7,5},{8,4},{9,11},{1... | collective-permute-start | bytes 417800 | tf_op jit(solution)/shard_map/to_owners/ppermute | solution.py:522
  10.1 0.5 collective-permute-start.3
  10.6 0.0 collective-permute-start.4
  10.6 2.0 %collective-permute-start.5 = (bf16[136,512]{1,0:T(8,128)(2,1)S(1)}, bf16[136,512]{1,0:T(8,128)(2,1)S(1)}, u32[]{:S(2)}, u32[]{:S(2)}) collective-permute-start(bf16[136,512]{1,0:T(8,128)(2,1)S(1)} %get-tuple-element.59), channel_id=1, source_target_pairs={{0,8},{1,7},{2,10},{3,5},{4,12},{5,3},{6,14},{7,1},{8,0},{9,15},{1... | collective-permute-start | bytes 417800 | tf_op jit(solution)/shard_map/to_owners/ppermute | solution.py:522
  12.6 0.0 collective-permute-done.1.refs_1_
  12.6 2.4 %collective-permute-start.6 = (bf16[136,512]{1,0:T(8,128)(2,1)S(1)}, bf16[136,512]{1,0:T(8,128)(2,1)S(1)}, u32[]{:S(2)}, u32[]{:S(2)}) collective-permute-start(bf16[136,512]{1,0:T(8,128)(2,1)S(1)} %get-tuple-element.60), channel_id=1, source_target_pairs={{0,6},{1,9},{2,4},{3,11},{4,2},{5,13},{6,0},{7,15},{8,14},{9,1},{1... | collective-permute-start | bytes 417800 | tf_op jit(solution)/shard_map/to_owners/ppermute | solution.py:522
  15.0 0.0 collective-permute-done.2.refs_2_
  15.0 3.6 %collective-permute-start.7 = (bf16[136,512]{1,0:T(8,128)(2,1)S(1)}, bf16[136,512]{1,0:T(8,128)(2,1)S(1)}, u32[]{:S(2)}, u32[]{:S(2)}) collective-permute-start(bf16[136,512]{1,0:T(8,128)(2,1)S(1)} %get-tuple-element.61), channel_id=1, source_target_pairs={{0,14},{1,15},{2,12},{3,13},{4,10},{5,11},{6,8},{7,9},{8,6},{9,7},... | collective-permute-start | bytes 417800 | tf_op jit(solution)/shard_map/to_owners/ppermute | solution.py:522
  18.6 5.0 %inner.2 = (f32[5,256,512]{2,1,0:T(8,128)S(1)}, f32[5,256,512]{2,1,0:T(8,128)S(1)}, f32[8,128]{1,0:T(8,128)S(1)}, bf16[8,256,512]{2,1,0:T(8,128)(2,1)S(1)}) custom-call(bf16[256,256]{1,0:T(8,128)(2,1)S(1)} %get-tuple-element.44.proj, f32[256,64]{1,0:T(8,128)S(1)} %get-tuple-element.45.cum, f32[64,256]{1,0:T(8,128)S(1)} %get-tuple-element.46.cum_rows, ...), custom_call_target="tpu_custom_call" | custom-call | flops 1342177280 | bytes 7864320 | tf_op jit(solution)/shard_map/inner/inner/pallas_call | solution.py:419
  23.6 0.0 collective-permute-done.3.refs_3_
  23.6 0.0 collective-permute-done.4.refs_4_
  23.6 0.0 collective-permute-done.5.refs_5_
  23.6 0.0 collective-permute-done.6.refs_6_
  23.6 0.0 collective-permute-done.7.refs_7_
  23.7 0.7 %total.1 = (bf16[128,512]{1,0:T(8,128)(2,1)S(1)}, f32[8,512]{1,0:T(8,128)}) custom-call(bf16[136,512]{1,0:T(8,128)(2,1)S(1)} %get-tuple-element.54.refs_0_, bf16[136,512]{1,0:T(8,128)(2,1)S(1)} %collective-permute-done.1.refs_1_, bf16[136,512]{1,0:T(8,128)(2,1)S(1)} %collective-permute-done.2.refs_2_, bf16[136,512]{1,0:T(8,128)(2,1)S(1)} %collective-permute-done.3.refs_3_, ...), custom_call_target="tpu_custom_call" | custom-call | flops 1048576 | bytes 1048576 | tf_op jit(solution)/shard_map/groups/total/pallas_call | solution.py:246
  24.3 2.6 %collective-permute-start.8 = (bf16[128,512]{1,0:T(8,128)(2,1)S(1)}, bf16[128,512]{1,0:T(8,128)(2,1)S(1)}, u32[]{:S(2)}, u32[]{:S(2)}) collective-permute-start(bf16[128,512]{1,0:T(8,128)(2,1)S(1)} %get-tuple-element.65), channel_id=1, source_target_pairs={{0,16},{2,18},{4,20},{6,22},{8,24},{10,26},{12,28},{14,30},{16,0},... | collective-permute-start | bytes 393224 | tf_op jit(solution)/shard_map/groups/ppermute | solution.py:574
  26.9 2.5 %inner.3 = (f32[3,256,512]{2,1,0:T(8,128)S(1)}, f32[3,256,512]{2,1,0:T(8,128)S(1)}, f32[8,128]{1,0:T(8,128)S(1)}) custom-call(bf16[256,256]{1,0:T(8,128)(2,1)S(1)} %get-tuple-element.44.proj, f32[256,64]{1,0:T(8,128)S(1)} %get-tuple-element.45.cum, f32[64,256]{1,0:T(8,128)S(1)} %get-tuple-element.46.cum_rows, f32[256,64]{1,0:T(8,128)S(1)} %get-tuple-element.47.step, ...), custom_call_target="tpu_custom_call" | custom-call | flops 805306368 | bytes 4718592 | tf_op jit(solution)/shard_map/inner/inner/pallas_call | solution.py:419
  29.5 0.4 local.1
  29.9 2.2 %collective-permute-done.8.before = bf16[128,512]{1,0:T(8,128)(2,1)S(1)} collective-permute-done((bf16[128,512]{1,0:T(8,128)(2,1)S(1)}, bf16[128,512]{1,0:T(8,128)(2,1)S(1)}, u32[]{:S(2)}, u32[]{:S(2)}) %collective-permute-start.8) | collective-permute-done | bytes 131104 | tf_op jit(solution)/shard_map/groups/ppermute | solution.py:574
  32.1 0.2 entering.1
  32.4 0.3 collective-permute-start.9
  32.7 1.6 %collective-permute-start.10 = (bf16[128,512]{1,0:T(8,128)(2,1)S(1)}, bf16[128,512]{1,0:T(8,128)(2,1)S(1)}, u32[]{:S(2)}, u32[]{:S(2)}) collective-permute-start(bf16[128,512]{1,0:T(8,128)(2,1)S(1)} %get-tuple-element.69), channel_id=1, source_target_pairs={{0,12},{1,3},{2,14},{3,1},{4,8},{5,7},{6,10},{7,5},{8,4},{9,11},{1... | collective-permute-start | bytes 393224 | tf_op jit(solution)/shard_map/from_owners/ppermute | solution.py:522
  34.3 1.1 %collective-permute-start.11 = (bf16[128,512]{1,0:T(8,128)(2,1)S(1)}, bf16[128,512]{1,0:T(8,128)(2,1)S(1)}, u32[]{:S(2)}, u32[]{:S(2)}) collective-permute-start(bf16[128,512]{1,0:T(8,128)(2,1)S(1)} %get-tuple-element.70), channel_id=1, source_target_pairs={{0,4},{1,11},{2,6},{3,9},{4,0},{5,15},{6,2},{7,13},{8,12},{9,3},{1... | collective-permute-start | bytes 393224 | tf_op jit(solution)/shard_map/from_owners/ppermute | solution.py:522
  35.4 2.0 %collective-permute-start.12 = (bf16[128,512]{1,0:T(8,128)(2,1)S(1)}, bf16[128,512]{1,0:T(8,128)(2,1)S(1)}, u32[]{:S(2)}, u32[]{:S(2)}) collective-permute-start(bf16[128,512]{1,0:T(8,128)(2,1)S(1)} %get-tuple-element.71), channel_id=1, source_target_pairs={{0,10},{1,5},{2,8},{3,7},{4,14},{5,1},{6,12},{7,3},{8,2},{9,13},{1... | collective-permute-start | bytes 393224 | tf_op jit(solution)/shard_map/from_owners/ppermute | solution.py:522
  37.4 0.5 collective-permute-start.13
  37.9 2.6 %collective-permute-done.9.refs_1_ = bf16[128,512]{1,0:T(8,128)(2,1)S(1)} collective-permute-done((bf16[128,512]{1,0:T(8,128)(2,1)S(1)}, bf16[128,512]{1,0:T(8,128)(2,1)S(1)}, u32[]{:S(2)}, u32[]{:S(2)}) %collective-permute-start.9) | collective-permute-done | bytes 131104 | tf_op jit(solution)/shard_map/from_owners/ppermute | solution.py:522
  40.5 1.1 %collective-permute-start.14 = (bf16[128,512]{1,0:T(8,128)(2,1)S(1)}, bf16[128,512]{1,0:T(8,128)(2,1)S(1)}, u32[]{:S(2)}, u32[]{:S(2)}) collective-permute-start(bf16[128,512]{1,0:T(8,128)(2,1)S(1)} %get-tuple-element.74), channel_id=1, source_target_pairs={{0,6},{1,9},{2,4},{3,11},{4,2},{5,13},{6,0},{7,15},{8,14},{9,1},{1... | collective-permute-start | bytes 393224 | tf_op jit(solution)/shard_map/from_owners/ppermute | solution.py:522
  41.5 0.0 collective-permute-done.10.refs_2_
  41.5 1.4 %collective-permute-start.15 = (bf16[128,512]{1,0:T(8,128)(2,1)S(1)}, bf16[128,512]{1,0:T(8,128)(2,1)S(1)}, u32[]{:S(2)}, u32[]{:S(2)}) collective-permute-start(bf16[128,512]{1,0:T(8,128)(2,1)S(1)} %get-tuple-element.75), channel_id=1, source_target_pairs={{0,14},{1,15},{2,12},{3,13},{4,10},{5,11},{6,8},{7,9},{8,6},{9,7},... | collective-permute-start | bytes 393224 | tf_op jit(solution)/shard_map/from_owners/ppermute | solution.py:522
  43.0 0.0 collective-permute-done.11.refs_3_
  43.0 0.0 collective-permute-done.12.refs_4_
  43.0 0.5 %outer.2 = (f32[5,256,512]{2,1,0:T(8,128)S(1)}, f32[256,128]{1,0:T(8,128)S(1)}) custom-call(bf16[256,256]{1,0:T(8,128)(2,1)S(1)} %get-tuple-element.44.proj, f32[5,256,512]{2,1,0:T(8,128)S(1)} %get-tuple-element.52.base, f32[5,256,512]{2,1,0:T(8,128)S(1)} %get-tuple-element.53.slope, bf16[128,512]{1,0:T(8,128)(2,1)S(1)} %get-tuple-element.67.refs_0_, ...), custom_call_target="tpu_custom_call" | custom-call | flops 167772160 | bytes 7864320 | tf_op jit(solution)/shard_map/outer/outer/pallas_call | solution.py:458
  43.5 0.0 copy-start.1
  43.5 1.9 %collective-permute-done.13.refs_1_ = bf16[128,512]{1,0:T(8,128)(2,1)S(1)} collective-permute-done((bf16[128,512]{1,0:T(8,128)(2,1)S(1)}, bf16[128,512]{1,0:T(8,128)(2,1)S(1)}, u32[]{:S(2)}, u32[]{:S(2)}) %collective-permute-start.13) | collective-permute-done | bytes 131104 | tf_op jit(solution)/shard_map/from_owners/ppermute | solution.py:522
  45.4 1.6 %collective-permute-done.14.refs_2_ = bf16[128,512]{1,0:T(8,128)(2,1)S(1)} collective-permute-done((bf16[128,512]{1,0:T(8,128)(2,1)S(1)}, bf16[128,512]{1,0:T(8,128)(2,1)S(1)}, u32[]{:S(2)}, u32[]{:S(2)}) %collective-permute-start.14) | collective-permute-done | bytes 131104 | tf_op jit(solution)/shard_map/from_owners/ppermute | solution.py:522
  47.0 1.4 %collective-permute-done.15.refs_3_ = bf16[128,512]{1,0:T(8,128)(2,1)S(1)} collective-permute-done((bf16[128,512]{1,0:T(8,128)(2,1)S(1)}, bf16[128,512]{1,0:T(8,128)(2,1)S(1)}, u32[]{:S(2)}, u32[]{:S(2)}) %collective-permute-start.15) | collective-permute-done | bytes 131104 | tf_op jit(solution)/shard_map/from_owners/ppermute | solution.py:522
  48.4 0.4 outer.3
  48.7 0.1 collective-permute-start.16
  48.8 1.3 %collective-permute-done.16.refs_1_ = f32[256,128]{1,0:T(8,128)S(1)} collective-permute-done((f32[256,128]{1,0:T(8,128)S(1)}, f32[256,128]{1,0:T(8,128)S(1)}, u32[]{:S(2)}, u32[]{:S(2)}) %collective-permute-start.16) | collective-permute-done | bytes 131104 | tf_op jit(solution)/shard_map/norm/ppermute | solution.py:512
  50.2 0.0 copy-done.1
  50.2 1.5 %norm.1 = bf16[256,4096]{1,0:T(8,128)(2,1)} custom-call(f32[1,4096]{1,0:T(1,128)S(1)} %bitcast.4, f32[256,128]{1,0:T(8,128)S(1)} %get-tuple-element.76.refs_0_, f32[256,128]{1,0:T(8,128)S(1)} %collective-permute-done.16.refs_1_, f32[5,256,512]{2,1,0:T(8,128)S(1)} %get-tuple-element.77.refs_2_, f32[3,256,512]{2,1,0:T(8,128)S(1)} %get-tuple-element.78.refs_3_), custom_call_target="tpu_custom_call" | custom-call | flops 4194304 | bytes 6291456 | tf_op jit(solution)/shard_map/norm/norm/pallas_call | solution.py:498
Async XLA Ops:
  0.0 2.6 %copy-start = (f32[256,64]{0,1:T(8,128)S(1)}, f32[256,64]{0,1:T(8,128)}, u32[]{:S(2)}) copy-start(f32[256,64]{0,1:T(8,128)} %param.11) | copy-start | bytes 196612
  0.0 2.6 %copy-start.2 = (f32[64]{0:T(128)S(1)}, f32[64]{0:T(128)}, u32[]{:S(2)}) copy-start(f32[64]{0:T(128)} %param.12) | copy-start | bytes 772
  2.0 2.4 %collective-permute-start = (f32[256,256]{1,0:T(8,128)S(1)}, f32[256,256]{1,0:T(8,128)S(1)}, u32[]{:S(2)}, u32[]{:S(2)}) collective-permute-start(f32[256,256]{1,0:T(8,128)S(1)} %project.1.refs_0_), channel_id=1, source_target_pairs={{0,1},{1,0},{2,3},{3,2},{4,5},{5,4},{6,7},{7,6},{8,9},{9,8},{10,11... | collective-permute-start | bytes 786440 | tf_op jit(solution)/shard_map/projection/ppermute | solution.py:512
  4.9 7.6 %collective-permute-start.1 = (bf16[136,512]{1,0:T(8,128)(2,1)S(1)}, bf16[136,512]{1,0:T(8,128)(2,1)S(1)}, u32[]{:S(2)}, u32[]{:S(2)}) collective-permute-start(bf16[136,512]{1,0:T(8,128)(2,1)S(1)} %get-tuple-element.55), channel_id=1, source_target_pairs={{0,2},{1,13},{2,0},{3,15},{4,6},{5,9},{6,4},{7,11},{8,10},{9,5},{1... | collective-permute-start | bytes 417800 | tf_op jit(solution)/shard_map/to_owners/ppermute | solution.py:522
  7.5 7.5 %collective-permute-start.2 = (bf16[136,512]{1,0:T(8,128)(2,1)S(1)}, bf16[136,512]{1,0:T(8,128)(2,1)S(1)}, u32[]{:S(2)}, u32[]{:S(2)}) collective-permute-start(bf16[136,512]{1,0:T(8,128)(2,1)S(1)} %get-tuple-element.56), channel_id=1, source_target_pairs={{0,12},{1,3},{2,14},{3,1},{4,8},{5,7},{6,10},{7,5},{8,4},{9,11},{1... | collective-permute-start | bytes 417800 | tf_op jit(solution)/shard_map/to_owners/ppermute | solution.py:522
  10.1 13.6 %collective-permute-start.3 = (bf16[136,512]{1,0:T(8,128)(2,1)S(1)}, bf16[136,512]{1,0:T(8,128)(2,1)S(1)}, u32[]{:S(2)}, u32[]{:S(2)}) collective-permute-start(bf16[136,512]{1,0:T(8,128)(2,1)S(1)} %get-tuple-element.57), channel_id=1, source_target_pairs={{0,4},{1,11},{2,6},{3,9},{4,0},{5,15},{6,2},{7,13},{8,12},{9,3},{1... | collective-permute-start | bytes 417800 | tf_op jit(solution)/shard_map/to_owners/ppermute | solution.py:522
  10.6 13.1 %collective-permute-start.4 = (bf16[136,512]{1,0:T(8,128)(2,1)S(1)}, bf16[136,512]{1,0:T(8,128)(2,1)S(1)}, u32[]{:S(2)}, u32[]{:S(2)}) collective-permute-start(bf16[136,512]{1,0:T(8,128)(2,1)S(1)} %get-tuple-element.58), channel_id=1, source_target_pairs={{0,10},{1,5},{2,8},{3,7},{4,14},{5,1},{6,12},{7,3},{8,2},{9,13},{1... | collective-permute-start | bytes 417800 | tf_op jit(solution)/shard_map/to_owners/ppermute | solution.py:522
  10.6 13.0 %collective-permute-start.5 = (bf16[136,512]{1,0:T(8,128)(2,1)S(1)}, bf16[136,512]{1,0:T(8,128)(2,1)S(1)}, u32[]{:S(2)}, u32[]{:S(2)}) collective-permute-start(bf16[136,512]{1,0:T(8,128)(2,1)S(1)} %get-tuple-element.59), channel_id=1, source_target_pairs={{0,8},{1,7},{2,10},{3,5},{4,12},{5,3},{6,14},{7,1},{8,0},{9,15},{1... | collective-permute-start | bytes 417800 | tf_op jit(solution)/shard_map/to_owners/ppermute | solution.py:522
  12.6 11.1 %collective-permute-start.6 = (bf16[136,512]{1,0:T(8,128)(2,1)S(1)}, bf16[136,512]{1,0:T(8,128)(2,1)S(1)}, u32[]{:S(2)}, u32[]{:S(2)}) collective-permute-start(bf16[136,512]{1,0:T(8,128)(2,1)S(1)} %get-tuple-element.60), channel_id=1, source_target_pairs={{0,6},{1,9},{2,4},{3,11},{4,2},{5,13},{6,0},{7,15},{8,14},{9,1},{1... | collective-permute-start | bytes 417800 | tf_op jit(solution)/shard_map/to_owners/ppermute | solution.py:522
  15.0 8.6 %collective-permute-start.7 = (bf16[136,512]{1,0:T(8,128)(2,1)S(1)}, bf16[136,512]{1,0:T(8,128)(2,1)S(1)}, u32[]{:S(2)}, u32[]{:S(2)}) collective-permute-start(bf16[136,512]{1,0:T(8,128)(2,1)S(1)} %get-tuple-element.61), channel_id=1, source_target_pairs={{0,14},{1,15},{2,12},{3,13},{4,10},{5,11},{6,8},{7,9},{8,6},{9,7},... | collective-permute-start | bytes 417800 | tf_op jit(solution)/shard_map/to_owners/ppermute | solution.py:522
  24.3 7.8 %collective-permute-start.8 = (bf16[128,512]{1,0:T(8,128)(2,1)S(1)}, bf16[128,512]{1,0:T(8,128)(2,1)S(1)}, u32[]{:S(2)}, u32[]{:S(2)}) collective-permute-start(bf16[128,512]{1,0:T(8,128)(2,1)S(1)} %get-tuple-element.65), channel_id=1, source_target_pairs={{0,16},{2,18},{4,20},{6,22},{8,24},{10,26},{12,28},{14,30},{16,0},... | collective-permute-start | bytes 393224 | tf_op jit(solution)/shard_map/groups/ppermute | solution.py:574
  32.4 8.1 %collective-permute-start.9 = (bf16[128,512]{1,0:T(8,128)(2,1)S(1)}, bf16[128,512]{1,0:T(8,128)(2,1)S(1)}, u32[]{:S(2)}, u32[]{:S(2)}) collective-permute-start(bf16[128,512]{1,0:T(8,128)(2,1)S(1)} %get-tuple-element.68), channel_id=1, source_target_pairs={{0,2},{1,13},{2,0},{3,15},{4,6},{5,9},{6,4},{7,11},{8,10},{9,5},{1... | collective-permute-start | bytes 393224 | tf_op jit(solution)/shard_map/from_owners/ppermute | solution.py:522
  32.7 8.8 %collective-permute-start.10 = (bf16[128,512]{1,0:T(8,128)(2,1)S(1)}, bf16[128,512]{1,0:T(8,128)(2,1)S(1)}, u32[]{:S(2)}, u32[]{:S(2)}) collective-permute-start(bf16[128,512]{1,0:T(8,128)(2,1)S(1)} %get-tuple-element.69), channel_id=1, source_target_pairs={{0,12},{1,3},{2,14},{3,1},{4,8},{5,7},{6,10},{7,5},{8,4},{9,11},{1... | collective-permute-start | bytes 393224 | tf_op jit(solution)/shard_map/from_owners/ppermute | solution.py:522
  34.3 8.7 %collective-permute-start.11 = (bf16[128,512]{1,0:T(8,128)(2,1)S(1)}, bf16[128,512]{1,0:T(8,128)(2,1)S(1)}, u32[]{:S(2)}, u32[]{:S(2)}) collective-permute-start(bf16[128,512]{1,0:T(8,128)(2,1)S(1)} %get-tuple-element.70), channel_id=1, source_target_pairs={{0,4},{1,11},{2,6},{3,9},{4,0},{5,15},{6,2},{7,13},{8,12},{9,3},{1... | collective-permute-start | bytes 393224 | tf_op jit(solution)/shard_map/from_owners/ppermute | solution.py:522
  35.4 7.6 %collective-permute-start.12 = (bf16[128,512]{1,0:T(8,128)(2,1)S(1)}, bf16[128,512]{1,0:T(8,128)(2,1)S(1)}, u32[]{:S(2)}, u32[]{:S(2)}) collective-permute-start(bf16[128,512]{1,0:T(8,128)(2,1)S(1)} %get-tuple-element.71), channel_id=1, source_target_pairs={{0,10},{1,5},{2,8},{3,7},{4,14},{5,1},{6,12},{7,3},{8,2},{9,13},{1... | collective-permute-start | bytes 393224 | tf_op jit(solution)/shard_map/from_owners/ppermute | solution.py:522
  37.4 8.0 %collective-permute-start.13 = (bf16[128,512]{1,0:T(8,128)(2,1)S(1)}, bf16[128,512]{1,0:T(8,128)(2,1)S(1)}, u32[]{:S(2)}, u32[]{:S(2)}) collective-permute-start(bf16[128,512]{1,0:T(8,128)(2,1)S(1)} %get-tuple-element.73), channel_id=1, source_target_pairs={{0,8},{1,7},{2,10},{3,5},{4,12},{5,3},{6,14},{7,1},{8,0},{9,15},{1... | collective-permute-start | bytes 393224 | tf_op jit(solution)/shard_map/from_owners/ppermute | solution.py:522
  40.5 6.5 %collective-permute-start.14 = (bf16[128,512]{1,0:T(8,128)(2,1)S(1)}, bf16[128,512]{1,0:T(8,128)(2,1)S(1)}, u32[]{:S(2)}, u32[]{:S(2)}) collective-permute-start(bf16[128,512]{1,0:T(8,128)(2,1)S(1)} %get-tuple-element.74), channel_id=1, source_target_pairs={{0,6},{1,9},{2,4},{3,11},{4,2},{5,13},{6,0},{7,15},{8,14},{9,1},{1... | collective-permute-start | bytes 393224 | tf_op jit(solution)/shard_map/from_owners/ppermute | solution.py:522
  41.5 6.9 %collective-permute-start.15 = (bf16[128,512]{1,0:T(8,128)(2,1)S(1)}, bf16[128,512]{1,0:T(8,128)(2,1)S(1)}, u32[]{:S(2)}, u32[]{:S(2)}) collective-permute-start(bf16[128,512]{1,0:T(8,128)(2,1)S(1)} %get-tuple-element.75), channel_id=1, source_target_pairs={{0,14},{1,15},{2,12},{3,13},{4,10},{5,11},{6,8},{7,9},{8,6},{9,7},... | collective-permute-start | bytes 393224 | tf_op jit(solution)/shard_map/from_owners/ppermute | solution.py:522
  43.5 6.6 %copy-start.1 = (f32[4096]{0:T(1024)S(1)}, f32[4096]{0:T(1024)}, u32[]{:S(2)}) copy-start(f32[4096]{0:T(1024)} %param.13) | copy-start | bytes 49156
  48.7 1.4 %collective-permute-start.16 = (f32[256,128]{1,0:T(8,128)S(1)}, f32[256,128]{1,0:T(8,128)S(1)}, u32[]{:S(2)}, u32[]{:S(2)}) collective-permute-start(f32[256,128]{1,0:T(8,128)S(1)} %get-tuple-element.76.refs_0_), channel_id=1, source_target_pairs={{0,1},{1,0},{2,3},{3,2},{4,5},{5,4},{6,7},{7,6},{8,9},{9,8},{10,11... | collective-permute-start | bytes 393224 | tf_op jit(solution)/shard_map/norm/ppermute | solution.py:512

commit v5 on v4

--- a/solution.py
+++ b/solution.py
@@ -13,7 +13,7 @@
 EPS = 1e-05
 EXTRA = 8
 LIMIT = 16 * 1024 * 1024
-SEND_ORDER = (0, 1, 6, 2, 5, 4, 3, 7)
+SEND_ORDER = (0, 1, 2, 3, 4, 5, 6, 7)
 BACK_ORDER = (0, 1, 6, 2, 5, 4, 3, 7)
 LOG2E = 1.4426950408889634
 
@@ -434,7 +434,7 @@
     )(proj, cum, cum_rows, step, x, in_hbm(gate) if first else gate)
 
 
-def outer_kernel(prior, proj, base, slope, *refs):
+def outer_kernel(prior, first, proj, base, slope, *refs):
     states, (gated, squares) = refs[:-2], refs[-2:]
     c_rows = proj[:, STATE:]
     if prior:
@@ -443,7 +443,7 @@
         total = jnp.zeros(squares.shape, F32)
     for m, state in enumerate(states):
         read = jnp.dot(c_rows, state[...], preferred_element_type=F32)
-        value = base[m] + slope[m] * read
+        value = base[first + m] + slope[first + m] * read
         gated[m] = value
         square = value * value
         for k in range(value.shape[1] // STATE):
@@ -451,12 +451,12 @@
     squares[...] = total
 
 
-def outer_part(proj, base, slope, prior, states):
+def outer_part(first, proj, base, slope, prior, states):
     n = len(states)
     _, rows, width = base.shape
     states = [*prior, *states]
     return pl.pallas_call(
-        functools.partial(outer_kernel, len(prior)),
+        functools.partial(outer_kernel, len(prior), first),
         in_specs=[VMEM] * (len(states) + 3),
         out_specs=[VMEM] * 2,
         out_shape=[
@@ -579,9 +579,12 @@
     with jax.named_scope("outer"):
         gated, squares = [], []
         for (a, b), (base, slope, _) in zip(bounds, inner):
-            value, total = outer_part(proj, base, slope, squares, back[a:b])
-            gated.append(value)
-            squares = [total]
+            cut = b - 1 if b == size and b - a > 1 else b
+            for i, j in ((a, cut), (cut, b)):
+                if i < j:
+                    value, total = outer_part(i - a, proj, base, slope, squares, back[i:j])
+                    gated.append(value)
+                    squares = [total]
     with jax.named_scope("norm"):
         count = head_input.shape[1] * lax.axis_size("head")
         sums = terms_of_sum(squares[0], "head")

time: 51.9 us -> 50.5 us (0.973)
  waiting for transfers between devices: 11 us -> 8.81 us
  starting transfers between devices: 24.8 us -> 25.6 us
    ppermute x14, waiting for transfers between devices: 7.45 us -> 5.74 us  [exchange(): return lax.ppermute(value, ('seq', 'head'), pairs)]
    ppermute x14, starting transfers between devices: 21.6 us -> 22.4 us  [exchange(): return lax.ppermute(value, ('seq', 'head'), pairs)]
  transfers between devices with their start and end apart: 17 -> 17, of which waited for: 6 -> 6; matrix products, arithmetic and copies ran while one was open for 0% -> 0% of each run, Pallas kernels for 20% -> 21%
where the time goes in v5:
time: 50.5 us; the launch traced here: 50.3 us
  starting transfers between devices  25.6 us (51%)
  Pallas kernels  15.7 us (31%)
  waiting for transfers between devices  8.81 us (17%)
    ppermute x14, starting transfers between devices, exchange(): return lax.ppermute(value, ('seq', 'head'), pairs)  22.4 us
    pallas_call x2, Pallas kernels, inside(): pl.pallas_call(functools.partial(inner_kernel, size, order if first else...  7.58 us
    ppermute x14, waiting for transfers between devices, exchange(): return lax.ppermute(value, ('seq', 'head'), pairs)  5.74 us
    ppermute x1, starting transfers between devices, shards(): before = lax.ppermute(sent, 'seq', up)  2.59 us
    pallas_call x1, Pallas kernels, project(): pl.pallas_call(functools.partial(project_kernel, tiles), in_specs=[pl.Blo...  2.02 us
    pallas_call x1, Pallas kernels, decays(): pl.pallas_call(functools.partial(decay_kernel, tiles), in_specs=[VMEM, VM...  1.78 us
    ppermute x1, waiting for transfers between devices, shards(): before = lax.ppermute(sent, 'seq', up)  1.73 us
    pallas_call x1, Pallas kernels, normalise(): pl.pallas_call(functools.partial(norm_kernel, count, order, n, k), in_spe...  1.54 us
  transfers between devices with their start and end apart: 17, of which 6 were waited for; matrix products, arithmetic and copies ran while one was open for 0% of the time, Pallas kernels for 21%

profile of v5, /device:TPU:0, one launch (start us, length us, event | category | flops | bytes accessed | tf_op | source)
XLA Modules:
  0.0 50.3 jit_solution(14078734847689339125)
XLA Ops:
  0.0 0.0 copy-start
  0.0 0.0 copy-start.2
  0.0 2.0 %project.1.refs_0_ = f32[256,256]{1,0:T(8,128)S(1)} custom-call(bf16[256,2048]{1,0:T(8,128)(2,1)} %hidden.1, bf16[4096,256]{1,0:T(8,128)(2,1)} %weight.1), custom_call_target="tpu_custom_call" | custom-call | flops 268435456 | bytes 2097152 | tf_op jit(solution)/shard_map/projection/project/pallas_call | solution.py:95
  2.0 0.5 %collective-permute-start = (f32[256,256]{1,0:T(8,128)S(1)}, f32[256,256]{1,0:T(8,128)S(1)}, u32[]{:S(2)}, u32[]{:S(2)}) collective-permute-start(f32[256,256]{1,0:T(8,128)S(1)} %project.1.refs_0_), channel_id=1, source_target_pairs={{0,1},{1,0},{2,3},{3,2},{4,5},{5,4},{6,7},{7,6},{8,9},{9,8},{10,11... | collective-permute-start | bytes 786440 | tf_op jit(solution)/shard_map/projection/ppermute | solution.py:512
  2.6 0.0 copy-done
  2.6 0.0 copy-done.2
  2.6 1.8 %decays.1 = (bf16[256,4096]{1,0:T(8,128)(2,1)S(1)}, f32[256,64]{1,0:T(8,128)S(1)}, f32[64,256]{1,0:T(8,128)S(1)}, bf16[8,4096]{1,0:T(8,128)(2,1)S(1)}, f32[256,6...) custom-call(f32[64,256]{1,0:T(8,128)S(1)} %bitcast.3, f32[1,64]{1,0:T(1,128)S(1)} %bitcast.5, bf16[256,4096]{1,0:T(8,128)(2,1)} %x.1), custom_call_target="tpu_custom_call" | custom-call | flops 536870912 | bytes 4194304 | tf_op jit(solution)/shard_map/decays/decays/pallas_call | solution.py:159
  4.3 0.0 collective-permute-done.refs_1_
  4.4 0.5 fresh.1
  4.8 2.6 %collective-permute-start.1 = (bf16[136,512]{1,0:T(8,128)(2,1)S(1)}, bf16[136,512]{1,0:T(8,128)(2,1)S(1)}, u32[]{:S(2)}, u32[]{:S(2)}) collective-permute-start(bf16[136,512]{1,0:T(8,128)(2,1)S(1)} %get-tuple-element.57), channel_id=1, source_target_pairs={{0,2},{1,13},{2,0},{3,15},{4,6},{5,9},{6,4},{7,11},{8,10},{9,5},{1... | collective-permute-start | bytes 417800 | tf_op jit(solution)/shard_map/to_owners/ppermute | solution.py:522
  7.4 1.5 %collective-permute-start.2 = (bf16[136,512]{1,0:T(8,128)(2,1)S(1)}, bf16[136,512]{1,0:T(8,128)(2,1)S(1)}, u32[]{:S(2)}, u32[]{:S(2)}) collective-permute-start(bf16[136,512]{1,0:T(8,128)(2,1)S(1)} %get-tuple-element.58), channel_id=1, source_target_pairs={{0,4},{1,11},{2,6},{3,9},{4,0},{5,15},{6,2},{7,13},{8,12},{9,3},{1... | collective-permute-start | bytes 417800 | tf_op jit(solution)/shard_map/to_owners/ppermute | solution.py:522
  9.0 0.0 collective-permute-start.3
  9.0 2.0 %collective-permute-start.4 = (bf16[136,512]{1,0:T(8,128)(2,1)S(1)}, bf16[136,512]{1,0:T(8,128)(2,1)S(1)}, u32[]{:S(2)}, u32[]{:S(2)}) collective-permute-start(bf16[136,512]{1,0:T(8,128)(2,1)S(1)} %get-tuple-element.60), channel_id=1, source_target_pairs={{0,8},{1,7},{2,10},{3,5},{4,12},{5,3},{6,14},{7,1},{8,0},{9,15},{1... | collective-permute-start | bytes 417800 | tf_op jit(solution)/shard_map/to_owners/ppermute | solution.py:522
  11.0 1.4 %collective-permute-start.5 = (bf16[136,512]{1,0:T(8,128)(2,1)S(1)}, bf16[136,512]{1,0:T(8,128)(2,1)S(1)}, u32[]{:S(2)}, u32[]{:S(2)}) collective-permute-start(bf16[136,512]{1,0:T(8,128)(2,1)S(1)} %get-tuple-element.61), channel_id=1, source_target_pairs={{0,10},{1,5},{2,8},{3,7},{4,14},{5,1},{6,12},{7,3},{8,2},{9,13},{1... | collective-permute-start | bytes 417800 | tf_op jit(solution)/shard_map/to_owners/ppermute | solution.py:522
  12.4 0.0 collective-permute-done.1.refs_1_
  12.4 2.5 %collective-permute-start.6 = (bf16[136,512]{1,0:T(8,128)(2,1)S(1)}, bf16[136,512]{1,0:T(8,128)(2,1)S(1)}, u32[]{:S(2)}, u32[]{:S(2)}) collective-permute-start(bf16[136,512]{1,0:T(8,128)(2,1)S(1)} %get-tuple-element.62), channel_id=1, source_target_pairs={{0,12},{1,3},{2,14},{3,1},{4,8},{5,7},{6,10},{7,5},{8,4},{9,11},{1... | collective-permute-start | bytes 417800 | tf_op jit(solution)/shard_map/to_owners/ppermute | solution.py:522
  14.9 0.0 collective-permute-done.2.refs_2_
  14.9 4.6 %collective-permute-start.7 = (bf16[136,512]{1,0:T(8,128)(2,1)S(1)}, bf16[136,512]{1,0:T(8,128)(2,1)S(1)}, u32[]{:S(2)}, u32[]{:S(2)}) collective-permute-start(bf16[136,512]{1,0:T(8,128)(2,1)S(1)} %get-tuple-element.63), channel_id=1, source_target_pairs={{0,14},{1,15},{2,12},{3,13},{4,10},{5,11},{6,8},{7,9},{8,6},{9,7},... | collective-permute-start | bytes 417800 | tf_op jit(solution)/shard_map/to_owners/ppermute | solution.py:522
  19.5 5.0 %inner.2 = (f32[5,256,512]{2,1,0:T(8,128)S(1)}, f32[5,256,512]{2,1,0:T(8,128)S(1)}, f32[8,128]{1,0:T(8,128)S(1)}, bf16[8,256,512]{2,1,0:T(8,128)(2,1)S(1)}) custom-call(bf16[256,256]{1,0:T(8,128)(2,1)S(1)} %get-tuple-element.46.proj, f32[256,64]{1,0:T(8,128)S(1)} %get-tuple-element.47.cum, f32[64,256]{1,0:T(8,128)S(1)} %get-tuple-element.48.cum_rows, ...), custom_call_target="tpu_custom_call" | custom-call | flops 1342177280 | bytes 7864320 | tf_op jit(solution)/shard_map/inner/inner/pallas_call | solution.py:419
  24.6 0.0 collective-permute-done.3.refs_3_
  24.6 0.0 collective-permute-done.4.refs_4_
  24.6 0.0 collective-permute-done.5.refs_5_
  24.6 0.0 collective-permute-done.6.refs_6_
  24.6 0.0 collective-permute-done.7.refs_7_
  24.6 0.7 %total.1 = (bf16[128,512]{1,0:T(8,128)(2,1)S(1)}, f32[8,512]{1,0:T(8,128)}) custom-call(bf16[136,512]{1,0:T(8,128)(2,1)S(1)} %get-tuple-element.56.refs_0_, bf16[136,512]{1,0:T(8,128)(2,1)S(1)} %collective-permute-done.1.refs_1_, bf16[136,512]{1,0:T(8,128)(2,1)S(1)} %collective-permute-done.2.refs_2_, bf16[136,512]{1,0:T(8,128)(2,1)S(1)} %collective-permute-done.3.refs_3_, ...), custom_call_target="tpu_custom_call" | custom-call | flops 1048576 | bytes 1048576 | tf_op jit(solution)/shard_map/groups/total/pallas_call | solution.py:246
  25.3 2.6 %collective-permute-start.8 = (bf16[128,512]{1,0:T(8,128)(2,1)S(1)}, bf16[128,512]{1,0:T(8,128)(2,1)S(1)}, u32[]{:S(2)}, u32[]{:S(2)}) collective-permute-start(bf16[128,512]{1,0:T(8,128)(2,1)S(1)} %get-tuple-element.67), channel_id=1, source_target_pairs={{0,16},{2,18},{4,20},{6,22},{8,24},{10,26},{12,28},{14,30},{16,0},... | collective-permute-start | bytes 393224 | tf_op jit(solution)/shard_map/groups/ppermute | solution.py:574
  27.9 2.5 %inner.3 = (f32[3,256,512]{2,1,0:T(8,128)S(1)}, f32[3,256,512]{2,1,0:T(8,128)S(1)}, f32[8,128]{1,0:T(8,128)S(1)}) custom-call(bf16[256,256]{1,0:T(8,128)(2,1)S(1)} %get-tuple-element.46.proj, f32[256,64]{1,0:T(8,128)S(1)} %get-tuple-element.47.cum, f32[64,256]{1,0:T(8,128)S(1)} %get-tuple-element.48.cum_rows, f32[256,64]{1,0:T(8,128)S(1)} %get-tuple-element.49.step, ...), custom_call_target="tpu_custom_call" | custom-call | flops 805306368 | bytes 4718592 | tf_op jit(solution)/shard_map/inner/inner/pallas_call | solution.py:419
  30.4 0.4 local.1
  30.8 1.7 %collective-permute-done.8.before = bf16[128,512]{1,0:T(8,128)(2,1)S(1)} collective-permute-done((bf16[128,512]{1,0:T(8,128)(2,1)S(1)}, bf16[128,512]{1,0:T(8,128)(2,1)S(1)}, u32[]{:S(2)}, u32[]{:S(2)}) %collective-permute-start.8) | collective-permute-done | bytes 131104 | tf_op jit(solution)/shard_map/groups/ppermute | solution.py:574
  32.6 0.2 entering.1
  32.8 0.2 collective-permute-start.9
  33.1 1.1 %collective-permute-start.10 = (bf16[128,512]{1,0:T(8,128)(2,1)S(1)}, bf16[128,512]{1,0:T(8,128)(2,1)S(1)}, u32[]{:S(2)}, u32[]{:S(2)}) collective-permute-start(bf16[128,512]{1,0:T(8,128)(2,1)S(1)} %get-tuple-element.71), channel_id=1, source_target_pairs={{0,12},{1,3},{2,14},{3,1},{4,8},{5,7},{6,10},{7,5},{8,4},{9,11},{1... | collective-permute-start | bytes 393224 | tf_op jit(solution)/shard_map/from_owners/ppermute | solution.py:522
  34.1 0.6 %collective-permute-start.11 = (bf16[128,512]{1,0:T(8,128)(2,1)S(1)}, bf16[128,512]{1,0:T(8,128)(2,1)S(1)}, u32[]{:S(2)}, u32[]{:S(2)}) collective-permute-start(bf16[128,512]{1,0:T(8,128)(2,1)S(1)} %get-tuple-element.72), channel_id=1, source_target_pairs={{0,4},{1,11},{2,6},{3,9},{4,0},{5,15},{6,2},{7,13},{8,12},{9,3},{1... | collective-permute-start | bytes 393224 | tf_op jit(solution)/shard_map/from_owners/ppermute | solution.py:522
  34.7 3.1 %collective-permute-start.12 = (bf16[128,512]{1,0:T(8,128)(2,1)S(1)}, bf16[128,512]{1,0:T(8,128)(2,1)S(1)}, u32[]{:S(2)}, u32[]{:S(2)}) collective-permute-start(bf16[128,512]{1,0:T(8,128)(2,1)S(1)} %get-tuple-element.73), channel_id=1, source_target_pairs={{0,10},{1,5},{2,8},{3,7},{4,14},{5,1},{6,12},{7,3},{8,2},{9,13},{1... | collective-permute-start | bytes 393224 | tf_op jit(solution)/shard_map/from_owners/ppermute | solution.py:522
  37.8 0.0 collective-permute-start.13
  37.8 1.6 %collective-permute-done.9.refs_1_ = bf16[128,512]{1,0:T(8,128)(2,1)S(1)} collective-permute-done((bf16[128,512]{1,0:T(8,128)(2,1)S(1)}, bf16[128,512]{1,0:T(8,128)(2,1)S(1)}, u32[]{:S(2)}, u32[]{:S(2)}) %collective-permute-start.9) | collective-permute-done | bytes 131104 | tf_op jit(solution)/shard_map/from_owners/ppermute | solution.py:522
  39.4 0.1 collective-permute-start.14
  39.5 0.0 collective-permute-done.10.refs_2_
  39.6 2.7 %collective-permute-start.15 = (bf16[128,512]{1,0:T(8,128)(2,1)S(1)}, bf16[128,512]{1,0:T(8,128)(2,1)S(1)}, u32[]{:S(2)}, u32[]{:S(2)}) collective-permute-start(bf16[128,512]{1,0:T(8,128)(2,1)S(1)} %get-tuple-element.78), channel_id=1, source_target_pairs={{0,14},{1,15},{2,12},{3,13},{4,10},{5,11},{6,8},{7,9},{8,6},{9,7},... | collective-permute-start | bytes 393224 | tf_op jit(solution)/shard_map/from_owners/ppermute | solution.py:522
  42.2 0.0 collective-permute-done.11.refs_3_
  42.2 0.0 collective-permute-done.12.refs_4_
  42.2 0.5 %outer.3 = (f32[5,256,512]{2,1,0:T(8,128)S(1)}, f32[256,128]{1,0:T(8,128)S(1)}) custom-call(bf16[256,256]{1,0:T(8,128)(2,1)S(1)} %get-tuple-element.46.proj, f32[5,256,512]{2,1,0:T(8,128)S(1)} %get-tuple-element.54.base, f32[5,256,512]{2,1,0:T(8,128)S(1)} %get-tuple-element.55.slope, bf16[128,512]{1,0:T(8,128)(2,1)S(1)} %get-tuple-element.69.refs_0_, ...), custom_call_target="tpu_custom_call" | custom-call | flops 167772160 | bytes 7864320 | tf_op jit(solution)/shard_map/outer/outer/pallas_call | solution.py:458
  42.8 2.0 %collective-permute-done.13.refs_1_ = bf16[128,512]{1,0:T(8,128)(2,1)S(1)} collective-permute-done((bf16[128,512]{1,0:T(8,128)(2,1)S(1)}, bf16[128,512]{1,0:T(8,128)(2,1)S(1)}, u32[]{:S(2)}, u32[]{:S(2)}) %collective-permute-start.13) | collective-permute-done | bytes 131104 | tf_op jit(solution)/shard_map/from_owners/ppermute | solution.py:522
  44.7 1.0 %collective-permute-done.14.refs_2_ = bf16[128,512]{1,0:T(8,128)(2,1)S(1)} collective-permute-done((bf16[128,512]{1,0:T(8,128)(2,1)S(1)}, bf16[128,512]{1,0:T(8,128)(2,1)S(1)}, u32[]{:S(2)}, u32[]{:S(2)}) %collective-permute-start.14) | collective-permute-done | bytes 131104 | tf_op jit(solution)/shard_map/from_owners/ppermute | solution.py:522
  45.7 0.3 outer.4
  46.0 0.0 copy-start.1
  46.0 1.1 %collective-permute-done.15.refs_1_ = bf16[128,512]{1,0:T(8,128)(2,1)S(1)} collective-permute-done((bf16[128,512]{1,0:T(8,128)(2,1)S(1)}, bf16[128,512]{1,0:T(8,128)(2,1)S(1)}, u32[]{:S(2)}, u32[]{:S(2)}) %collective-permute-start.15) | collective-permute-done | bytes 131104 | tf_op jit(solution)/shard_map/from_owners/ppermute | solution.py:522
  47.1 0.2 outer.5
  47.4 0.1 collective-permute-start.16
  47.4 1.3 %collective-permute-done.16.refs_1_ = f32[256,128]{1,0:T(8,128)S(1)} collective-permute-done((f32[256,128]{1,0:T(8,128)S(1)}, f32[256,128]{1,0:T(8,128)S(1)}, u32[]{:S(2)}, u32[]{:S(2)}) %collective-permute-start.16) | collective-permute-done | bytes 131104 | tf_op jit(solution)/shard_map/norm/ppermute | solution.py:512
  48.8 0.0 copy-done.1
  48.8 1.5 %norm.1 = bf16[256,4096]{1,0:T(8,128)(2,1)} custom-call(f32[1,4096]{1,0:T(1,128)S(1)} %bitcast.4, f32[256,128]{1,0:T(8,128)S(1)} %get-tuple-element.79.refs_0_, f32[256,128]{1,0:T(8,128)S(1)} %collective-permute-done.16.refs_1_, f32[5,256,512]{2,1,0:T(8,128)S(1)} %get-tuple-element.80.refs_2_, f32[2,256,512]{2,1,0:T(8,128)S(1)} %get-tuple-element.81.refs_3_, ...), custom_call_target="tpu_custom_call" | custom-call | flops 4194304 | bytes 6291456 | tf_op jit(solution)/shard_map/norm/norm/pallas_call | solution.py:498
Async XLA Ops:
  0.0 2.6 %copy-start = (f32[256,64]{0,1:T(8,128)S(1)}, f32[256,64]{0,1:T(8,128)}, u32[]{:S(2)}) copy-start(f32[256,64]{0,1:T(8,128)} %param.11) | copy-start | bytes 196612
  0.0 2.6 %copy-start.2 = (f32[64]{0:T(128)S(1)}, f32[64]{0:T(128)}, u32[]{:S(2)}) copy-start(f32[64]{0:T(128)} %param.12) | copy-start | bytes 772
  2.0 2.3 %collective-permute-start = (f32[256,256]{1,0:T(8,128)S(1)}, f32[256,256]{1,0:T(8,128)S(1)}, u32[]{:S(2)}, u32[]{:S(2)}) collective-permute-start(f32[256,256]{1,0:T(8,128)S(1)} %project.1.refs_0_), channel_id=1, source_target_pairs={{0,1},{1,0},{2,3},{3,2},{4,5},{5,4},{6,7},{7,6},{8,9},{9,8},{10,11... | collective-permute-start | bytes 786440 | tf_op jit(solution)/shard_map/projection/ppermute | solution.py:512
  4.8 7.5 %collective-permute-start.1 = (bf16[136,512]{1,0:T(8,128)(2,1)S(1)}, bf16[136,512]{1,0:T(8,128)(2,1)S(1)}, u32[]{:S(2)}, u32[]{:S(2)}) collective-permute-start(bf16[136,512]{1,0:T(8,128)(2,1)S(1)} %get-tuple-element.57), channel_id=1, source_target_pairs={{0,2},{1,13},{2,0},{3,15},{4,6},{5,9},{6,4},{7,11},{8,10},{9,5},{1... | collective-permute-start | bytes 417800 | tf_op jit(solution)/shard_map/to_owners/ppermute | solution.py:522
  7.4 7.5 %collective-permute-start.2 = (bf16[136,512]{1,0:T(8,128)(2,1)S(1)}, bf16[136,512]{1,0:T(8,128)(2,1)S(1)}, u32[]{:S(2)}, u32[]{:S(2)}) collective-permute-start(bf16[136,512]{1,0:T(8,128)(2,1)S(1)} %get-tuple-element.58), channel_id=1, source_target_pairs={{0,4},{1,11},{2,6},{3,9},{4,0},{5,15},{6,2},{7,13},{8,12},{9,3},{1... | collective-permute-start | bytes 417800 | tf_op jit(solution)/shard_map/to_owners/ppermute | solution.py:522
  9.0 15.6 %collective-permute-start.3 = (bf16[136,512]{1,0:T(8,128)(2,1)S(1)}, bf16[136,512]{1,0:T(8,128)(2,1)S(1)}, u32[]{:S(2)}, u32[]{:S(2)}) collective-permute-start(bf16[136,512]{1,0:T(8,128)(2,1)S(1)} %get-tuple-element.59), channel_id=1, source_target_pairs={{0,6},{1,9},{2,4},{3,11},{4,2},{5,13},{6,0},{7,15},{8,14},{9,1},{1... | collective-permute-start | bytes 417800 | tf_op jit(solution)/shard_map/to_owners/ppermute | solution.py:522
  9.0 15.6 %collective-permute-start.4 = (bf16[136,512]{1,0:T(8,128)(2,1)S(1)}, bf16[136,512]{1,0:T(8,128)(2,1)S(1)}, u32[]{:S(2)}, u32[]{:S(2)}) collective-permute-start(bf16[136,512]{1,0:T(8,128)(2,1)S(1)} %get-tuple-element.60), channel_id=1, source_target_pairs={{0,8},{1,7},{2,10},{3,5},{4,12},{5,3},{6,14},{7,1},{8,0},{9,15},{1... | collective-permute-start | bytes 417800 | tf_op jit(solution)/shard_map/to_owners/ppermute | solution.py:522
  11.0 13.6 %collective-permute-start.5 = (bf16[136,512]{1,0:T(8,128)(2,1)S(1)}, bf16[136,512]{1,0:T(8,128)(2,1)S(1)}, u32[]{:S(2)}, u32[]{:S(2)}) collective-permute-start(bf16[136,512]{1,0:T(8,128)(2,1)S(1)} %get-tuple-element.61), channel_id=1, source_target_pairs={{0,10},{1,5},{2,8},{3,7},{4,14},{5,1},{6,12},{7,3},{8,2},{9,13},{1... | collective-permute-start | bytes 417800 | tf_op jit(solution)/shard_map/to_owners/ppermute | solution.py:522
  12.4 12.2 %collective-permute-start.6 = (bf16[136,512]{1,0:T(8,128)(2,1)S(1)}, bf16[136,512]{1,0:T(8,128)(2,1)S(1)}, u32[]{:S(2)}, u32[]{:S(2)}) collective-permute-start(bf16[136,512]{1,0:T(8,128)(2,1)S(1)} %get-tuple-element.62), channel_id=1, source_target_pairs={{0,12},{1,3},{2,14},{3,1},{4,8},{5,7},{6,10},{7,5},{8,4},{9,11},{1... | collective-permute-start | bytes 417800 | tf_op jit(solution)/shard_map/to_owners/ppermute | solution.py:522
  14.9 9.7 %collective-permute-start.7 = (bf16[136,512]{1,0:T(8,128)(2,1)S(1)}, bf16[136,512]{1,0:T(8,128)(2,1)S(1)}, u32[]{:S(2)}, u32[]{:S(2)}) collective-permute-start(bf16[136,512]{1,0:T(8,128)(2,1)S(1)} %get-tuple-element.63), channel_id=1, source_target_pairs={{0,14},{1,15},{2,12},{3,13},{4,10},{5,11},{6,8},{7,9},{8,6},{9,7},... | collective-permute-start | bytes 417800 | tf_op jit(solution)/shard_map/to_owners/ppermute | solution.py:522
  25.3 7.3 %collective-permute-start.8 = (bf16[128,512]{1,0:T(8,128)(2,1)S(1)}, bf16[128,512]{1,0:T(8,128)(2,1)S(1)}, u32[]{:S(2)}, u32[]{:S(2)}) collective-permute-start(bf16[128,512]{1,0:T(8,128)(2,1)S(1)} %get-tuple-element.67), channel_id=1, source_target_pairs={{0,16},{2,18},{4,20},{6,22},{8,24},{10,26},{12,28},{14,30},{16,0},... | collective-permute-start | bytes 393224 | tf_op jit(solution)/shard_map/groups/ppermute | solution.py:574
  32.8 6.6 %collective-permute-start.9 = (bf16[128,512]{1,0:T(8,128)(2,1)S(1)}, bf16[128,512]{1,0:T(8,128)(2,1)S(1)}, u32[]{:S(2)}, u32[]{:S(2)}) collective-permute-start(bf16[128,512]{1,0:T(8,128)(2,1)S(1)} %get-tuple-element.70), channel_id=1, source_target_pairs={{0,2},{1,13},{2,0},{3,15},{4,6},{5,9},{6,4},{7,11},{8,10},{9,5},{1... | collective-permute-start | bytes 393224 | tf_op jit(solution)/shard_map/from_owners/ppermute | solution.py:522
  33.1 6.5 %collective-permute-start.10 = (bf16[128,512]{1,0:T(8,128)(2,1)S(1)}, bf16[128,512]{1,0:T(8,128)(2,1)S(1)}, u32[]{:S(2)}, u32[]{:S(2)}) collective-permute-start(bf16[128,512]{1,0:T(8,128)(2,1)S(1)} %get-tuple-element.71), channel_id=1, source_target_pairs={{0,12},{1,3},{2,14},{3,1},{4,8},{5,7},{6,10},{7,5},{8,4},{9,11},{1... | collective-permute-start | bytes 393224 | tf_op jit(solution)/shard_map/from_owners/ppermute | solution.py:522
  34.1 8.1 %collective-permute-start.11 = (bf16[128,512]{1,0:T(8,128)(2,1)S(1)}, bf16[128,512]{1,0:T(8,128)(2,1)S(1)}, u32[]{:S(2)}, u32[]{:S(2)}) collective-permute-start(bf16[128,512]{1,0:T(8,128)(2,1)S(1)} %get-tuple-element.72), channel_id=1, source_target_pairs={{0,4},{1,11},{2,6},{3,9},{4,0},{5,15},{6,2},{7,13},{8,12},{9,3},{1... | collective-permute-start | bytes 393224 | tf_op jit(solution)/shard_map/from_owners/ppermute | solution.py:522
  34.7 7.5 %collective-permute-start.12 = (bf16[128,512]{1,0:T(8,128)(2,1)S(1)}, bf16[128,512]{1,0:T(8,128)(2,1)S(1)}, u32[]{:S(2)}, u32[]{:S(2)}) collective-permute-start(bf16[128,512]{1,0:T(8,128)(2,1)S(1)} %get-tuple-element.73), channel_id=1, source_target_pairs={{0,10},{1,5},{2,8},{3,7},{4,14},{5,1},{6,12},{7,3},{8,2},{9,13},{1... | collective-permute-start | bytes 393224 | tf_op jit(solution)/shard_map/from_owners/ppermute | solution.py:522
  37.8 6.9 %collective-permute-start.13 = (bf16[128,512]{1,0:T(8,128)(2,1)S(1)}, bf16[128,512]{1,0:T(8,128)(2,1)S(1)}, u32[]{:S(2)}, u32[]{:S(2)}) collective-permute-start(bf16[128,512]{1,0:T(8,128)(2,1)S(1)} %get-tuple-element.75), channel_id=1, source_target_pairs={{0,8},{1,7},{2,10},{3,5},{4,12},{5,3},{6,14},{7,1},{8,0},{9,15},{1... | collective-permute-start | bytes 393224 | tf_op jit(solution)/shard_map/from_owners/ppermute | solution.py:522
  39.4 6.3 %collective-permute-start.14 = (bf16[128,512]{1,0:T(8,128)(2,1)S(1)}, bf16[128,512]{1,0:T(8,128)(2,1)S(1)}, u32[]{:S(2)}, u32[]{:S(2)}) collective-permute-start(bf16[128,512]{1,0:T(8,128)(2,1)S(1)} %get-tuple-element.76), channel_id=1, source_target_pairs={{0,6},{1,9},{2,4},{3,11},{4,2},{5,13},{6,0},{7,15},{8,14},{9,1},{1... | collective-permute-start | bytes 393224 | tf_op jit(solution)/shard_map/from_owners/ppermute | solution.py:522
  39.6 7.6 %collective-permute-start.15 = (bf16[128,512]{1,0:T(8,128)(2,1)S(1)}, bf16[128,512]{1,0:T(8,128)(2,1)S(1)}, u32[]{:S(2)}, u32[]{:S(2)}) collective-permute-start(bf16[128,512]{1,0:T(8,128)(2,1)S(1)} %get-tuple-element.78), channel_id=1, source_target_pairs={{0,14},{1,15},{2,12},{3,13},{4,10},{5,11},{6,8},{7,9},{8,6},{9,7},... | collective-permute-start | bytes 393224 | tf_op jit(solution)/shard_map/from_owners/ppermute | solution.py:522
  46.0 2.7 %copy-start.1 = (f32[4096]{0:T(1024)S(1)}, f32[4096]{0:T(1024)}, u32[]{:S(2)}) copy-start(f32[4096]{0:T(1024)} %param.13) | copy-start | bytes 49156
  47.4 1.4 %collective-permute-start.16 = (f32[256,128]{1,0:T(8,128)S(1)}, f32[256,128]{1,0:T(8,128)S(1)}, u32[]{:S(2)}, u32[]{:S(2)}) collective-permute-start(f32[256,128]{1,0:T(8,128)S(1)} %get-tuple-element.79.refs_0_), channel_id=1, source_target_pairs={{0,1},{1,0},{2,3},{3,2},{4,5},{5,4},{6,7},{7,6},{8,9},{9,8},{10,11... | collective-permute-start | bytes 393224 | tf_op jit(solution)/shard_map/norm/ppermute | solution.py:512

commit v6 on v5

--- a/solution.py
+++ b/solution.py
@@ -14,7 +14,7 @@
 EXTRA = 8
 LIMIT = 16 * 1024 * 1024
 SEND_ORDER = (0, 1, 2, 3, 4, 5, 6, 7)
-BACK_ORDER = (0, 1, 6, 2, 5, 4, 3, 7)
+BACK_ORDER = (0, 1, 6, 2, 5, 3, 4, 7)
 LOG2E = 1.4426950408889634
 
 F32 = jnp.float32
@@ -33,6 +33,11 @@
 
 def cost(flops, moved, exps=0):
     return pl.CostEstimate(flops=flops, bytes_accessed=moved, transcendentals=exps)
+
+
+def message(width):
+    groups = width // STATE
+    return groups * STATE, groups * STATE + -(-2 * groups // 8) * 8
 
 
 def turns(order, size):
@@ -191,8 +196,16 @@
         state = lax.dot_general(
             b_rows, weighted[:, cols], (((0,), (0,)), ((), ())), preferred_element_type=F32
         )
-        slices[m][:STATE, :] = state.astype(BF16)
-        slices[m][STATE:, :] = ends[:, cols]
+        end = ends[:, cols].astype(F32)
+        body, whole = message(width)
+        tail = []
+        for g in range(width // STATE):
+            lanes = slice(g * STATE, (g + 1) * STATE)
+            slices[m][lanes, :] = state[:, lanes].astype(BF16)
+            tail.append(end[:2, lanes])
+        tail.append(jnp.zeros((whole - body - 2 * len(tail), STATE), F32))
+        tail = [part for part in tail if part.shape[0]]
+        slices[m][body:, :] = jnp.concatenate(tail, axis=0).astype(BF16)
 
 
 def fresh_states(order, parts, weighted, ends):
@@ -205,7 +218,7 @@
         in_specs=[VMEM] * (n + 2),
         out_specs=[VMEM] * (1 + size),
         out_shape=[jax.ShapeDtypeStruct((rows, 2 * STATE), BF16)]
-        + [jax.ShapeDtypeStruct((STATE + EXTRA, width), BF16)] * size,
+        + [jax.ShapeDtypeStruct((message(width)[1], STATE), BF16)] * size,
         compiler_params=params(),
         cost_estimate=cost(2 * rows * cols * STATE, 4 * rows * cols),
         name="fresh",
@@ -215,8 +228,12 @@
 def gather_factors(order, slices, factors):
     place = position(len(order))
     for pair, piece in zip(order, slices):
-        tail = piece[STATE:, :].astype(F32)
-        factors[place ^ partner(pair)] = jnp.broadcast_to(tail[0:1] + (tail[1:2] + tail[2:3]), factors.shape[1:])
+        width = factors.shape[2]
+        tail = piece[message(width)[0] :, :].astype(F32)
+        terms = [tail[2 * g : 2 * g + 1] + tail[2 * g + 1 : 2 * g + 2] for g in range(width // STATE)]
+        factors[place ^ partner(pair)] = jnp.broadcast_to(
+            jnp.concatenate(terms, axis=1), factors.shape[1:]
+        )
 
 
 def total_kernel(order, *refs):
@@ -231,18 +248,24 @@
         product = product * factor
     decay[...] = product
     scales = [factors[place ^ partner(pair)][:1] for pair in order]
-    step = 16
-    for row in range(0, STATE, step):
-        rows = slice(row, row + step)
-        total = jnp.zeros((step, out.shape[1]), F32)
-        for scale, piece in zip(scales, slices):
-            total = total + scale * piece[rows, :].astype(F32)
-        out[rows, :] = total.astype(BF16)
+    step = 64
+    for g in range(out.shape[1] // STATE):
+        lanes = slice(g * STATE, (g + 1) * STATE)
+        for row in range(0, STATE, step):
+            total = jnp.zeros((step, STATE), F32)
+            for scale, piece in zip(scales, slices):
+                rows = slice(g * STATE + row, g * STATE + row + step)
+                total = total + scale[:, lanes] * piece[rows, :].astype(F32)
+            out[row : row + step, lanes] = total.astype(BF16)
+
+
+def lanes_of(piece):
+    return piece.shape[0] // STATE * STATE
 
 
 def group_total(order, slices, token):
     size = len(slices)
-    width = slices[0].shape[1]
+    width = lanes_of(slices[0])
     return pl.pallas_call(
         functools.partial(total_kernel, order),
         in_specs=[VMEM] * (size + 1),
@@ -264,7 +287,7 @@
     size = len(slices)
     gather_factors(order, slices, factors)
     for pair, piece in zip(order, slices):
-        ordered[place ^ partner(pair)] = piece[:STATE, :]
+        ordered[place ^ partner(pair)] = piece[: ordered.shape[1], :]
     running = jnp.zeros(states.shape[1:], F32)
     product = jnp.ones(factors.shape[1:], F32)
     for j in range(size):
@@ -273,13 +296,17 @@
             at = jnp.where(place ^ j == partner(pair), i, at)
         states[at] = running
         scales[at] = product
-        running = running * factors[j][:1] + ordered[j].astype(F32)
+        fresh = [
+            ordered[j, g * STATE : (g + 1) * STATE, :].astype(F32)
+            for g in range(running.shape[1] // STATE)
+        ]
+        running = running * factors[j][:1] + jnp.concatenate(fresh, axis=1)
         product = product * factors[j]
 
 
 def local_states(order, back_order, slices):
     size = len(slices)
-    width = slices[0].shape[1]
+    width = lanes_of(slices[0])
     return pl.pallas_call(
         functools.partial(local_kernel, order, back_order),
         in_specs=[VMEM] * size,
@@ -289,7 +316,7 @@
             jax.ShapeDtypeStruct((size, 8, width), F32),
         ],
         scratch_shapes=[
-            pltpu.VMEM((size, STATE, width), BF16),
+            pltpu.VMEM((size, width, STATE), BF16),
             pltpu.VMEM((size, 8, width), F32),
         ],
         compiler_params=params(),

time: 50.5 us -> 50 us (0.990)
  transfers between devices with their start and end apart: 17 -> 17, of which waited for: 6 -> 5; matrix products, arithmetic and copies ran while one was open for 0% -> 0% of each run, Pallas kernels for 21% -> 21%
where the time goes in v6:
time: 50 us; the launch traced here: 49.9 us
  starting transfers between devices  25.6 us (51%)
  Pallas kernels  15.8 us (32%)
  waiting for transfers between devices  8.36 us (17%)
    ppermute x14, starting transfers between devices, exchange(): return lax.ppermute(value, ('seq', 'head'), pairs)  22.4 us
    pallas_call x2, Pallas kernels, inside(): pl.pallas_call(functools.partial(inner_kernel, size, order if first else...  7.57 us
    ppermute x14, waiting for transfers between devices, exchange(): return lax.ppermute(value, ('seq', 'head'), pairs)  5.25 us
    ppermute x1, starting transfers between devices, shards(): before = lax.ppermute(sent, 'seq', up)  2.59 us
    pallas_call x1, Pallas kernels, project(): pl.pallas_call(functools.partial(project_kernel, tiles), in_specs=[pl.Blo...  2.02 us
    pallas_call x1, Pallas kernels, decays(): pl.pallas_call(functools.partial(decay_kernel, tiles), in_specs=[VMEM, VM...  1.78 us
    ppermute x1, waiting for transfers between devices, shards(): before = lax.ppermute(sent, 'seq', up)  1.77 us
    pallas_call x1, Pallas kernels, normalise(): pl.pallas_call(functools.partial(norm_kernel, count, order, n, k), in_spe...  1.54 us
  transfers between devices with their start and end apart: 17, of which 5 were waited for; matrix products, arithmetic and copies ran while one was open for 0% of the time, Pallas kernels for 21%

profile of v6, /device:TPU:0, one launch (start us, length us, event | category | flops | bytes accessed | tf_op | source)
XLA Modules:
  0.0 49.9 jit_solution(15588544753453285963)
XLA Ops:
  0.0 0.0 copy-start
  0.0 0.0 copy-start.2
  0.0 2.0 %project.1.refs_0_ = f32[256,256]{1,0:T(8,128)S(1)} custom-call(bf16[256,2048]{1,0:T(8,128)(2,1)} %hidden.1, bf16[4096,256]{1,0:T(8,128)(2,1)} %weight.1), custom_call_target="tpu_custom_call" | custom-call | flops 268435456 | bytes 2097152 | tf_op jit(solution)/shard_map/projection/project/pallas_call | solution.py:100
  2.0 0.5 %collective-permute-start = (f32[256,256]{1,0:T(8,128)S(1)}, f32[256,256]{1,0:T(8,128)S(1)}, u32[]{:S(2)}, u32[]{:S(2)}) collective-permute-start(f32[256,256]{1,0:T(8,128)S(1)} %project.1.refs_0_), channel_id=1, source_target_pairs={{0,1},{1,0},{2,3},{3,2},{4,5},{5,4},{6,7},{7,6},{8,9},{9,8},{10,11... | collective-permute-start | bytes 786440 | tf_op jit(solution)/shard_map/projection/ppermute | solution.py:539
  2.6 0.0 copy-done
  2.6 0.0 copy-done.2
  2.6 1.8 %decays.1 = (bf16[256,4096]{1,0:T(8,128)(2,1)S(1)}, f32[256,64]{1,0:T(8,128)S(1)}, f32[64,256]{1,0:T(8,128)S(1)}, bf16[8,4096]{1,0:T(8,128)(2,1)S(1)}, f32[256,6...) custom-call(f32[64,256]{1,0:T(8,128)S(1)} %bitcast.3, f32[1,64]{1,0:T(1,128)S(1)} %bitcast.5, bf16[256,4096]{1,0:T(8,128)(2,1)} %x.1), custom_call_target="tpu_custom_call" | custom-call | flops 536870912 | bytes 4194304 | tf_op jit(solution)/shard_map/decays/decays/pallas_call | solution.py:164
  4.3 0.0 collective-permute-done.refs_1_
  4.4 0.5 fresh.1
  4.8 2.6 %collective-permute-start.1 = (bf16[520,128]{1,0:T(8,128)(2,1)S(1)}, bf16[520,128]{1,0:T(8,128)(2,1)S(1)}, u32[]{:S(2)}, u32[]{:S(2)}) collective-permute-start(bf16[520,128]{1,0:T(8,128)(2,1)S(1)} %get-tuple-element.57), channel_id=1, source_target_pairs={{0,2},{1,13},{2,0},{3,15},{4,6},{5,9},{6,4},{7,11},{8,10},{9,5},{1... | collective-permute-start | bytes 399368 | tf_op jit(solution)/shard_map/to_owners/ppermute | solution.py:549
  7.4 1.5 %collective-permute-start.2 = (bf16[520,128]{1,0:T(8,128)(2,1)S(1)}, bf16[520,128]{1,0:T(8,128)(2,1)S(1)}, u32[]{:S(2)}, u32[]{:S(2)}) collective-permute-start(bf16[520,128]{1,0:T(8,128)(2,1)S(1)} %get-tuple-element.58), channel_id=1, source_target_pairs={{0,4},{1,11},{2,6},{3,9},{4,0},{5,15},{6,2},{7,13},{8,12},{9,3},{1... | collective-permute-start | bytes 399368 | tf_op jit(solution)/shard_map/to_owners/ppermute | solution.py:549
  8.9 0.0 collective-permute-start.3
  9.0 2.0 %collective-permute-start.4 = (bf16[520,128]{1,0:T(8,128)(2,1)S(1)}, bf16[520,128]{1,0:T(8,128)(2,1)S(1)}, u32[]{:S(2)}, u32[]{:S(2)}) collective-permute-start(bf16[520,128]{1,0:T(8,128)(2,1)S(1)} %get-tuple-element.60), channel_id=1, source_target_pairs={{0,8},{1,7},{2,10},{3,5},{4,12},{5,3},{6,14},{7,1},{8,0},{9,15},{1... | collective-permute-start | bytes 399368 | tf_op jit(solution)/shard_map/to_owners/ppermute | solution.py:549
  11.0 1.4 %collective-permute-start.5 = (bf16[520,128]{1,0:T(8,128)(2,1)S(1)}, bf16[520,128]{1,0:T(8,128)(2,1)S(1)}, u32[]{:S(2)}, u32[]{:S(2)}) collective-permute-start(bf16[520,128]{1,0:T(8,128)(2,1)S(1)} %get-tuple-element.61), channel_id=1, source_target_pairs={{0,10},{1,5},{2,8},{3,7},{4,14},{5,1},{6,12},{7,3},{8,2},{9,13},{1... | collective-permute-start | bytes 399368 | tf_op jit(solution)/shard_map/to_owners/ppermute | solution.py:549
  12.4 0.0 collective-permute-done.1.refs_1_
  12.4 2.5 %collective-permute-start.6 = (bf16[520,128]{1,0:T(8,128)(2,1)S(1)}, bf16[520,128]{1,0:T(8,128)(2,1)S(1)}, u32[]{:S(2)}, u32[]{:S(2)}) collective-permute-start(bf16[520,128]{1,0:T(8,128)(2,1)S(1)} %get-tuple-element.62), channel_id=1, source_target_pairs={{0,12},{1,3},{2,14},{3,1},{4,8},{5,7},{6,10},{7,5},{8,4},{9,11},{1... | collective-permute-start | bytes 399368 | tf_op jit(solution)/shard_map/to_owners/ppermute | solution.py:549
  14.9 0.0 collective-permute-done.2.refs_2_
  14.9 4.2 %collective-permute-start.7 = (bf16[520,128]{1,0:T(8,128)(2,1)S(1)}, bf16[520,128]{1,0:T(8,128)(2,1)S(1)}, u32[]{:S(2)}, u32[]{:S(2)}) collective-permute-start(bf16[520,128]{1,0:T(8,128)(2,1)S(1)} %get-tuple-element.63), channel_id=1, source_target_pairs={{0,14},{1,15},{2,12},{3,13},{4,10},{5,11},{6,8},{7,9},{8,6},{9,7},... | collective-permute-start | bytes 399368 | tf_op jit(solution)/shard_map/to_owners/ppermute | solution.py:549
  19.1 5.0 %inner.2 = (f32[5,256,512]{2,1,0:T(8,128)S(1)}, f32[5,256,512]{2,1,0:T(8,128)S(1)}, f32[8,128]{1,0:T(8,128)S(1)}, bf16[8,256,512]{2,1,0:T(8,128)(2,1)S(1)}) custom-call(bf16[256,256]{1,0:T(8,128)(2,1)S(1)} %get-tuple-element.46.proj, f32[256,64]{1,0:T(8,128)S(1)} %get-tuple-element.47.cum, f32[64,256]{1,0:T(8,128)S(1)} %get-tuple-element.48.cum_rows, ...), custom_call_target="tpu_custom_call" | custom-call | flops 1342177280 | bytes 7864320 | tf_op jit(solution)/shard_map/inner/inner/pallas_call | solution.py:446
  24.2 0.0 collective-permute-done.3.refs_3_
  24.2 0.0 collective-permute-done.4.refs_4_
  24.2 0.0 collective-permute-done.5.refs_5_
  24.2 0.0 collective-permute-done.6.refs_6_
  24.2 0.0 collective-permute-done.7.refs_7_
  24.2 0.7 %total.1 = (bf16[128,512]{1,0:T(8,128)(2,1)S(1)}, f32[8,512]{1,0:T(8,128)}) custom-call(bf16[520,128]{1,0:T(8,128)(2,1)S(1)} %get-tuple-element.56.refs_0_, bf16[520,128]{1,0:T(8,128)(2,1)S(1)} %collective-permute-done.1.refs_1_, bf16[520,128]{1,0:T(8,128)(2,1)S(1)} %collective-permute-done.2.refs_2_, bf16[520,128]{1,0:T(8,128)(2,1)S(1)} %collective-permute-done.3.refs_3_, ...), custom_call_target="tpu_custom_call" | custom-call | flops 1048576 | bytes 1048576 | tf_op jit(solution)/shard_map/groups/total/pallas_call | solution.py:269
  24.9 2.6 %collective-permute-start.8 = (bf16[128,512]{1,0:T(8,128)(2,1)S(1)}, bf16[128,512]{1,0:T(8,128)(2,1)S(1)}, u32[]{:S(2)}, u32[]{:S(2)}) collective-permute-start(bf16[128,512]{1,0:T(8,128)(2,1)S(1)} %get-tuple-element.67), channel_id=1, source_target_pairs={{0,16},{2,18},{4,20},{6,22},{8,24},{10,26},{12,28},{14,30},{16,0},... | collective-permute-start | bytes 393224 | tf_op jit(solution)/shard_map/groups/ppermute | solution.py:601
  27.5 2.5 %inner.3 = (f32[3,256,512]{2,1,0:T(8,128)S(1)}, f32[3,256,512]{2,1,0:T(8,128)S(1)}, f32[8,128]{1,0:T(8,128)S(1)}) custom-call(bf16[256,256]{1,0:T(8,128)(2,1)S(1)} %get-tuple-element.46.proj, f32[256,64]{1,0:T(8,128)S(1)} %get-tuple-element.47.cum, f32[64,256]{1,0:T(8,128)S(1)} %get-tuple-element.48.cum_rows, f32[256,64]{1,0:T(8,128)S(1)} %get-tuple-element.49.step, ...), custom_call_target="tpu_custom_call" | custom-call | flops 805306368 | bytes 4718592 | tf_op jit(solution)/shard_map/inner/inner/pallas_call | solution.py:446
  30.0 0.5 local.1
  30.5 1.8 %collective-permute-done.8.before = bf16[128,512]{1,0:T(8,128)(2,1)S(1)} collective-permute-done((bf16[128,512]{1,0:T(8,128)(2,1)S(1)}, bf16[128,512]{1,0:T(8,128)(2,1)S(1)}, u32[]{:S(2)}, u32[]{:S(2)}) %collective-permute-start.8) | collective-permute-done | bytes 131104 | tf_op jit(solution)/shard_map/groups/ppermute | solution.py:601
  32.3 0.2 entering.1
  32.5 0.1 collective-permute-start.9
  32.6 0.8 %collective-permute-start.10 = (bf16[128,512]{1,0:T(8,128)(2,1)S(1)}, bf16[128,512]{1,0:T(8,128)(2,1)S(1)}, u32[]{:S(2)}, u32[]{:S(2)}) collective-permute-start(bf16[128,512]{1,0:T(8,128)(2,1)S(1)} %get-tuple-element.71), channel_id=1, source_target_pairs={{0,12},{1,3},{2,14},{3,1},{4,8},{5,7},{6,10},{7,5},{8,4},{9,11},{1... | collective-permute-start | bytes 393224 | tf_op jit(solution)/shard_map/from_owners/ppermute | solution.py:549
  33.5 0.8 %collective-permute-start.11 = (bf16[128,512]{1,0:T(8,128)(2,1)S(1)}, bf16[128,512]{1,0:T(8,128)(2,1)S(1)}, u32[]{:S(2)}, u32[]{:S(2)}) collective-permute-start(bf16[128,512]{1,0:T(8,128)(2,1)S(1)} %get-tuple-element.72), channel_id=1, source_target_pairs={{0,4},{1,11},{2,6},{3,9},{4,0},{5,15},{6,2},{7,13},{8,12},{9,3},{1... | collective-permute-start | bytes 393224 | tf_op jit(solution)/shard_map/from_owners/ppermute | solution.py:549
  34.3 3.3 %collective-permute-start.12 = (bf16[128,512]{1,0:T(8,128)(2,1)S(1)}, bf16[128,512]{1,0:T(8,128)(2,1)S(1)}, u32[]{:S(2)}, u32[]{:S(2)}) collective-permute-start(bf16[128,512]{1,0:T(8,128)(2,1)S(1)} %get-tuple-element.73), channel_id=1, source_target_pairs={{0,10},{1,5},{2,8},{3,7},{4,14},{5,1},{6,12},{7,3},{8,2},{9,13},{1... | collective-permute-start | bytes 393224 | tf_op jit(solution)/shard_map/from_owners/ppermute | solution.py:549
  37.5 1.1 %collective-permute-start.13 = (bf16[128,512]{1,0:T(8,128)(2,1)S(1)}, bf16[128,512]{1,0:T(8,128)(2,1)S(1)}, u32[]{:S(2)}, u32[]{:S(2)}) collective-permute-start(bf16[128,512]{1,0:T(8,128)(2,1)S(1)} %get-tuple-element.75), channel_id=1, source_target_pairs={{0,6},{1,9},{2,4},{3,11},{4,2},{5,13},{6,0},{7,15},{8,14},{9,1},{1... | collective-permute-start | bytes 393224 | tf_op jit(solution)/shard_map/from_owners/ppermute | solution.py:549
  38.6 0.0 collective-permute-done.9.refs_1_
  38.6 0.0 collective-permute-start.14
  38.6 1.3 %collective-permute-done.10.refs_2_ = bf16[128,512]{1,0:T(8,128)(2,1)S(1)} collective-permute-done((bf16[128,512]{1,0:T(8,128)(2,1)S(1)}, bf16[128,512]{1,0:T(8,128)(2,1)S(1)}, u32[]{:S(2)}, u32[]{:S(2)}) %collective-permute-start.10) | collective-permute-done | bytes 131104 | tf_op jit(solution)/shard_map/from_owners/ppermute | solution.py:549
  39.9 2.0 %collective-permute-start.15 = (bf16[128,512]{1,0:T(8,128)(2,1)S(1)}, bf16[128,512]{1,0:T(8,128)(2,1)S(1)}, u32[]{:S(2)}, u32[]{:S(2)}) collective-permute-start(bf16[128,512]{1,0:T(8,128)(2,1)S(1)} %get-tuple-element.78), channel_id=1, source_target_pairs={{0,14},{1,15},{2,12},{3,13},{4,10},{5,11},{6,8},{7,9},{8,6},{9,7},... | collective-permute-start | bytes 393224 | tf_op jit(solution)/shard_map/from_owners/ppermute | solution.py:549
  41.9 0.0 collective-permute-done.11.refs_3_
  41.9 0.0 collective-permute-done.12.refs_4_
  41.9 0.5 %outer.3 = (f32[5,256,512]{2,1,0:T(8,128)S(1)}, f32[256,128]{1,0:T(8,128)S(1)}) custom-call(bf16[256,256]{1,0:T(8,128)(2,1)S(1)} %get-tuple-element.46.proj, f32[5,256,512]{2,1,0:T(8,128)S(1)} %get-tuple-element.54.base, f32[5,256,512]{2,1,0:T(8,128)S(1)} %get-tuple-element.55.slope, bf16[128,512]{1,0:T(8,128)(2,1)S(1)} %get-tuple-element.69.refs_0_, ...), custom_call_target="tpu_custom_call" | custom-call | flops 167772160 | bytes 7864320 | tf_op jit(solution)/shard_map/outer/outer/pallas_call | solution.py:485
  42.4 2.1 %collective-permute-done.13.refs_1_ = bf16[128,512]{1,0:T(8,128)(2,1)S(1)} collective-permute-done((bf16[128,512]{1,0:T(8,128)(2,1)S(1)}, bf16[128,512]{1,0:T(8,128)(2,1)S(1)}, u32[]{:S(2)}, u32[]{:S(2)}) %collective-permute-start.13) | collective-permute-done | bytes 131104 | tf_op jit(solution)/shard_map/from_owners/ppermute | solution.py:549
  44.5 0.0 collective-permute-done.14.refs_2_
  44.5 0.3 outer.4
  44.8 0.0 copy-start.1
  44.8 1.9 %collective-permute-done.15.refs_1_ = bf16[128,512]{1,0:T(8,128)(2,1)S(1)} collective-permute-done((bf16[128,512]{1,0:T(8,128)(2,1)S(1)}, bf16[128,512]{1,0:T(8,128)(2,1)S(1)}, u32[]{:S(2)}, u32[]{:S(2)}) %collective-permute-start.15) | collective-permute-done | bytes 131104 | tf_op jit(solution)/shard_map/from_owners/ppermute | solution.py:549
  46.7 0.2 outer.5
  46.9 0.1 collective-permute-start.16
  47.0 1.3 %collective-permute-done.16.refs_1_ = f32[256,128]{1,0:T(8,128)S(1)} collective-permute-done((f32[256,128]{1,0:T(8,128)S(1)}, f32[256,128]{1,0:T(8,128)S(1)}, u32[]{:S(2)}, u32[]{:S(2)}) %collective-permute-start.16) | collective-permute-done | bytes 131104 | tf_op jit(solution)/shard_map/norm/ppermute | solution.py:539
  48.3 0.0 copy-done.1
  48.3 1.5 %norm.1 = bf16[256,4096]{1,0:T(8,128)(2,1)} custom-call(f32[1,4096]{1,0:T(1,128)S(1)} %bitcast.4, f32[256,128]{1,0:T(8,128)S(1)} %get-tuple-element.79.refs_0_, f32[256,128]{1,0:T(8,128)S(1)} %collective-permute-done.16.refs_1_, f32[5,256,512]{2,1,0:T(8,128)S(1)} %get-tuple-element.80.refs_2_, f32[2,256,512]{2,1,0:T(8,128)S(1)} %get-tuple-element.81.refs_3_, ...), custom_call_target="tpu_custom_call" | custom-call | flops 4194304 | bytes 6291456 | tf_op jit(solution)/shard_map/norm/norm/pallas_call | solution.py:525
Async XLA Ops:
  0.0 2.6 %copy-start = (f32[256,64]{0,1:T(8,128)S(1)}, f32[256,64]{0,1:T(8,128)}, u32[]{:S(2)}) copy-start(f32[256,64]{0,1:T(8,128)} %param.11) | copy-start | bytes 196612
  0.0 2.6 %copy-start.2 = (f32[64]{0:T(128)S(1)}, f32[64]{0:T(128)}, u32[]{:S(2)}) copy-start(f32[64]{0:T(128)} %param.12) | copy-start | bytes 772
  2.0 2.3 %collective-permute-start = (f32[256,256]{1,0:T(8,128)S(1)}, f32[256,256]{1,0:T(8,128)S(1)}, u32[]{:S(2)}, u32[]{:S(2)}) collective-permute-start(f32[256,256]{1,0:T(8,128)S(1)} %project.1.refs_0_), channel_id=1, source_target_pairs={{0,1},{1,0},{2,3},{3,2},{4,5},{5,4},{6,7},{7,6},{8,9},{9,8},{10,11... | collective-permute-start | bytes 786440 | tf_op jit(solution)/shard_map/projection/ppermute | solution.py:539
  4.8 7.5 %collective-permute-start.1 = (bf16[520,128]{1,0:T(8,128)(2,1)S(1)}, bf16[520,128]{1,0:T(8,128)(2,1)S(1)}, u32[]{:S(2)}, u32[]{:S(2)}) collective-permute-start(bf16[520,128]{1,0:T(8,128)(2,1)S(1)} %get-tuple-element.57), channel_id=1, source_target_pairs={{0,2},{1,13},{2,0},{3,15},{4,6},{5,9},{6,4},{7,11},{8,10},{9,5},{1... | collective-permute-start | bytes 399368 | tf_op jit(solution)/shard_map/to_owners/ppermute | solution.py:549
  7.4 7.5 %collective-permute-start.2 = (bf16[520,128]{1,0:T(8,128)(2,1)S(1)}, bf16[520,128]{1,0:T(8,128)(2,1)S(1)}, u32[]{:S(2)}, u32[]{:S(2)}) collective-permute-start(bf16[520,128]{1,0:T(8,128)(2,1)S(1)} %get-tuple-element.58), channel_id=1, source_target_pairs={{0,4},{1,11},{2,6},{3,9},{4,0},{5,15},{6,2},{7,13},{8,12},{9,3},{1... | collective-permute-start | bytes 399368 | tf_op jit(solution)/shard_map/to_owners/ppermute | solution.py:549
  8.9 15.2 %collective-permute-start.3 = (bf16[520,128]{1,0:T(8,128)(2,1)S(1)}, bf16[520,128]{1,0:T(8,128)(2,1)S(1)}, u32[]{:S(2)}, u32[]{:S(2)}) collective-permute-start(bf16[520,128]{1,0:T(8,128)(2,1)S(1)} %get-tuple-element.59), channel_id=1, source_target_pairs={{0,6},{1,9},{2,4},{3,11},{4,2},{5,13},{6,0},{7,15},{8,14},{9,1},{1... | collective-permute-start | bytes 399368 | tf_op jit(solution)/shard_map/to_owners/ppermute | solution.py:549
  9.0 15.2 %collective-permute-start.4 = (bf16[520,128]{1,0:T(8,128)(2,1)S(1)}, bf16[520,128]{1,0:T(8,128)(2,1)S(1)}, u32[]{:S(2)}, u32[]{:S(2)}) collective-permute-start(bf16[520,128]{1,0:T(8,128)(2,1)S(1)} %get-tuple-element.60), channel_id=1, source_target_pairs={{0,8},{1,7},{2,10},{3,5},{4,12},{5,3},{6,14},{7,1},{8,0},{9,15},{1... | collective-permute-start | bytes 399368 | tf_op jit(solution)/shard_map/to_owners/ppermute | solution.py:549
  11.0 13.2 %collective-permute-start.5 = (bf16[520,128]{1,0:T(8,128)(2,1)S(1)}, bf16[520,128]{1,0:T(8,128)(2,1)S(1)}, u32[]{:S(2)}, u32[]{:S(2)}) collective-permute-start(bf16[520,128]{1,0:T(8,128)(2,1)S(1)} %get-tuple-element.61), channel_id=1, source_target_pairs={{0,10},{1,5},{2,8},{3,7},{4,14},{5,1},{6,12},{7,3},{8,2},{9,13},{1... | collective-permute-start | bytes 399368 | tf_op jit(solution)/shard_map/to_owners/ppermute | solution.py:549
  12.4 11.8 %collective-permute-start.6 = (bf16[520,128]{1,0:T(8,128)(2,1)S(1)}, bf16[520,128]{1,0:T(8,128)(2,1)S(1)}, u32[]{:S(2)}, u32[]{:S(2)}) collective-permute-start(bf16[520,128]{1,0:T(8,128)(2,1)S(1)} %get-tuple-element.62), channel_id=1, source_target_pairs={{0,12},{1,3},{2,14},{3,1},{4,8},{5,7},{6,10},{7,5},{8,4},{9,11},{1... | collective-permute-start | bytes 399368 | tf_op jit(solution)/shard_map/to_owners/ppermute | solution.py:549
  14.9 9.3 %collective-permute-start.7 = (bf16[520,128]{1,0:T(8,128)(2,1)S(1)}, bf16[520,128]{1,0:T(8,128)(2,1)S(1)}, u32[]{:S(2)}, u32[]{:S(2)}) collective-permute-start(bf16[520,128]{1,0:T(8,128)(2,1)S(1)} %get-tuple-element.63), channel_id=1, source_target_pairs={{0,14},{1,15},{2,12},{3,13},{4,10},{5,11},{6,8},{7,9},{8,6},{9,7},... | collective-permute-start | bytes 399368 | tf_op jit(solution)/shard_map/to_owners/ppermute | solution.py:549
  24.9 7.4 %collective-permute-start.8 = (bf16[128,512]{1,0:T(8,128)(2,1)S(1)}, bf16[128,512]{1,0:T(8,128)(2,1)S(1)}, u32[]{:S(2)}, u32[]{:S(2)}) collective-permute-start(bf16[128,512]{1,0:T(8,128)(2,1)S(1)} %get-tuple-element.67), channel_id=1, source_target_pairs={{0,16},{2,18},{4,20},{6,22},{8,24},{10,26},{12,28},{14,30},{16,0},... | collective-permute-start | bytes 393224 | tf_op jit(solution)/shard_map/groups/ppermute | solution.py:601
  32.5 6.1 %collective-permute-start.9 = (bf16[128,512]{1,0:T(8,128)(2,1)S(1)}, bf16[128,512]{1,0:T(8,128)(2,1)S(1)}, u32[]{:S(2)}, u32[]{:S(2)}) collective-permute-start(bf16[128,512]{1,0:T(8,128)(2,1)S(1)} %get-tuple-element.70), channel_id=1, source_target_pairs={{0,2},{1,13},{2,0},{3,15},{4,6},{5,9},{6,4},{7,11},{8,10},{9,5},{1... | collective-permute-start | bytes 393224 | tf_op jit(solution)/shard_map/from_owners/ppermute | solution.py:549
  32.6 7.3 %collective-permute-start.10 = (bf16[128,512]{1,0:T(8,128)(2,1)S(1)}, bf16[128,512]{1,0:T(8,128)(2,1)S(1)}, u32[]{:S(2)}, u32[]{:S(2)}) collective-permute-start(bf16[128,512]{1,0:T(8,128)(2,1)S(1)} %get-tuple-element.71), channel_id=1, source_target_pairs={{0,12},{1,3},{2,14},{3,1},{4,8},{5,7},{6,10},{7,5},{8,4},{9,11},{1... | collective-permute-start | bytes 393224 | tf_op jit(solution)/shard_map/from_owners/ppermute | solution.py:549
  33.5 8.4 %collective-permute-start.11 = (bf16[128,512]{1,0:T(8,128)(2,1)S(1)}, bf16[128,512]{1,0:T(8,128)(2,1)S(1)}, u32[]{:S(2)}, u32[]{:S(2)}) collective-permute-start(bf16[128,512]{1,0:T(8,128)(2,1)S(1)} %get-tuple-element.72), channel_id=1, source_target_pairs={{0,4},{1,11},{2,6},{3,9},{4,0},{5,15},{6,2},{7,13},{8,12},{9,3},{1... | collective-permute-start | bytes 393224 | tf_op jit(solution)/shard_map/from_owners/ppermute | solution.py:549
  34.3 7.7 %collective-permute-start.12 = (bf16[128,512]{1,0:T(8,128)(2,1)S(1)}, bf16[128,512]{1,0:T(8,128)(2,1)S(1)}, u32[]{:S(2)}, u32[]{:S(2)}) collective-permute-start(bf16[128,512]{1,0:T(8,128)(2,1)S(1)} %get-tuple-element.73), channel_id=1, source_target_pairs={{0,10},{1,5},{2,8},{3,7},{4,14},{5,1},{6,12},{7,3},{8,2},{9,13},{1... | collective-permute-start | bytes 393224 | tf_op jit(solution)/shard_map/from_owners/ppermute | solution.py:549
  37.5 7.0 %collective-permute-start.13 = (bf16[128,512]{1,0:T(8,128)(2,1)S(1)}, bf16[128,512]{1,0:T(8,128)(2,1)S(1)}, u32[]{:S(2)}, u32[]{:S(2)}) collective-permute-start(bf16[128,512]{1,0:T(8,128)(2,1)S(1)} %get-tuple-element.75), channel_id=1, source_target_pairs={{0,6},{1,9},{2,4},{3,11},{4,2},{5,13},{6,0},{7,15},{8,14},{9,1},{1... | collective-permute-start | bytes 393224 | tf_op jit(solution)/shard_map/from_owners/ppermute | solution.py:549
  38.6 5.9 %collective-permute-start.14 = (bf16[128,512]{1,0:T(8,128)(2,1)S(1)}, bf16[128,512]{1,0:T(8,128)(2,1)S(1)}, u32[]{:S(2)}, u32[]{:S(2)}) collective-permute-start(bf16[128,512]{1,0:T(8,128)(2,1)S(1)} %get-tuple-element.76), channel_id=1, source_target_pairs={{0,8},{1,7},{2,10},{3,5},{4,12},{5,3},{6,14},{7,1},{8,0},{9,15},{1... | collective-permute-start | bytes 393224 | tf_op jit(solution)/shard_map/from_owners/ppermute | solution.py:549
  39.9 6.8 %collective-permute-start.15 = (bf16[128,512]{1,0:T(8,128)(2,1)S(1)}, bf16[128,512]{1,0:T(8,128)(2,1)S(1)}, u32[]{:S(2)}, u32[]{:S(2)}) collective-permute-start(bf16[128,512]{1,0:T(8,128)(2,1)S(1)} %get-tuple-element.78), channel_id=1, source_target_pairs={{0,14},{1,15},{2,12},{3,13},{4,10},{5,11},{6,8},{7,9},{8,6},{9,7},... | collective-permute-start | bytes 393224 | tf_op jit(solution)/shard_map/from_owners/ppermute | solution.py:549
  44.8 3.5 %copy-start.1 = (f32[4096]{0:T(1024)S(1)}, f32[4096]{0:T(1024)}, u32[]{:S(2)}) copy-start(f32[4096]{0:T(1024)} %param.13) | copy-start | bytes 49156
  46.9 1.4 %collective-permute-start.16 = (f32[256,128]{1,0:T(8,128)S(1)}, f32[256,128]{1,0:T(8,128)S(1)}, u32[]{:S(2)}, u32[]{:S(2)}) collective-permute-start(f32[256,128]{1,0:T(8,128)S(1)} %get-tuple-element.79.refs_0_), channel_id=1, source_target_pairs={{0,1},{1,0},{2,3},{3,2},{4,5},{5,4},{6,7},{7,6},{8,9},{9,8},{10,11... | collective-permute-start | bytes 393224 | tf_op jit(solution)/shard_map/norm/ppermute | solution.py:539
